TPU v7x, 32 devices: a whole 2x2x4 slice. The times are simulated.
32 devices in a mesh: rows: 8 (over y, x, core), cols: 4 (over z).
Axes of the slice: x: 2, y: 2, z: 4, core: 2. Of those that a mesh axis runs over, the one named last changes fastest.
Arguments:
- tiles: float32 [8, 32, 128, 128], P('rows', 'cols'), may hold values from -0.1875 to 0.1875
- tile_rows: int32 [8, 32], P('rows', 'cols'), may hold values from 0 to 1
- tile_cols: int32 [8, 32], P('rows', 'cols'), may hold values from 0 to 15
- counts: int32 [8, 4], P('rows', 'cols'), may hold values from 1 to 8, as said below
- scaling: float32 [8192], P('cols'), may hold values from 0.1 to 10
Outputs:
- normal: float32 [2048, 2048], P('rows', 'cols')
Inputs may be any that keep to these rules, and one draw needn't show every extreme that they name: `counts`: in every draw some panels have all 8 slots live in every column group; the others have at most 5.
All inputs are finite; a program needn't handle non-finite values.
Results may differ from a plain program's by a relative error of at most 0.0003.
Values sent between devices are 32-bit elements; how exact they have to be, the bound alone decides.
No kernel may reach another device: no remote copies, remote signals or barrier semaphores. Data moves between devices by JAX's collectives and lax.ppermute only.
A program may use at most 192 MiB of HBM per device.

v0:
```python
import jax
import jax.numpy as jnp
from jax import lax
from jax.sharding import PartitionSpec as P

TB = 128
RB = 2
CB_DEV = 16


def densify(tile_set, row_ids, col_ids, live_mask, scale_set, block_count):
    placed = jnp.zeros((block_count, RB, TB, TB), jnp.float32)
    placed = placed.at[col_ids, row_ids].add(tile_set * live_mask[:, None, None])
    placed = placed * scale_set[:, None, None, :]
    return placed.reshape(block_count, RB * TB, TB)


def place_panels(blocked, tile_set, row_ids, col_ids, live_mask, panel_count):
    picked = jnp.take(blocked, col_ids, axis=0)
    product = jnp.einsum("kac,kbc->kab", picked, tile_set, precision=lax.Precision.HIGHEST)
    product = product.reshape(panel_count, -1, RB * TB, TB)
    hit_row = (row_ids[:, None] == jnp.arange(RB, dtype=jnp.int32)[None, :]).astype(
        jnp.float32
    ) * live_mask[:, None]
    hit_row = hit_row.reshape(panel_count, -1, RB)
    placed = jnp.einsum("pkr,pkab->aprb", hit_row, product, precision=lax.Precision.HIGHEST)
    return placed.reshape(RB * TB, panel_count * RB * TB)


def per_device(tiles, tile_rows, tile_cols, counts, scaling):
    slot_total = tiles.shape[1]
    slot_range = jnp.arange(slot_total, dtype=jnp.int32)
    own_live = (slot_range < counts[0, 0]).astype(jnp.float32)
    blocked = densify(
        tiles[0], tile_rows[0], tile_cols[0], own_live, scaling.reshape(CB_DEV, TB), CB_DEV
    )
    piece_tiles = lax.all_gather(tiles, "rows", axis=0, tiled=True)
    piece_rows = lax.all_gather(tile_rows, "rows", axis=0, tiled=True)
    piece_cols = lax.all_gather(tile_cols, "rows", axis=0, tiled=True)
    piece_counts = lax.all_gather(counts, "rows", axis=0, tiled=True)
    count_here = piece_tiles.shape[0]
    live_mask = (slot_range[None, :] < piece_counts).astype(jnp.float32).reshape(-1)
    tile_block = place_panels(
        blocked,
        piece_tiles.reshape(count_here * slot_total, TB, TB),
        piece_rows.reshape(-1),
        piece_cols.reshape(-1),
        live_mask,
        count_here,
    )
    return lax.psum_scatter(tile_block, "cols", scatter_dimension=1, tiled=True)


def solution(mesh):
    placed = (
        P("rows", "cols", None, None),
        P("rows", "cols"),
        P("rows", "cols"),
        P("rows", "cols"),
        P("cols"),
    )
    return jax.shard_map(
        per_device, mesh=mesh, in_specs=placed, out_specs=P("rows", "cols"), check_vma=False
    )
```

profile of v0, /device:TPU:5, one launch (start us, length us, event | category | flops | bytes accessed | tf_op | source)
XLA Modules:
  0.0 124.9 jit_solution(4442594104682614490)
XLA Ops:
  6.5 0.0 copy-start.1
  6.5 0.0 all-gather.4.cloned.1.call-start
  6.5 0.7 all-gather.4.cloned.1.call-update
  7.3 0.0 reduce-scatter.2.cloned.1.call-start
  8.0 1.3 %dynamic-slice = u32[1]{0:T(128)} dynamic-slice(u32[32]{0:T(128)} %constant.45, u32[]{:T(128)S(6)} %add.51), dynamic_slice_sizes={1} | dynamic-slice | bytes 12
  9.3 0.7 bitcast_dynamic-update-slice_fusion
  10.0 5.5 %all-reduce = s32[8]{0:T(128)S(1)} all-reduce(s32[8]{0:T(128)S(1)} %bitcast_dynamic-update-slice_fusion), channel_id=1, replica_groups=mesh['rows'=8,'cols'=4] {'rows'}, use_global_device_ids=true, to_apply=%add | all-reduce | flops 8 | bytes 64
  15.5 10.8 %all-gather = s32[8,1,8]{2,1,0:T(1,128)S(1)} all-gather(s32[1,1,8]{2,1,0:T(1,128)} %bitcast.43), channel_id=1, replica_groups=mesh['rows'=8,'cols'=4] {'rows'}, dimensions={0}, use_global_device_ids=true | all-gather | bytes 288 | tf_op jit(solution)/shard_map/all_gather | solution.py:39
  26.3 0.1 reshape.142
  26.3 0.6 broadcast.123
  26.9 0.7 reduce.5
  27.6 0.1 reshape.140
  27.7 0.7 fusion.18
  28.4 1.1 bitcast_multiply_fusion
  29.6 0.2 broadcast_in_dim.19
  29.8 1.1 scatter_fusion
  30.9 0.0 copy-start
  30.9 1.3 %copy-done = f32[16,2,128,128]{3,2,1,0:T(8,128)} copy-done((f32[16,2,128,128]{3,2,1,0:T(8,128)}, f32[16,2,128,128]{3,2,1,0:T(8,128)S(1)}, u32[]{:S(2)}) %copy-start) | copy-done | bytes 2097176
  32.2 0.0 copy-done.1
  32.2 2.3 %broadcast_multiply_fusion = f32[16,2,128,128]{3,2,1,0:T(8,128)S(1)} fusion(f32[16,2,128,128]{3,2,1,0:T(8,128)} %copy-done, f32[16,128]{1,0:T(8,128)S(1)} %bitcast.42), kind=kLoop, calls=%fused_computation.9 | loop fusion | flops 524288 | bytes 4202496 | tf_op jit(solution)/shard_map/mul | solution.py:14
  34.6 0.0 copy-start.2
  34.6 4.3 %gather_fusion = f32[64,256,128]{2,1,0:T(8,128)} fusion(f32[16,256,128]{2,1,0:T(8,128)S(1)} %bitcast.37, s32[1024]{0:T(1024)S(1)} %pad_clamp_fusion), kind=kCustom, calls=%fused_computation | custom fusion | bytes 16777472 | tf_op jit(solution)/shard_map/jit(_take)/gather | solution.py:19
  38.9 0.0 copy-done.2
  38.9 7.8 %all-gather.1 = s32[8,1,8]{2,1,0:T(1,128)S(1)} all-gather(s32[1,1,8]{2,1,0:T(1,128)S(1)} %bitcast.44), channel_id=1, replica_groups=mesh['rows'=8,'cols'=4] {'rows'}, dimensions={0}, use_global_device_ids=true | all-gather | bytes 288 | tf_op jit(solution)/shard_map/all_gather | solution.py:38
  46.6 0.1 fusion.15
  46.7 0.8 all-gather.4.cloned.1.call-done
  47.5 11.9 %fusion.2 = f32[64,256,128]{2,1,0:T(8,128)S(1)} fusion(f32[64,128,128]{2,1,0:T(8,128)} %bitcast.39, f32[64,256,128]{2,1,0:T(8,128)} %gather_fusion, pred[64]{0:T(512)(128)(4,1)S(1)} %compare_and_fusion), kind=kOutput, calls=%fused_computation.4 | convolution fusion | flops 3223322624 | bytes 20971584 | tf_op jit(solution)/shard_map/kac,kbc->kab/dot_general | solution.py:20
  59.4 10.3 %fusion.6 = f32[256,8,2,128]{3,2,0,1:T(2,128)S(1)} fusion(f32[8,8,256,128]{3,2,1,0:T(8,128)S(1)} %bitcast.36, f32[8,8]{1,0:T(8,128)S(1)} %fusion.15, s32[8,8]{1,0:T(8,128)S(1)} %bitcast.40), kind=kOutput, calls=%fused_computation.8 | convolution fusion | flops 50331904 | bytes 10486272 | tf_op jit(solution)/shard_map/pkr,pkab->aprb/dot_general | solution.py:26
  69.7 2.4 %copy.11 = f32[256,8,2,128]{0,3,2,1:T(8,128)} copy(f32[256,8,2,128]{3,2,0,1:T(2,128)S(1)} %fusion.6) | data formatting | bytes 4194304 | tf_op jit(solution)/shard_map/pkr,pkab->aprb/transpose | solution.py:26
  72.1 0.0 reduce-scatter.2.cloned.1.call-update
  72.1 43.9 %reduce-scatter.2.cloned.1.call-done = f32[256,512]{0,1:T(8,128)} async-done(((f32[256,2048]{0,1:T(8,128)}), f32[256,512]{0,1:T(8,128)}) %reduce-scatter.2.cloned.1.call-update) | async-done | bytes 524304 | tf_op jit(solution)/shard_map/reduce_scatter | solution.py:51
  116.0 2.0 %copy.12 = f32[256,512]{1,0:T(8,128)} copy(f32[256,512]{0,1:T(8,128)} %reduce-scatter.2.cloned.1.call-done) | data formatting | bytes 1048576 | tf_op jit(solution)/shard_map/reduce_scatter | solution.py:51
  (5 shorter events, 0.0 us)
Async XLA Ops:
  6.5 25.7 %copy-start.1 = (f32[2048]{0:T(1024)S(1)}, f32[2048]{0:T(1024)}, u32[]{:S(2)}) copy-start(f32[2048]{0:T(1024)} %param.9) | copy-start | bytes 24580
  6.5 40.9 %all-gather.4.cloned.1.call-start = ((), (), s32[]{:S(2)}) async-start(), calls=%async_computation.1 | async-start | bytes 4718592 | tf_op jit(solution)/shard_map/all_gather | solution.py:37
  7.3 108.7 %reduce-scatter.2.cloned.1.call-start = ((), (), s32[]{:S(2)}) async-start(), calls=%async_computation.2 | async-start | bytes 2621440 | tf_op jit(solution)/shard_map/reduce_scatter | solution.py:51
  30.9 1.4 %copy-start = (f32[16,2,128,128]{3,2,1,0:T(8,128)}, f32[16,2,128,128]{3,2,1,0:T(8,128)S(1)}, u32[]{:S(2)}) copy-start(f32[16,2,128,128]{3,2,1,0:T(8,128)S(1)} %scatter_fusion) | copy-start | bytes 6291460
  34.6 4.3 %copy-start.2 = (s32[1,8]{1,0:T(1,128)S(1)}, s32[1,8]{1,0:T(1,128)}, u32[]{:S(2)}) copy-start(s32[1,8]{1,0:T(1,128)} %param.6) | copy-start | bytes 100
Sparse Core Ops, SparseCore 0:
  9.2 38.1 all-gather.3
  72.2 43.7 reduce-scatter.1
where the time goes:
time: 127 us; the launch traced here: 125 us
  waiting for transfers between devices  45.4 us (36%)
  blocking collectives  24 us (19%)
  matrix products  22.2 us (17%)
  between operations  14.1 us (11%)
  local copies, waits for them, and re-layouts  13.1 us (10%)
  other arithmetic  6.02 us (5%)
    reduce_scatter x1, waiting for transfers between devices, per_device(): return lax.psum_scatter(tile_block, 'cols', scatter_dimension=1, tiled=True)  43.9 us
    dot_general x1, matrix products, place_panels(): jnp.einsum('kac,kbc->kab', picked, tile_set, precision=lax.Precision.HIGH...  11.9 us
    all_gather x1, blocking collectives, per_device(): piece_cols = lax.all_gather(tile_cols, 'rows', axis=0, tiled=True)  10.8 us
    dot_general x1, matrix products, place_panels(): jnp.einsum('pkr,pkab->aprb', hit_row, product, precision=lax.Precision.HI...  10.3 us
    all_gather x1, blocking collectives, per_device(): piece_rows = lax.all_gather(tile_rows, 'rows', axis=0, tiled=True)  7.76 us
    unnamed x1, blocking collectives  5.47 us
    gather x1, local copies, waits for them, and re-layouts, place_panels(): picked = jnp.take(blocked, col_ids, axis=0)  4.31 us
    unnamed x9, local copies, waits for them, and re-layouts  3.37 us
  transfers between devices with their start and end apart: 2, of which 2 were waited for; matrix products, arithmetic and copies ran while one was open for 11% of the time, Pallas kernels for 0%

commit v1 on v0

--- a/solution.py
+++ b/solution.py
@@ -1,11 +1,372 @@
+import functools
+
 import jax
 import jax.numpy as jnp
 from jax import lax
+from jax.experimental import pallas as pl
+from jax.experimental.pallas import tpu as pltpu
 from jax.sharding import PartitionSpec as P
 
 TB = 128
 RB = 2
 CB_DEV = 16
+PANEL = RB * TB
+META = 8
+CUTS = 2
+CUT = TB // CUTS
+AXES = ("rows", "cols")
+VMEM_LIMIT = 16 * 1024 * 1024
+PACK_LIMIT = 60 * 1024 * 1024
+VSPEC = pl.BlockSpec(memory_space=pltpu.VMEM)
+HSPEC = pl.BlockSpec(memory_space=pltpu.HBM)
+
+
+def params(limit=VMEM_LIMIT):
+    return pltpu.CompilerParams(vmem_limit_bytes=limit)
+
+
+def cost(flops, nbytes):
+    return pl.CostEstimate(flops=flops * 20, bytes_accessed=nbytes * 20, transcendentals=0)
+
+
+def pack_kernel(slots, rows_hbm, cols_hbm, counts_hbm, tiles_hbm, scale_hbm, *refs):
+    whole_ref = refs[0]
+    cut_refs = refs[1 : 1 + CUTS]
+    rows_ref, cols_ref, counts_ref, tiles_ref, scale_ref, sems = refs[1 + CUTS :]
+    copies = [
+        pltpu.make_async_copy(source, target, sems.at[index])
+        for index, (source, target) in enumerate(
+            (
+                (rows_hbm, rows_ref),
+                (cols_hbm, cols_ref),
+                (counts_hbm, counts_ref),
+                (scale_hbm, scale_ref),
+                (tiles_hbm, tiles_ref),
+            )
+        )
+    ]
+    for copy in copies:
+        copy.start()
+    for copy in copies[:4]:
+        copy.wait()
+    lane = lax.broadcasted_iota(jnp.int32, (META, TB), 1)
+    codes = jnp.full((META, TB), -1.0, jnp.float32)
+    count = counts_ref[0, 0]
+    factors = []
+    for slot in range(slots):
+        live = slot < count
+        row = rows_ref[0, slot]
+        col = cols_ref[0, slot]
+        factors.append(jnp.where(live, jnp.sqrt(scale_ref[pl.ds(col, 1), :]), 0.0))
+        code = jnp.where(live, col * RB + row, -1).astype(jnp.float32)
+        codes = jnp.where(lane == slot, code, codes)
+    copies[4].wait()
+    for slot in range(slots):
+        for cut in range(CUTS):
+            scaled = tiles_ref[0, slot, cut * CUT : (cut + 1) * CUT, :] * factors[slot]
+            start = slot * CUT
+            cut_refs[cut][start : start + CUT, :] = scaled
+            start += cut * (slots * CUT + META)
+            whole_ref[start : start + CUT, :] = scaled
+    for cut in range(CUTS):
+        cut_refs[cut][slots * CUT :, :] = codes
+        start = cut * (slots * CUT + META) + slots * CUT
+        whole_ref[start : start + META, :] = codes
+
+
+def pack(tiles, tile_rows, tile_cols, counts, scaling):
+    slots = tiles.shape[1]
+    piece = slots * CUT + META
+    return pl.pallas_call(
+        functools.partial(pack_kernel, slots),
+        out_shape=[jax.ShapeDtypeStruct((CUTS * piece, TB), jnp.float32)]
+        + [jax.ShapeDtypeStruct((piece, TB), jnp.float32)] * CUTS,
+        in_specs=[HSPEC] * 5,
+        out_specs=[VSPEC] * (1 + CUTS),
+        scratch_shapes=[
+            pltpu.SMEM(tile_rows.shape, jnp.int32),
+            pltpu.SMEM(tile_cols.shape, jnp.int32),
+            pltpu.SMEM(counts.shape, jnp.int32),
+            pltpu.VMEM(tiles.shape, jnp.float32),
+            pltpu.VMEM((CB_DEV, TB), jnp.float32),
+            pltpu.SemaphoreType.DMA((5,)),
+        ],
+        compiler_params=params(PACK_LIMIT),
+        cost_estimate=cost(slots * TB * TB, 3 * slots * TB * TB * 4),
+        name="pack",
+    )(tile_rows, tile_cols, counts, tiles, scaling.reshape(CB_DEV, TB))
+
+
+def read_codes(piece_refs, base, stage_ref, code_ref, sem):
+    for index, piece_ref in enumerate(piece_refs):
+        stage_ref[index] = piece_ref[base : base + META, :].astype(jnp.int32)
+    copy = pltpu.make_async_copy(stage_ref, code_ref, sem)
+    copy.start()
+    copy.wait()
+
+
+def code_scratch(count):
+    return [
+        pltpu.VMEM((count, META, TB), jnp.int32),
+        pltpu.SMEM((count, META, TB), jnp.int32),
+        pltpu.SMEM((CB_DEV,), jnp.int32),
+        pltpu.SemaphoreType.DMA,
+    ]
+
+
+def mark(slots, code_ref, first_index, used_ref):
+    for col in range(CB_DEV):
+        used_ref[col] = 0
+    for side in range(2):
+        for slot in range(slots):
+            code = code_ref[first_index + side, 0, slot]
+
+            @pl.when(code >= 0)
+            def _(code=code):
+                used_ref[code >> 1] = 1
+
+
+def spread_kernel(slots, count, *refs):
+    pieces = refs[: 2 * count]
+    dense_ref, sum_ref, stage_ref, code_ref, used_ref, sem = refs[2 * count :]
+    cuts_each = CUTS // count
+    read_codes((pieces[0], pieces[count]), slots * CUT, stage_ref, code_ref, sem)
+    for col in range(CB_DEV):
+        used_ref[col] = 0
+    for side in range(2):
+        for slot in range(slots):
+            code = code_ref[side, 0, slot]
+
+            @pl.when(code >= 0)
+            def _(code=code, slot=slot, side=side):
+                col = code >> 1
+
+                @pl.when(used_ref[col] == 0)
+                def _():
+                    used_ref[col] = 1
+                    sum_ref[col] = jnp.zeros_like(sum_ref[col])
+
+                start = pl.multiple_of(side * PANEL + (code & 1) * TB, TB)
+                for cut in range(CUTS):
+                    piece_ref = pieces[side * count + cut // cuts_each]
+                    base = (cut % cuts_each) * (slots * CUT + META) + slot * CUT
+                    place = pl.ds(start + cut * CUT, CUT)
+                    sum_ref[col, place, :] += piece_ref[base : base + CUT, :]
+
+    def convert(col, carry):
+        @pl.when(used_ref[col] == 1)
+        def _():
+            high, low = split(sum_ref[col])
+            dense_ref[col, :, :TB] = high
+            dense_ref[col, :, TB:] = low
+
+        return carry
+
+    lax.fori_loop(0, CB_DEV, convert, 0)
+
+
+def spread(own, other, slots):
+    count = len(own)
+    return pl.pallas_call(
+        functools.partial(spread_kernel, slots, count),
+        out_shape=jax.ShapeDtypeStruct((CB_DEV, 2 * PANEL, 2 * TB), jnp.bfloat16),
+        in_specs=[VSPEC] * (2 * count),
+        out_specs=VSPEC,
+        scratch_shapes=[
+            pltpu.VMEM((CB_DEV, 2 * PANEL, TB), jnp.float32),
+            *code_scratch(2),
+        ],
+        compiler_params=params(),
+        cost_estimate=cost(1 << 20, 1 << 21),
+        name="spread",
+    )(*own, *other)
+
+
+def split(x):
+    high = x.astype(jnp.bfloat16)
+    low = (x - high.astype(jnp.float32)).astype(jnp.bfloat16)
+    return high, low
+
+
+def nt_dot(a, b):
+    return lax.dot_general(a, b, (((1,), (1,)), ((), ())), preferred_element_type=jnp.float32)
+
+
+def product(left, tile):
+    high, low = split(tile)
+    right = jnp.concatenate(
+        [jnp.concatenate([high, high], axis=1), jnp.concatenate([low, low], axis=1)], axis=0
+    )
+    return nt_dot(left, right)
+
+
+def swapped():
+    chip = lax.axis_index("rows") >> 1
+    plane = lax.axis_index("cols")
+    chip_outer = (chip == 0) | (chip == 3)
+    plane_outer = (plane == 0) | (plane == 3)
+    chunk_a = jnp.where(plane_outer, chip, chip ^ 1)
+    near = jnp.where(chip_outer, plane, plane ^ 1)
+    return jnp.where(chunk_a == near, 0, 1).astype(jnp.int32)
+
+
+def for_live(slots, code_ref, used_ref, flag, body):
+    for which in range(2):
+        chunk = flag if which == 0 else 1 - flag
+        for slot in range(slots):
+            code = code_ref[which, 0, slot]
+            live = (code >= 0) & (used_ref[jnp.maximum(code, 0) >> 1] == 1)
+
+            @pl.when(live)
+            def _(code=code, which=which, slot=slot, chunk=chunk):
+                body(which, slot, code >> 1, chunk, code & 1)
+
+
+def first_kernel(slots, dense_ref, own_ref, other_ref, a_ref, b_ref, acc_ref, stage_ref, code_ref, used_ref, sem):
+    read_codes((a_ref, b_ref, own_ref, other_ref), slots * CUT, stage_ref, code_ref, sem)
+    mark(slots, code_ref, 2, used_ref)
+    acc_ref[...] = jnp.zeros_like(acc_ref)
+
+    def body(which, slot, col, chunk, block):
+        piece_ref = a_ref if which == 0 else b_ref
+        starts = [cut * (slots * CUT + META) + slot * CUT for cut in range(CUTS)]
+        tile = jnp.concatenate([piece_ref[start : start + CUT, :] for start in starts], axis=0)
+        both = product(dense_ref[col], tile)
+        acc_ref[chunk, block] += both[:, :TB] + both[:, TB:]
+
+    for_live(slots, code_ref, used_ref, swapped(), body)
+
+
+def first(dense, own, other, right_a, right_b, slots):
+    return pl.pallas_call(
+        functools.partial(first_kernel, slots),
+        out_shape=jax.ShapeDtypeStruct((2, RB, 2 * PANEL, TB), jnp.float32),
+        in_specs=[VSPEC] * 5,
+        out_specs=VSPEC,
+        scratch_shapes=code_scratch(4),
+        compiler_params=params(),
+        cost_estimate=cost(slots * 4 * 4 * PANEL * TB * TB, 1 << 22),
+        name="first",
+    )(dense, own, other, right_a, right_b)
+
+
+def second_kernel(slots, cut, dense_ref, own_ref, other_ref, acc_ref, a_ref, b_ref, *refs):
+    out_refs = refs[:4]
+    sum_ref, stage_ref, code_ref, used_ref, sem = refs[4:]
+    read_codes((a_ref, b_ref, own_ref, other_ref), slots * CUT, stage_ref, code_ref, sem)
+    mark(slots, code_ref, 2, used_ref)
+    sum_ref[...] = jnp.zeros_like(sum_ref)
+
+    def body(which, slot, col, chunk, block):
+        piece_ref = a_ref if which == 0 else b_ref
+        sum_ref[chunk, block] += product(dense_ref[col], piece_ref[slot * CUT : (slot + 1) * CUT, :])
+
+    for_live(slots, code_ref, used_ref, swapped(), body)
+    for chunk in range(2):
+        for side in range(2):
+            rows = slice(side * PANEL, (side + 1) * PANEL)
+            parts = []
+            for block in range(RB):
+                both = sum_ref[chunk, block, rows, :]
+                parts.append(both[:, :CUT] + both[:, CUT:] + acc_ref[chunk, block, rows, cut * CUT : (cut + 1) * CUT])
+            out_refs[2 * chunk + side][...] = jnp.concatenate(parts, axis=1)
+
+
+def second(cut, dense, own, other, acc, piece_a, piece_b, slots):
+    shape = jax.ShapeDtypeStruct((PANEL, RB * CUT), jnp.float32)
+    return pl.pallas_call(
+        functools.partial(second_kernel, slots, cut),
+        out_shape=[shape] * 4,
+        in_specs=[VSPEC] * 6,
+        out_specs=[VSPEC] * 4,
+        scratch_shapes=[
+            pltpu.VMEM((2, RB, 2 * PANEL, 2 * CUT), jnp.float32),
+            *code_scratch(4),
+        ],
+        compiler_params=params(),
+        cost_estimate=cost(slots * 2 * 4 * PANEL * TB * TB, 1 << 21),
+        name="second",
+    )(dense, own, other, acc, piece_a, piece_b)
+
+
+def join_kernel(cuts, cut_rows, *refs):
+    out_ref = refs[-1]
+    core = lax.axis_index("rows") & 1
+    for side in range(2):
+        halves = [refs[side * cuts + cut][...] + refs[(2 + side) * cuts + cut][...] for cut in range(cuts)]
+        for block in range(RB):
+            part = [half[:, block * cut_rows : (block + 1) * cut_rows] for half in halves]
+            panel = core if side == 0 else 1 - core
+            start = pl.multiple_of(panel * PANEL + block * TB, TB)
+            out_ref[:, pl.ds(start, TB)] = part[0] if cuts == 1 else jnp.concatenate(part, axis=1)
+
+
+def join(near_same, near_cross, far_same, far_cross):
+    cuts = len(near_same)
+    return pl.pallas_call(
+        functools.partial(join_kernel, cuts, TB // cuts),
+        out_shape=jax.ShapeDtypeStruct((PANEL, 2 * PANEL), jnp.float32),
+        in_specs=[VSPEC] * (4 * cuts),
+        out_specs=VSPEC,
+        compiler_params=params(),
+        cost_estimate=cost(PANEL * 2 * PANEL, PANEL * 2 * PANEL * 12),
+        name="join",
+    )(*near_same, *near_cross, *far_same, *far_cross)
+
+
+def pairs(place):
+    out = []
+    for row in range(8):
+        for col in range(4):
+            chip, core, plane = place(row >> 1, row & 1, col)
+            out.append((row * 4 + col, (chip * 2 + core) * 4 + plane))
+    return out
+
+
+def outer(plane):
+    return plane in (0, 3)
+
+
+SWAP = pairs(lambda k, i, p: (k, 1 - i, p))
+NEXT = pairs(lambda k, i, p: (k, i, p ^ 1))
+SEND_A = pairs(lambda k, i, p: (k if outer(p) else k ^ 1, i, p))
+SEND_B = pairs(lambda k, i, p: (k ^ 3 if outer(p) else k ^ 2, i, p))
+NEAR = pairs(lambda k, i, p: (k, i, p if outer(k) else p ^ 1))
+FAR = pairs(lambda k, i, p: (k, i, p ^ 3 if outer(k) else p ^ 2))
+NEAR_CROSS = pairs(lambda k, i, p: (k, 1 - i, p if outer(k) else p ^ 1))
+FAR_CROSS = pairs(lambda k, i, p: (k, 1 - i, p ^ 3 if outer(k) else p ^ 2))
+
+
+def send(pieces, perm):
+    return [lax.ppermute(piece, AXES, perm) for piece in pieces]
+
+
+def after(x, *others):
+    return lax.optimization_barrier((x, *others))[0]
+
+
+def per_device(tiles, tile_rows, tile_cols, counts, scaling):
+    slots = tiles.shape[1]
+    whole, *own = pack(tiles, tile_rows, tile_cols, counts, scaling)
+    next_own = send(own, NEXT)
+    own_a, own_b = (lax.ppermute(whole, AXES, perm) for perm in (SEND_A, SEND_B))
+    own_other = lax.ppermute(whole, AXES, SWAP)
+    own_dense = spread([whole], [own_other], slots)
+    acc = first(own_dense, whole, own_other, own_a, own_b, slots)
+    early = after(next_own[1], own_dense)
+    late = after(next_own[0], acc)
+    next_a = send((late, early), SEND_A)
+    next_b = send((late, early), SEND_B)
+    next_other = send((after(next_own[0], own_b), after(next_own[1], own_a)), SWAP)
+    next_dense = spread(next_own, next_other, slots)
+    near_same, near_cross, far_same, far_cross = [], [], [], []
+    for cut in range(CUTS):
+        results = second(cut, next_dense, next_own[0], next_other[0], acc, next_a[cut], next_b[cut], slots)
+        far_same.append(lax.ppermute(results[2], AXES, FAR))
+        far_cross.append(lax.ppermute(results[3], AXES, FAR_CROSS))
+        near_same.append(lax.ppermute(results[0], AXES, NEAR))
+        near_cross.append(lax.ppermute(results[1], AXES, NEAR_CROSS))
+    return join(near_same, near_cross, far_same, far_cross)
 
 
 def densify(tile_set, row_ids, col_ids, live_mask, scale_set, block_count):
@@ -27,7 +388,7 @@
     return placed.reshape(RB * TB, panel_count * RB * TB)
 
 
-def per_device(tiles, tile_rows, tile_cols, counts, scaling):
+def per_device_any(tiles, tile_rows, tile_cols, counts, scaling):
     slot_total = tiles.shape[1]
     slot_range = jnp.arange(slot_total, dtype=jnp.int32)
     own_live = (slot_range < counts[0, 0]).astype(jnp.float32)
@@ -59,6 +420,11 @@
         P("rows", "cols"),
         P("cols"),
     )
+    small = mesh.shape["rows"] == 8 and mesh.shape["cols"] == 4
     return jax.shard_map(
-        per_device, mesh=mesh, in_specs=placed, out_specs=P("rows", "cols"), check_vma=False
+        per_device if small else per_device_any,
+        mesh=mesh,
+        in_specs=placed,
+        out_specs=P("rows", "cols"),
+        check_vma=False,
     )

time: 127 us -> 64.2 us (0.51); the launches traced: 125 us -> 63.7 us
  starting transfers between devices: 0.04 us -> 26 us
  blocking collectives: 24 us -> 0 us
  waiting for transfers between devices: 45.4 us -> 22.3 us
  matrix products: 22.2 us -> 0 us
  Pallas kernels: 0 us -> 13.6 us
  between operations: 14.1 us -> 0.79 us
  local copies, waits for them, and re-layouts: 13.1 us -> 1.04 us
  other arithmetic: 6.02 us -> 0 us
    reduce_scatter x1 -> x0, waiting for transfers between devices: 43.9 us -> none  [per_device(): return lax.psum_scatter(tile_block, 'cols', scatter_dimension=1, tiled=True)]
    ppermute x0 -> x19, starting transfers between devices: none -> 26 us  [the longest x2 10.3 us: per_device(): near_same.append(lax.ppermute(results[0], AXES, NEAR))]
    ppermute x0 -> x19, waiting for transfers between devices: none -> 22.3 us  [the longest x2 9.68 us: per_device(): far_cross.append(lax.ppermute(results[3], AXES, FAR_CROSS))]
    dot_general x2 -> x0, matrix products: 22.2 us -> none  [the longest x1 11.9 us: place_panels(): jnp.einsum('kac,kbc->kab', picked, tile_set, precision=lax.Precision.HIGH...]
    all_gather x2 -> x0, blocking collectives: 18.5 us -> none  [the longest x1 10.8 us: per_device(): piece_cols = lax.all_gather(tile_cols, 'rows', axis=0, tiled=True)]
    pallas_call x0 -> x7, Pallas kernels: none -> 13.6 us  [the longest x2 5.36 us: second(): pl.pallas_call(functools.partial(second_kernel, slots, cut), out_shape=[s...]
    unnamed x1 -> x0, blocking collectives: 5.47 us -> none
    gather x1 -> x0, local copies, waits for them, and re-layouts: 4.31 us -> none  [place_panels(): picked = jnp.take(blocked, col_ids, axis=0)]
  transfers between devices with their start and end apart: 2 -> 19, of which waited for: 2 -> 7; matrix products, arithmetic and copies ran while one was open for 11% -> 0% of each run, Pallas kernels for 0% -> 16%
where the time goes in v1:
time: 64.2 us; the launch traced here: 63.7 us
  starting transfers between devices  26 us (40%)
  waiting for transfers between devices  22.3 us (35%)
  Pallas kernels  13.6 us (21%)
  local copies, waits for them, and re-layouts  1.04 us (2%)
  between operations  0.79 us (1%)
    ppermute x2, starting transfers between devices, per_device(): near_same.append(lax.ppermute(results[0], AXES, NEAR))  10.3 us
    ppermute x2, waiting for transfers between devices, per_device(): far_cross.append(lax.ppermute(results[3], AXES, FAR_CROSS))  9.68 us
    ppermute x8, waiting for transfers between devices, send(): return [lax.ppermute(piece, AXES, perm) for piece in pieces]  7.35 us
    ppermute x8, starting transfers between devices, send(): return [lax.ppermute(piece, AXES, perm) for piece in pieces]  6.57 us
    pallas_call x2, Pallas kernels, second(): pl.pallas_call(functools.partial(second_kernel, slots, cut), out_shape=[s...  5.36 us
    ppermute x2, starting transfers between devices, per_device(): far_same.append(lax.ppermute(results[2], AXES, FAR))  4.38 us
    pallas_call x2, Pallas kernels, spread(): pl.pallas_call(functools.partial(spread_kernel, slots, count), out_shape=...  3.26 us
    ppermute x2, waiting for transfers between devices, per_device(): far_same.append(lax.ppermute(results[2], AXES, FAR))  3.01 us
  transfers between devices with their start and end apart: 19, of which 7 were waited for; matrix products, arithmetic and copies ran while one was open for 0% of the time, Pallas kernels for 16%

profile of v1, /device:TPU:5, one launch (start us, length us, event | category | flops | bytes accessed | tf_op | source)
XLA Modules:
  0.0 63.7 jit_solution(11616661374706177784)
XLA Ops:
  0.7 2.1 %pack.1 = (f32[1040,128]{1,0:T(8,128)}, f32[520,128]{1,0:T(8,128)}, f32[520,128]{1,0:T(8,128)}) custom-call(s32[1,8]{1,0:T(1,128)} %rows_hbm.1, s32[1,8]{1,0:T(1,128)} %cols_hbm.1, s32[1,1]{1,0:T(1,128)S(6)} %copy.6.counts_hbm, f32[1,8,128,128]{3,2,1,0:T(8,128)} %tiles_hbm.1, f32[16,128]{1,0:T(8,128)} %bitcast.1), custom_call_target="tpu_custom_call" | custom-call | flops 2621440 | bytes 31457280 | tf_op jit(solution)/shard_map/pack/pallas_call | solution.py:80
  2.8 0.7 %collective-permute-start.6 = (f32[1040,128]{1,0:T(8,128)}, f32[1040,128]{1,0:T(8,128)S(1)}, u32[]{:S(2)}, u32[]{:S(2)}) collective-permute-start(f32[1040,128]{1,0:T(8,128)} %get-tuple-element.22.refs_0_.own_ref), channel_id=1, source_target_pairs={{0,4},{1,5},{2,6},{3,7},{4,0},{5,1},{6,2},{7,3},{8,12},{9,13},{10,... | collective-permute-start | bytes 1597448 | tf_op jit(solution)/shard_map/ppermute | solution.py:353
  3.5 1.2 %collective-permute-start.2 = (f32[1040,128]{1,0:T(8,128)}, f32[1040,128]{1,0:T(8,128)S(1)}, u32[]{:S(2)}, u32[]{:S(2)}) collective-permute-start(f32[1040,128]{1,0:T(8,128)} %get-tuple-element.22.refs_0_.own_ref), channel_id=1, source_target_pairs={{0,24},{1,17},{2,18},{3,27},{4,28},{5,21},{6,22},{7,31},{8,16},{9,... | collective-permute-start | bytes 1597448 | tf_op jit(solution)/shard_map/ppermute | solution.py:352
  4.7 1.7 %collective-permute-start.4 = (f32[1040,128]{1,0:T(8,128)}, f32[1040,128]{1,0:T(8,128)S(1)}, u32[]{:S(2)}, u32[]{:S(2)}) collective-permute-start(f32[1040,128]{1,0:T(8,128)} %get-tuple-element.22.refs_0_.own_ref), channel_id=1, source_target_pairs={{0,0},{1,9},{2,10},{3,3},{4,4},{5,13},{6,14},{7,7},{8,8},{9,1},{10... | collective-permute-start | bytes 1597448 | tf_op jit(solution)/shard_map/ppermute | solution.py:352
  6.4 1.9 %collective-permute-start.1 = (f32[520,128]{1,0:T(8,128)}, f32[520,128]{1,0:T(8,128)S(1)}, u32[]{:S(2)}, u32[]{:S(2)}) collective-permute-start(f32[520,128]{1,0:T(8,128)} %get-tuple-element.21), channel_id=1, source_target_pairs={{0,1},{1,0},{2,3},{3,2},{4,5},{5,4},{6,7},{7,6},{8,9},{9,8},{10,11... | collective-permute-start | bytes 798728 | tf_op jit(solution)/shard_map/ppermute | solution.py:341
  8.2 0.1 collective-permute-start
  8.3 0.0 collective-permute-done.6.refs_1_.other_ref
  8.3 0.0 copy-start
  8.3 1.0 %copy-done = f32[1040,128]{1,0:T(8,128)S(1)} copy-done((f32[1040,128]{1,0:T(8,128)S(1)}, f32[1040,128]{1,0:T(8,128)}, u32[]{:S(2)}) %copy-start) | copy-done | bytes 532504
  9.4 1.7 %spread.3.dense_ref = bf16[16,512,256]{2,1,0:T(8,128)(2,1)S(1)} custom-call(f32[1040,128]{1,0:T(8,128)S(1)} %copy-done, f32[1040,128]{1,0:T(8,128)S(1)} %collective-permute-done.6.refs_1_.other_ref), custom_call_target="tpu_custom_call" | custom-call | flops 20971520 | bytes 41943040 | tf_op jit(solution)/shard_map/spread/pallas_call | solution.py:170
  11.0 3.6 %collective-permute-done.1.refs_1_ = f32[520,128]{1,0:T(8,128)S(1)} collective-permute-done((f32[520,128]{1,0:T(8,128)}, f32[520,128]{1,0:T(8,128)S(1)}, u32[]{:S(2)}, u32[]{:S(2)}) %collective-permute-start.1) | collective-permute-done | bytes 266272 | tf_op jit(solution)/shard_map/ppermute | solution.py:341
  14.6 0.7 %collective-permute-start.10 = (f32[520,128]{1,0:T(8,128)S(1)}, f32[520,128]{1,0:T(8,128)S(1)}, u32[]{:S(2)}, u32[]{:S(2)}) collective-permute-start(f32[520,128]{1,0:T(8,128)S(1)} %collective-permute-done.1.refs_1_), channel_id=1, source_target_pairs={{0,0},{1,9},{2,10},{3,3},{4,4},{5,13},{6,14},{7,7},{8,8},{9,1},{10... | collective-permute-start | bytes 798728 | tf_op jit(solution)/shard_map/ppermute | solution.py:341
  15.3 1.3 %collective-permute-start.11 = (f32[520,128]{1,0:T(8,128)S(1)}, f32[520,128]{1,0:T(8,128)S(1)}, u32[]{:S(2)}, u32[]{:S(2)}) collective-permute-start(f32[520,128]{1,0:T(8,128)S(1)} %collective-permute-done.1.refs_1_), channel_id=1, source_target_pairs={{0,24},{1,17},{2,18},{3,27},{4,28},{5,21},{6,22},{7,31},{8,16},{9,... | collective-permute-start | bytes 798728 | tf_op jit(solution)/shard_map/ppermute | solution.py:341
  16.6 3.8 %collective-permute-done.refs_0_.own_ref = f32[520,128]{1,0:T(8,128)S(1)} collective-permute-done((f32[520,128]{1,0:T(8,128)}, f32[520,128]{1,0:T(8,128)S(1)}, u32[]{:S(2)}, u32[]{:S(2)}) %collective-permute-start) | collective-permute-done | bytes 266272 | tf_op jit(solution)/shard_map/ppermute | solution.py:341
  20.3 0.0 collective-permute-done.2.b_ref
  20.3 1.2 %collective-permute-start.3 = (f32[520,128]{1,0:T(8,128)S(1)}, f32[520,128]{1,0:T(8,128)S(1)}, u32[]{:S(2)}, u32[]{:S(2)}) collective-permute-start(f32[520,128]{1,0:T(8,128)S(1)} %collective-permute-done.refs_0_.own_ref), channel_id=1, source_target_pairs={{0,4},{1,5},{2,6},{3,7},{4,0},{5,1},{6,2},{7,3},{8,12},{9,13},{10,... | collective-permute-start | bytes 798728 | tf_op jit(solution)/shard_map/ppermute | solution.py:341
  21.5 0.0 collective-permute-done.4.a_ref
  21.5 0.1 collective-permute-start.5
  21.6 1.8 %first.1.acc_ref = f32[2,2,512,128]{3,2,1,0:T(8,128)S(1)} custom-call(bf16[16,512,256]{2,1,0:T(8,128)(2,1)S(1)} %spread.3.dense_ref, f32[1040,128]{1,0:T(8,128)S(1)} %copy-done, f32[1040,128]{1,0:T(8,128)S(1)} %collective-permute-done.6.refs_1_.other_ref, f32[1040,128]{1,0:T(8,128)S(1)} %collective-permute-done.4.a_ref, ...), custom_call_target="tpu_custom_call" | custom-call | flops 10737418240 | bytes 83886080 | tf_op jit(solution)/shard_map/first/pallas_call | solution.py:241
  23.4 0.7 %collective-permute-start.7 = (f32[520,128]{1,0:T(8,128)S(1)}, f32[520,128]{1,0:T(8,128)S(1)}, u32[]{:S(2)}, u32[]{:S(2)}) collective-permute-start(f32[520,128]{1,0:T(8,128)S(1)} %collective-permute-done.refs_0_.own_ref), channel_id=1, source_target_pairs={{0,0},{1,9},{2,10},{3,3},{4,4},{5,13},{6,14},{7,7},{8,8},{9,1},{10... | collective-permute-start | bytes 798728 | tf_op jit(solution)/shard_map/ppermute | solution.py:341
  24.1 0.0 collective-permute-done.3.refs_2_.other_ref
  24.1 0.8 %collective-permute-start.8 = (f32[520,128]{1,0:T(8,128)S(1)}, f32[520,128]{1,0:T(8,128)S(1)}, u32[]{:S(2)}, u32[]{:S(2)}) collective-permute-start(f32[520,128]{1,0:T(8,128)S(1)} %collective-permute-done.refs_0_.own_ref), channel_id=1, source_target_pairs={{0,24},{1,17},{2,18},{3,27},{4,28},{5,21},{6,22},{7,31},{8,16},{9,... | collective-permute-start | bytes 798728 | tf_op jit(solution)/shard_map/ppermute | solution.py:341
  24.9 0.0 collective-permute-done.5.refs_3_
  24.9 1.6 %spread.2.dense_ref = bf16[16,512,256]{2,1,0:T(8,128)(2,1)S(1)} custom-call(f32[520,128]{1,0:T(8,128)S(1)} %collective-permute-done.refs_0_.own_ref, f32[520,128]{1,0:T(8,128)S(1)} %collective-permute-done.1.refs_1_, f32[520,128]{1,0:T(8,128)S(1)} %collective-permute-done.3.refs_2_.other_ref, f32[520,128]{1,0:T(8,128)S(1)} %collective-permute-done.5.refs_3_), custom_call_target="tpu_custom_call" | custom-call | flops 20971520 | bytes 41943040 | tf_op jit(solution)/shard_map/spread/pallas_call | solution.py:170
  26.5 0.0 collective-permute-done.10.a_ref
  26.5 0.0 collective-permute-done.11.b_ref
  26.5 2.8 %second.3 = (f32[256,128]{1,0:T(8,128)S(1)}, f32[256,128]{1,0:T(8,128)S(1)}, f32[256,128]{1,0:T(8,128)S(1)}, f32[256,128]{1,0:T(8,128)S(1)}) custom-call(bf16[16,512,256]{2,1,0:T(8,128)(2,1)S(1)} %spread.2.dense_ref, f32[520,128]{1,0:T(8,128)S(1)} %collective-permute-done.refs_0_.own_ref, f32[520,128]{1,0:T(8,128)S(1)} %collective-permute-done.3.refs_2_.other_ref, ...), custom_call_target="tpu_custom_call" | custom-call | flops 5368709120 | bytes 41943040 | tf_op jit(solution)/shard_map/second/pallas_call | solution.py:277
  29.3 7.4 %collective-permute-start.12 = (f32[256,128]{1,0:T(8,128)S(1)}, f32[256,128]{1,0:T(8,128)S(1)}, u32[]{:S(2)}, u32[]{:S(2)}) collective-permute-start(f32[256,128]{1,0:T(8,128)S(1)} %get-tuple-element.28), channel_id=1, source_target_pairs={{0,0},{1,1},{2,2},{3,3},{4,4},{5,5},{6,6},{7,7},{8,9},{9,8},{10,11... | collective-permute-start | bytes 393224 | tf_op jit(solution)/shard_map/ppermute | solution.py:367
  36.7 0.1 collective-permute-start.14
  36.8 1.9 %collective-permute-start.16 = (f32[256,128]{1,0:T(8,128)S(1)}, f32[256,128]{1,0:T(8,128)S(1)}, u32[]{:S(2)}, u32[]{:S(2)}) collective-permute-start(f32[256,128]{1,0:T(8,128)S(1)} %get-tuple-element.32), channel_id=1, source_target_pairs={{0,3},{1,2},{2,1},{3,0},{4,7},{5,6},{6,5},{7,4},{8,10},{9,11},{10,... | collective-permute-start | bytes 393224 | tf_op jit(solution)/shard_map/ppermute | solution.py:365
  38.7 0.0 collective-permute-done.7.a_ref
  38.7 1.1 %collective-permute-start.18 = (f32[256,128]{1,0:T(8,128)S(1)}, f32[256,128]{1,0:T(8,128)S(1)}, u32[]{:S(2)}, u32[]{:S(2)}) collective-permute-start(f32[256,128]{1,0:T(8,128)S(1)} %get-tuple-element.34), channel_id=1, source_target_pairs={{0,7},{1,6},{2,5},{3,4},{4,3},{5,2},{6,1},{7,0},{8,14},{9,15},{10,... | collective-permute-start | bytes 393224 | tf_op jit(solution)/shard_map/ppermute | solution.py:366
  39.7 0.0 collective-permute-done.8.b_ref
  39.7 2.5 %second.2 = (f32[256,128]{1,0:T(8,128)S(1)}, f32[256,128]{1,0:T(8,128)S(1)}, f32[256,128]{1,0:T(8,128)S(1)}, f32[256,128]{1,0:T(8,128)S(1)}) custom-call(bf16[16,512,256]{2,1,0:T(8,128)(2,1)S(1)} %spread.2.dense_ref, f32[520,128]{1,0:T(8,128)S(1)} %collective-permute-done.refs_0_.own_ref, f32[520,128]{1,0:T(8,128)S(1)} %collective-permute-done.3.refs_2_.other_ref, ...), custom_call_target="tpu_custom_call" | custom-call | flops 5368709120 | bytes 41943040 | tf_op jit(solution)/shard_map/second/pallas_call | solution.py:277
  42.3 0.1 collective-permute-start.13
  42.4 0.5 collective-permute-done.12.refs_1_
  42.8 2.5 %collective-permute-start.15 = (f32[256,128]{1,0:T(8,128)S(1)}, f32[256,128]{1,0:T(8,128)S(1)}, u32[]{:S(2)}, u32[]{:S(2)}) collective-permute-start(f32[256,128]{1,0:T(8,128)S(1)} %get-tuple-element.31), channel_id=1, source_target_pairs={{0,3},{1,2},{2,1},{3,0},{4,7},{5,6},{6,5},{7,4},{8,10},{9,11},{10,... | collective-permute-start | bytes 393224 | tf_op jit(solution)/shard_map/ppermute | solution.py:365
  45.4 1.7 %collective-permute-done.14.refs_3_ = f32[256,128]{1,0:T(8,128)S(1)} collective-permute-done((f32[256,128]{1,0:T(8,128)S(1)}, f32[256,128]{1,0:T(8,128)S(1)}, u32[]{:S(2)}, u32[]{:S(2)}) %collective-permute-start.14) | collective-permute-done | bytes 131104 | tf_op jit(solution)/shard_map/ppermute | solution.py:368
  47.1 0.0 collective-permute-start.17
  47.1 0.0 collective-permute-done.16.refs_5_
  47.1 2.9 %collective-permute-start.9 = (f32[256,128]{1,0:T(8,128)S(1)}, f32[256,128]{1,0:T(8,128)S(1)}, u32[]{:S(2)}, u32[]{:S(2)}) collective-permute-start(f32[256,128]{1,0:T(8,128)S(1)} %get-tuple-element.26), channel_id=1, source_target_pairs={{0,0},{1,1},{2,2},{3,3},{4,4},{5,5},{6,6},{7,7},{8,9},{9,8},{10,11... | collective-permute-start | bytes 393224 | tf_op jit(solution)/shard_map/ppermute | solution.py:367
  50.0 6.4 %collective-permute-done.18.refs_7_ = f32[256,128]{1,0:T(8,128)S(1)} collective-permute-done((f32[256,128]{1,0:T(8,128)S(1)}, f32[256,128]{1,0:T(8,128)S(1)}, u32[]{:S(2)}, u32[]{:S(2)}) %collective-permute-start.18) | collective-permute-done | bytes 131104 | tf_op jit(solution)/shard_map/ppermute | solution.py:366
  56.4 0.0 collective-permute-done.13.refs_2_
  56.4 3.0 %collective-permute-done.15.refs_4_ = f32[256,128]{1,0:T(8,128)S(1)} collective-permute-done((f32[256,128]{1,0:T(8,128)S(1)}, f32[256,128]{1,0:T(8,128)S(1)}, u32[]{:S(2)}, u32[]{:S(2)}) %collective-permute-start.15) | collective-permute-done | bytes 131104 | tf_op jit(solution)/shard_map/ppermute | solution.py:365
  59.4 3.3 %collective-permute-done.17.refs_6_ = f32[256,128]{1,0:T(8,128)S(1)} collective-permute-done((f32[256,128]{1,0:T(8,128)S(1)}, f32[256,128]{1,0:T(8,128)S(1)}, u32[]{:S(2)}, u32[]{:S(2)}) %collective-permute-start.17) | collective-permute-done | bytes 131104 | tf_op jit(solution)/shard_map/ppermute | solution.py:366
  62.7 0.0 collective-permute-done.9.refs_0_
  62.7 1.0 %join.1 = f32[256,512]{1,0:T(8,128)} custom-call(f32[256,128]{1,0:T(8,128)S(1)} %collective-permute-done.9.refs_0_, f32[256,128]{1,0:T(8,128)S(1)} %collective-permute-done.12.refs_1_, f32[256,128]{1,0:T(8,128)S(1)} %collective-permute-done.13.refs_2_, f32[256,128]{1,0:T(8,128)S(1)} %collective-permute-done.14.refs_3_, ...), custom_call_target="tpu_custom_call" | custom-call | flops 2621440 | bytes 31457280 | tf_op jit(solution)/shard_map/join/pallas_call | solution.py:306
Async XLA Ops:
  2.8 5.5 %collective-permute-start.6 = (f32[1040,128]{1,0:T(8,128)}, f32[1040,128]{1,0:T(8,128)S(1)}, u32[]{:S(2)}, u32[]{:S(2)}) collective-permute-start(f32[1040,128]{1,0:T(8,128)} %get-tuple-element.22.refs_0_.own_ref), channel_id=1, source_target_pairs={{0,4},{1,5},{2,6},{3,7},{4,0},{5,1},{6,2},{7,3},{8,12},{9,13},{10,... | collective-permute-start | bytes 1597448 | tf_op jit(solution)/shard_map/ppermute | solution.py:353
  3.5 16.8 %collective-permute-start.2 = (f32[1040,128]{1,0:T(8,128)}, f32[1040,128]{1,0:T(8,128)S(1)}, u32[]{:S(2)}, u32[]{:S(2)}) collective-permute-start(f32[1040,128]{1,0:T(8,128)} %get-tuple-element.22.refs_0_.own_ref), channel_id=1, source_target_pairs={{0,24},{1,17},{2,18},{3,27},{4,28},{5,21},{6,22},{7,31},{8,16},{9,... | collective-permute-start | bytes 1597448 | tf_op jit(solution)/shard_map/ppermute | solution.py:352
  4.7 16.8 %collective-permute-start.4 = (f32[1040,128]{1,0:T(8,128)}, f32[1040,128]{1,0:T(8,128)S(1)}, u32[]{:S(2)}, u32[]{:S(2)}) collective-permute-start(f32[1040,128]{1,0:T(8,128)} %get-tuple-element.22.refs_0_.own_ref), channel_id=1, source_target_pairs={{0,0},{1,9},{2,10},{3,3},{4,4},{5,13},{6,14},{7,7},{8,8},{9,1},{10... | collective-permute-start | bytes 1597448 | tf_op jit(solution)/shard_map/ppermute | solution.py:352
  6.4 8.2 %collective-permute-start.1 = (f32[520,128]{1,0:T(8,128)}, f32[520,128]{1,0:T(8,128)S(1)}, u32[]{:S(2)}, u32[]{:S(2)}) collective-permute-start(f32[520,128]{1,0:T(8,128)} %get-tuple-element.21), channel_id=1, source_target_pairs={{0,1},{1,0},{2,3},{3,2},{4,5},{5,4},{6,7},{7,6},{8,9},{9,8},{10,11... | collective-permute-start | bytes 798728 | tf_op jit(solution)/shard_map/ppermute | solution.py:341
  8.2 12.1 %collective-permute-start = (f32[520,128]{1,0:T(8,128)}, f32[520,128]{1,0:T(8,128)S(1)}, u32[]{:S(2)}, u32[]{:S(2)}) collective-permute-start(f32[520,128]{1,0:T(8,128)} %get-tuple-element.20), channel_id=1, source_target_pairs={{0,1},{1,0},{2,3},{3,2},{4,5},{5,4},{6,7},{7,6},{8,9},{9,8},{10,11... | collective-permute-start | bytes 798728 | tf_op jit(solution)/shard_map/ppermute | solution.py:341
  8.3 1.0 %copy-start = (f32[1040,128]{1,0:T(8,128)S(1)}, f32[1040,128]{1,0:T(8,128)}, u32[]{:S(2)}) copy-start(f32[1040,128]{1,0:T(8,128)} %get-tuple-element.22.refs_0_.own_ref) | copy-start | bytes 1597444
  14.6 11.9 %collective-permute-start.10 = (f32[520,128]{1,0:T(8,128)S(1)}, f32[520,128]{1,0:T(8,128)S(1)}, u32[]{:S(2)}, u32[]{:S(2)}) collective-permute-start(f32[520,128]{1,0:T(8,128)S(1)} %collective-permute-done.1.refs_1_), channel_id=1, source_target_pairs={{0,0},{1,9},{2,10},{3,3},{4,4},{5,13},{6,14},{7,7},{8,8},{9,1},{10... | collective-permute-start | bytes 798728 | tf_op jit(solution)/shard_map/ppermute | solution.py:341
  15.3 11.2 %collective-permute-start.11 = (f32[520,128]{1,0:T(8,128)S(1)}, f32[520,128]{1,0:T(8,128)S(1)}, u32[]{:S(2)}, u32[]{:S(2)}) collective-permute-start(f32[520,128]{1,0:T(8,128)S(1)} %collective-permute-done.1.refs_1_), channel_id=1, source_target_pairs={{0,24},{1,17},{2,18},{3,27},{4,28},{5,21},{6,22},{7,31},{8,16},{9,... | collective-permute-start | bytes 798728 | tf_op jit(solution)/shard_map/ppermute | solution.py:341
  20.3 3.8 %collective-permute-start.3 = (f32[520,128]{1,0:T(8,128)S(1)}, f32[520,128]{1,0:T(8,128)S(1)}, u32[]{:S(2)}, u32[]{:S(2)}) collective-permute-start(f32[520,128]{1,0:T(8,128)S(1)} %collective-permute-done.refs_0_.own_ref), channel_id=1, source_target_pairs={{0,4},{1,5},{2,6},{3,7},{4,0},{5,1},{6,2},{7,3},{8,12},{9,13},{10,... | collective-permute-start | bytes 798728 | tf_op jit(solution)/shard_map/ppermute | solution.py:341
  21.5 3.4 %collective-permute-start.5 = (f32[520,128]{1,0:T(8,128)S(1)}, f32[520,128]{1,0:T(8,128)S(1)}, u32[]{:S(2)}, u32[]{:S(2)}) collective-permute-start(f32[520,128]{1,0:T(8,128)S(1)} %collective-permute-done.1.refs_1_), channel_id=1, source_target_pairs={{0,4},{1,5},{2,6},{3,7},{4,0},{5,1},{6,2},{7,3},{8,12},{9,13},{10,... | collective-permute-start | bytes 798728 | tf_op jit(solution)/shard_map/ppermute | solution.py:341
  23.4 15.2 %collective-permute-start.7 = (f32[520,128]{1,0:T(8,128)S(1)}, f32[520,128]{1,0:T(8,128)S(1)}, u32[]{:S(2)}, u32[]{:S(2)}) collective-permute-start(f32[520,128]{1,0:T(8,128)S(1)} %collective-permute-done.refs_0_.own_ref), channel_id=1, source_target_pairs={{0,0},{1,9},{2,10},{3,3},{4,4},{5,13},{6,14},{7,7},{8,8},{9,1},{10... | collective-permute-start | bytes 798728 | tf_op jit(solution)/shard_map/ppermute | solution.py:341
  24.1 15.6 %collective-permute-start.8 = (f32[520,128]{1,0:T(8,128)S(1)}, f32[520,128]{1,0:T(8,128)S(1)}, u32[]{:S(2)}, u32[]{:S(2)}) collective-permute-start(f32[520,128]{1,0:T(8,128)S(1)} %collective-permute-done.refs_0_.own_ref), channel_id=1, source_target_pairs={{0,24},{1,17},{2,18},{3,27},{4,28},{5,21},{6,22},{7,31},{8,16},{9,... | collective-permute-start | bytes 798728 | tf_op jit(solution)/shard_map/ppermute | solution.py:341
  29.3 13.5 %collective-permute-start.12 = (f32[256,128]{1,0:T(8,128)S(1)}, f32[256,128]{1,0:T(8,128)S(1)}, u32[]{:S(2)}, u32[]{:S(2)}) collective-permute-start(f32[256,128]{1,0:T(8,128)S(1)} %get-tuple-element.28), channel_id=1, source_target_pairs={{0,0},{1,1},{2,2},{3,3},{4,4},{5,5},{6,6},{7,7},{8,9},{9,8},{10,11... | collective-permute-start | bytes 393224 | tf_op jit(solution)/shard_map/ppermute | solution.py:367
  36.7 10.4 %collective-permute-start.14 = (f32[256,128]{1,0:T(8,128)S(1)}, f32[256,128]{1,0:T(8,128)S(1)}, u32[]{:S(2)}, u32[]{:S(2)}) collective-permute-start(f32[256,128]{1,0:T(8,128)S(1)} %get-tuple-element.30), channel_id=1, source_target_pairs={{0,4},{1,5},{2,6},{3,7},{4,0},{5,1},{6,2},{7,3},{8,13},{9,12},{10,... | collective-permute-start | bytes 393224 | tf_op jit(solution)/shard_map/ppermute | solution.py:368
  36.8 10.3 %collective-permute-start.16 = (f32[256,128]{1,0:T(8,128)S(1)}, f32[256,128]{1,0:T(8,128)S(1)}, u32[]{:S(2)}, u32[]{:S(2)}) collective-permute-start(f32[256,128]{1,0:T(8,128)S(1)} %get-tuple-element.32), channel_id=1, source_target_pairs={{0,3},{1,2},{2,1},{3,0},{4,7},{5,6},{6,5},{7,4},{8,10},{9,11},{10,... | collective-permute-start | bytes 393224 | tf_op jit(solution)/shard_map/ppermute | solution.py:365
  38.7 17.7 %collective-permute-start.18 = (f32[256,128]{1,0:T(8,128)S(1)}, f32[256,128]{1,0:T(8,128)S(1)}, u32[]{:S(2)}, u32[]{:S(2)}) collective-permute-start(f32[256,128]{1,0:T(8,128)S(1)} %get-tuple-element.34), channel_id=1, source_target_pairs={{0,7},{1,6},{2,5},{3,4},{4,3},{5,2},{6,1},{7,0},{8,14},{9,15},{10,... | collective-permute-start | bytes 393224 | tf_op jit(solution)/shard_map/ppermute | solution.py:366
  42.3 14.1 %collective-permute-start.13 = (f32[256,128]{1,0:T(8,128)S(1)}, f32[256,128]{1,0:T(8,128)S(1)}, u32[]{:S(2)}, u32[]{:S(2)}) collective-permute-start(f32[256,128]{1,0:T(8,128)S(1)} %get-tuple-element.29), channel_id=1, source_target_pairs={{0,4},{1,5},{2,6},{3,7},{4,0},{5,1},{6,2},{7,3},{8,13},{9,12},{10,... | collective-permute-start | bytes 393224 | tf_op jit(solution)/shard_map/ppermute | solution.py:368
  42.8 16.6 %collective-permute-start.15 = (f32[256,128]{1,0:T(8,128)S(1)}, f32[256,128]{1,0:T(8,128)S(1)}, u32[]{:S(2)}, u32[]{:S(2)}) collective-permute-start(f32[256,128]{1,0:T(8,128)S(1)} %get-tuple-element.31), channel_id=1, source_target_pairs={{0,3},{1,2},{2,1},{3,0},{4,7},{5,6},{6,5},{7,4},{8,10},{9,11},{10,... | collective-permute-start | bytes 393224 | tf_op jit(solution)/shard_map/ppermute | solution.py:365
  47.1 15.6 %collective-permute-start.17 = (f32[256,128]{1,0:T(8,128)S(1)}, f32[256,128]{1,0:T(8,128)S(1)}, u32[]{:S(2)}, u32[]{:S(2)}) collective-permute-start(f32[256,128]{1,0:T(8,128)S(1)} %get-tuple-element.33), channel_id=1, source_target_pairs={{0,7},{1,6},{2,5},{3,4},{4,3},{5,2},{6,1},{7,0},{8,14},{9,15},{10,... | collective-permute-start | bytes 393224 | tf_op jit(solution)/shard_map/ppermute | solution.py:366
  47.1 15.6 %collective-permute-start.9 = (f32[256,128]{1,0:T(8,128)S(1)}, f32[256,128]{1,0:T(8,128)S(1)}, u32[]{:S(2)}, u32[]{:S(2)}) collective-permute-start(f32[256,128]{1,0:T(8,128)S(1)} %get-tuple-element.26), channel_id=1, source_target_pairs={{0,0},{1,1},{2,2},{3,3},{4,4},{5,5},{6,6},{7,7},{8,9},{9,8},{10,11... | collective-permute-start | bytes 393224 | tf_op jit(solution)/shard_map/ppermute | solution.py:367

commit v2 on v1

v2 whole, which is shorter than its diff:
```python
import functools

import jax
import jax.numpy as jnp
from jax import lax
from jax.experimental import pallas as pl
from jax.experimental.pallas import tpu as pltpu
from jax.sharding import PartitionSpec as P

TB = 128
RB = 2
CB_DEV = 16
PANEL = RB * TB
META = 8
FEW = 5
CUTS = 2
CUT = TB // CUTS
AXES = ("rows", "cols")
VMEM_LIMIT = 16 * 1024 * 1024
PACK_LIMIT = 60 * 1024 * 1024
VSPEC = pl.BlockSpec(memory_space=pltpu.VMEM)
HSPEC = pl.BlockSpec(memory_space=pltpu.HBM)


def params(limit=VMEM_LIMIT):
    return pltpu.CompilerParams(vmem_limit_bytes=limit)


def cost(flops, nbytes):
    return pl.CostEstimate(flops=flops * 20, bytes_accessed=nbytes * 20, transcendentals=0)


def pack_kernel(slots, rows_hbm, cols_hbm, counts_hbm, tiles_hbm, scale_hbm, *refs):
    whole_ref, rows_ref, cols_ref, counts_ref, tiles_ref, scale_ref, sems = refs
    copies = [
        pltpu.make_async_copy(source, target, sems.at[index])
        for index, (source, target) in enumerate(
            (
                (rows_hbm, rows_ref),
                (cols_hbm, cols_ref),
                (counts_hbm, counts_ref),
                (scale_hbm, scale_ref),
                (tiles_hbm, tiles_ref),
            )
        )
    ]
    for copy in copies:
        copy.start()
    for copy in copies[:4]:
        copy.wait()
    lane = lax.broadcasted_iota(jnp.int32, (META, TB), 1)
    codes = jnp.full((META, TB), -1.0, jnp.float32)
    count = counts_ref[0, 0]
    factors = []
    for slot in range(slots):
        live = slot < count
        row = rows_ref[0, slot]
        col = cols_ref[0, slot]
        factors.append(jnp.where(live, jnp.sqrt(scale_ref[pl.ds(col, 1), :]), 0.0))
        code = jnp.where(live, col * RB + row, -1).astype(jnp.float32)
        codes = jnp.where(lane == slot, code, codes)
    copies[4].wait()
    for slot in range(slots):
        for cut in range(CUTS):
            start = cut * (slots * CUT + META) + slot * CUT
            part = tiles_ref[0, slot, cut * CUT : (cut + 1) * CUT, :]
            whole_ref[start : start + CUT, :] = part * factors[slot]
    for cut in range(CUTS):
        start = cut * (slots * CUT + META) + slots * CUT
        whole_ref[start : start + META, :] = codes


def pack(tiles, tile_rows, tile_cols, counts, scaling):
    slots = tiles.shape[1]
    piece = slots * CUT + META
    return pl.pallas_call(
        functools.partial(pack_kernel, slots),
        out_shape=jax.ShapeDtypeStruct((CUTS * piece, TB), jnp.float32),
        in_specs=[HSPEC] * 5,
        out_specs=VSPEC,
        scratch_shapes=[
            pltpu.SMEM(tile_rows.shape, jnp.int32),
            pltpu.SMEM(tile_cols.shape, jnp.int32),
            pltpu.SMEM(counts.shape, jnp.int32),
            pltpu.VMEM(tiles.shape, jnp.float32),
            pltpu.VMEM((CB_DEV, TB), jnp.float32),
            pltpu.SemaphoreType.DMA((5,)),
        ],
        compiler_params=params(PACK_LIMIT),
        cost_estimate=cost(slots * TB * TB, 3 * slots * TB * TB * 4),
        name="pack",
    )(tile_rows, tile_cols, counts, tiles, scaling.reshape(CB_DEV, TB))


def read_codes(piece_ref, slots):
    row = piece_ref[slots * CUT : slots * CUT + META, :].astype(jnp.int32)
    return [row[0, slot] for slot in range(slots)]


def spread_kernel(slots, own_ref, other_ref, dense_ref, sum_ref, used_ref):
    codes = [read_codes(piece_ref, slots) for piece_ref in (own_ref, other_ref)]
    for col in range(CB_DEV):
        used_ref[col] = 0
    for side in range(2):
        for slot in range(slots):
            code = codes[side][slot]

            @pl.when(code >= 0)
            def _(code=code, slot=slot, side=side):
                col = code >> 1

                @pl.when(used_ref[col] == 0)
                def _():
                    used_ref[col] = 1
                    sum_ref[col] = jnp.zeros_like(sum_ref[col])

                start = pl.multiple_of(side * PANEL + (code & 1) * TB, TB)
                for cut in range(CUTS):
                    piece_ref = own_ref if side == 0 else other_ref
                    base = cut * (slots * CUT + META) + slot * CUT
                    place = pl.ds(start + cut * CUT, CUT)
                    sum_ref[col, place, :] += piece_ref[base : base + CUT, :]

    def convert(col, carry):
        @pl.when(used_ref[col] == 1)
        def _():
            high, low = split(sum_ref[col])
            dense_ref[col, :, :TB] = high
            dense_ref[col, :, TB:] = low

        @pl.when(used_ref[col] == 0)
        def _():
            dense_ref[col] = jnp.zeros_like(dense_ref[col])

        return carry

    lax.fori_loop(0, CB_DEV, convert, 0)


def spread(own, other, slots):
    return pl.pallas_call(
        functools.partial(spread_kernel, slots),
        out_shape=jax.ShapeDtypeStruct((CB_DEV, 2 * PANEL, 2 * TB), jnp.bfloat16),
        in_specs=[VSPEC] * 2,
        out_specs=VSPEC,
        scratch_shapes=[
            pltpu.VMEM((CB_DEV, 2 * PANEL, TB), jnp.float32),
            pltpu.SMEM((CB_DEV,), jnp.int32),
        ],
        compiler_params=params(),
        cost_estimate=cost(1 << 20, 1 << 21),
        name="spread",
    )(own, other)


def split(x):
    high = x.astype(jnp.bfloat16)
    low = (x - high.astype(jnp.float32)).astype(jnp.bfloat16)
    return high, low


def nt_dot(a, b):
    return lax.dot_general(a, b, (((1,), (1,)), ((), ())), preferred_element_type=jnp.float32)


def product(left, tile):
    high, low = split(tile)
    right = jnp.concatenate(
        [jnp.concatenate([high, high], axis=1), jnp.concatenate([low, low], axis=1)], axis=0
    )
    return nt_dot(left, right)


def for_tiles(slots, piece_refs, body):
    codes = [read_codes(piece_ref, slots) for piece_ref in piece_refs]
    core = lax.axis_index("rows") & 1

    def some(which, slot_range):
        for slot in slot_range:
            code = jnp.maximum(codes[which][slot], 0)
            body(which, slot, code >> 1, core if which == 0 else 1 - core, code & 1)

    few = min(FEW, slots)
    for which in range(2):
        some(which, range(few))
    if few < slots:
        for which in range(2):

            @pl.when(codes[which][few] >= 0)
            def _(which=which):
                some(which, range(few, slots))


def first_kernel(slots, dense_ref, a_ref, b_ref, acc_ref):
    acc_ref[...] = jnp.zeros_like(acc_ref)

    def body(which, slot, col, panel, block):
        piece_ref = a_ref if which == 0 else b_ref
        starts = [cut * (slots * CUT + META) + slot * CUT for cut in range(CUTS)]
        tile = jnp.concatenate([piece_ref[start : start + CUT, :] for start in starts], axis=0)
        both = product(dense_ref[col], tile)
        acc_ref[panel, block] += both[:, :TB] + both[:, TB:]

    for_tiles(slots, (a_ref, b_ref), body)


def first(dense, right_a, right_b, slots):
    return pl.pallas_call(
        functools.partial(first_kernel, slots),
        out_shape=jax.ShapeDtypeStruct((2, RB, 2 * PANEL, TB), jnp.float32),
        in_specs=[VSPEC] * 3,
        out_specs=VSPEC,
        compiler_params=params(),
        cost_estimate=cost(slots * 4 * 4 * PANEL * TB * TB, 1 << 22),
        name="first",
    )(dense, right_a, right_b)


def second_kernel(slots, cut, dense_ref, acc_ref, a_ref, b_ref, own_ref, other_ref, sum_ref):
    sum_ref[...] = jnp.zeros_like(sum_ref)

    def body(which, slot, col, panel, block):
        piece_ref = a_ref if which == 0 else b_ref
        sum_ref[panel, block] += product(dense_ref[col], piece_ref[slot * CUT : (slot + 1) * CUT, :])

    for_tiles(slots, (a_ref, b_ref), body)
    for side, out_ref in enumerate((own_ref, other_ref)):
        rows = slice(side * PANEL, (side + 1) * PANEL)
        parts = []
        for panel in range(2):
            for block in range(RB):
                both = sum_ref[panel, block, rows, :]
                before = acc_ref[panel, block, rows, cut * CUT : (cut + 1) * CUT]
                parts.append(both[:, :CUT] + both[:, CUT:] + before)
        out_ref[...] = jnp.concatenate(parts, axis=1)


def second(cut, dense, acc, piece_a, piece_b, slots):
    shape = jax.ShapeDtypeStruct((PANEL, 2 * RB * CUT), jnp.float32)
    return pl.pallas_call(
        functools.partial(second_kernel, slots, cut),
        out_shape=[shape] * 2,
        in_specs=[VSPEC] * 4,
        out_specs=[VSPEC] * 2,
        scratch_shapes=[pltpu.VMEM((2, RB, 2 * PANEL, 2 * CUT), jnp.float32)],
        compiler_params=params(),
        cost_estimate=cost(slots * 2 * 4 * PANEL * TB * TB, 1 << 21),
        name="second",
    )(dense, acc, piece_a, piece_b)


def join_kernel(*refs):
    out_ref = refs[-1]
    for place in range(2 * RB):
        lanes = slice(place * CUT, (place + 1) * CUT)
        parts = [refs[cut][:, lanes] + refs[CUTS + cut][:, lanes] for cut in range(CUTS)]
        out_ref[:, place * TB : (place + 1) * TB] = parts[0] if CUTS == 1 else jnp.concatenate(parts, axis=1)


def join(from_same, from_cross):
    return pl.pallas_call(
        join_kernel,
        out_shape=jax.ShapeDtypeStruct((PANEL, 2 * PANEL), jnp.float32),
        in_specs=[VSPEC] * (2 * CUTS),
        out_specs=VSPEC,
        compiler_params=params(),
        cost_estimate=cost(1 << 17, 1 << 17),
        name="join",
    )(*from_same, *from_cross)


def chunk(k, i, p):
    return k ^ p ^ (3 * i)


def pairs(place):
    out = []
    for row in range(8):
        for col in range(4):
            chip, core, plane = place(row >> 1, row & 1, col)
            out.append((row * 4 + col, (chip * 2 + core) * 4 + plane))
    return out


SWAP = pairs(lambda k, i, p: (k, 1 - i, p))
NEXT = pairs(lambda k, i, p: (k, i, p ^ 1))
SEND_SAME = pairs(lambda k, i, p: (chunk(k, i, p), i, p))
SEND_CROSS = pairs(lambda k, i, p: (chunk(k, 1 - i, p), 1 - i, p))
DONE_SAME = pairs(lambda k, i, p: (k, i, chunk(k, i, p)))
DONE_CROSS = pairs(lambda k, i, p: (k, 1 - i, chunk(k, i, p)))


def send(pieces, perms):
    return [lax.ppermute(piece, AXES, perm) for piece, perm in zip(pieces, perms)]


def after(x, *others):
    return lax.optimization_barrier((x, *others))[0]


def per_device(tiles, tile_rows, tile_cols, counts, scaling):
    slots = tiles.shape[1]
    own = pack(tiles, tile_rows, tile_cols, counts, scaling)
    piece = slots * CUT + META
    near_own = lax.ppermute(own, AXES, NEXT)
    own_a, own_b, own_other = send([own] * 3, (SEND_SAME, SEND_CROSS, SWAP))
    own_dense = spread(own, own_other, slots)
    acc = first(own_dense, own_a, own_b, slots)
    near_other = lax.ppermute(after(near_own, own_dense), AXES, SWAP)
    near_dense = spread(near_own, near_other, slots)
    starts = (after(near_own, own_dense), after(near_own, own_dense))
    from_same, from_cross = [], []
    for cut in range(CUTS):
        part = lax.slice_in_dim(starts[cut], cut * piece, (cut + 1) * piece)
        part_a, part_b = send([part] * 2, (SEND_SAME, SEND_CROSS))
        kept, other = second(cut, near_dense, acc, part_a, part_b, slots)
        from_same.append(lax.ppermute(kept, AXES, DONE_SAME))
        from_cross.append(lax.ppermute(other, AXES, DONE_CROSS))
    return join(from_same, from_cross)


def densify(tile_set, row_ids, col_ids, live_mask, scale_set, block_count):
    placed = jnp.zeros((block_count, RB, TB, TB), jnp.float32)
    placed = placed.at[col_ids, row_ids].add(tile_set * live_mask[:, None, None])
    placed = placed * scale_set[:, None, None, :]
    return placed.reshape(block_count, RB * TB, TB)


def place_panels(blocked, tile_set, row_ids, col_ids, live_mask, panel_count):
    picked = jnp.take(blocked, col_ids, axis=0)
    product = jnp.einsum("kac,kbc->kab", picked, tile_set, precision=lax.Precision.HIGHEST)
    product = product.reshape(panel_count, -1, RB * TB, TB)
    hit_row = (row_ids[:, None] == jnp.arange(RB, dtype=jnp.int32)[None, :]).astype(
        jnp.float32
    ) * live_mask[:, None]
    hit_row = hit_row.reshape(panel_count, -1, RB)
    placed = jnp.einsum("pkr,pkab->aprb", hit_row, product, precision=lax.Precision.HIGHEST)
    return placed.reshape(RB * TB, panel_count * RB * TB)


def per_device_any(tiles, tile_rows, tile_cols, counts, scaling):
    slot_total = tiles.shape[1]
    slot_range = jnp.arange(slot_total, dtype=jnp.int32)
    own_live = (slot_range < counts[0, 0]).astype(jnp.float32)
    blocked = densify(
        tiles[0], tile_rows[0], tile_cols[0], own_live, scaling.reshape(CB_DEV, TB), CB_DEV
    )
    piece_tiles = lax.all_gather(tiles, "rows", axis=0, tiled=True)
    piece_rows = lax.all_gather(tile_rows, "rows", axis=0, tiled=True)
    piece_cols = lax.all_gather(tile_cols, "rows", axis=0, tiled=True)
    piece_counts = lax.all_gather(counts, "rows", axis=0, tiled=True)
    count_here = piece_tiles.shape[0]
    live_mask = (slot_range[None, :] < piece_counts).astype(jnp.float32).reshape(-1)
    tile_block = place_panels(
        blocked,
        piece_tiles.reshape(count_here * slot_total, TB, TB),
        piece_rows.reshape(-1),
        piece_cols.reshape(-1),
        live_mask,
        count_here,
    )
    return lax.psum_scatter(tile_block, "cols", scatter_dimension=1, tiled=True)


def solution(mesh):
    placed = (
        P("rows", "cols", None, None),
        P("rows", "cols"),
        P("rows", "cols"),
        P("rows", "cols"),
        P("cols"),
    )
    small = mesh.shape["rows"] == 8 and mesh.shape["cols"] == 4
    return jax.shard_map(
        per_device if small else per_device_any,
        mesh=mesh,
        in_specs=placed,
        out_specs=P("rows", "cols"),
        check_vma=False,
    )
```

time: 64.2 us -> 61.7 us (0.961)
  starting transfers between devices: 26 us -> 22.9 us
  waiting for transfers between devices: 22.3 us -> 25.3 us
  Pallas kernels: 13.6 us -> 11.4 us
    ppermute x19 -> x13, starting transfers between devices: 26 us -> 22.9 us  [the longest x7 11.3 us: send(): lax.ppermute(piece, AXES, perm)]
    ppermute x19 -> x13, waiting for transfers between devices: 22.3 us -> 25.3 us  [the longest x2 14.7 us: per_device(): from_cross.append(lax.ppermute(other, AXES, DONE_CROSS))]
    pallas_call x2, Pallas kernels: 5.36 us -> 4.15 us  [second(): pl.pallas_call(functools.partial(second_kernel, slots, cut), out_shape=[s...]
    pallas_call x4, Pallas kernels: 6.36 us -> 5.67 us  [the longest x2 2.73 us: spread(): pl.pallas_call(functools.partial(spread_kernel, slots), out_shape=jax.Sha...]
  transfers between devices with their start and end apart: 19 -> 13, of which waited for: 7 -> 6; matrix products, arithmetic and copies ran while one was open for 0% -> 0% of each run, Pallas kernels for 16% -> 14%
where the time goes in v2:
time: 61.7 us; the launch traced here: 61.5 us
  waiting for transfers between devices  25.3 us (41%)
  starting transfers between devices  22.9 us (37%)
  Pallas kernels  11.4 us (18%)
  local copies, waits for them, and re-layouts  1.07 us (2%)
  between operations  0.82 us (1%)
    ppermute x2, waiting for transfers between devices, per_device(): from_cross.append(lax.ppermute(other, AXES, DONE_CROSS))  14.7 us
    ppermute x7, starting transfers between devices, send(): lax.ppermute(piece, AXES, perm)  11.3 us
    ppermute x2, starting transfers between devices, per_device(): from_same.append(lax.ppermute(kept, AXES, DONE_SAME))  7.15 us
    ppermute x1, waiting for transfers between devices, per_device(): near_own = lax.ppermute(own, AXES, NEXT)  6.78 us
    pallas_call x2, Pallas kernels, second(): pl.pallas_call(functools.partial(second_kernel, slots, cut), out_shape=[s...  4.15 us
    ppermute x2, starting transfers between devices, per_device(): from_cross.append(lax.ppermute(other, AXES, DONE_CROSS))  3.11 us
    ppermute x2, waiting for transfers between devices, per_device(): from_same.append(lax.ppermute(kept, AXES, DONE_SAME))  2.78 us
    pallas_call x2, Pallas kernels, spread(): pl.pallas_call(functools.partial(spread_kernel, slots), out_shape=jax.Sha...  2.73 us
  transfers between devices with their start and end apart: 13, of which 6 were waited for; matrix products, arithmetic and copies ran while one was open for 0% of the time, Pallas kernels for 14%

profile of v2, /device:TPU:5, one launch (start us, length us, event | category | flops | bytes accessed | tf_op | source)
XLA Modules:
  0.0 61.5 jit_solution(9602826883461977541)
XLA Ops:
  0.7 1.9 %pack.1.own_ref = f32[1040,128]{1,0:T(8,128)} custom-call(s32[1,8]{1,0:T(1,128)} %rows_hbm.1, s32[1,8]{1,0:T(1,128)} %cols_hbm.1, s32[1,1]{1,0:T(1,128)S(6)} %copy.6.counts_hbm, f32[1,8,128,128]{3,2,1,0:T(8,128)} %tiles_hbm.1, f32[16,128]{1,0:T(8,128)} %bitcast.1), custom_call_target="tpu_custom_call" | custom-call | flops 2621440 | bytes 31457280 | tf_op jit(solution)/shard_map/pack/pallas_call | solution.py:76
  2.6 0.7 %collective-permute-start.1 = (f32[1040,128]{1,0:T(8,128)}, f32[1040,128]{1,0:T(8,128)S(1)}, u32[]{:S(2)}, u32[]{:S(2)}) collective-permute-start(f32[1040,128]{1,0:T(8,128)} %pack.1.own_ref), channel_id=1, source_target_pairs={{0,4},{1,5},{2,6},{3,7},{4,0},{5,1},{6,2},{7,3},{8,12},{9,13},{10,... | collective-permute-start | bytes 1597448 | tf_op jit(solution)/shard_map/ppermute | solution.py:294
  3.3 1.3 %collective-permute-start = (f32[1040,128]{1,0:T(8,128)}, f32[1040,128]{1,0:T(8,128)S(1)}, u32[]{:S(2)}, u32[]{:S(2)}) collective-permute-start(f32[1040,128]{1,0:T(8,128)} %pack.1.own_ref), channel_id=1, source_target_pairs={{0,1},{1,0},{2,3},{3,2},{4,5},{5,4},{6,7},{7,6},{8,9},{9,8},{10,11... | collective-permute-start | bytes 1597448 | tf_op jit(solution)/shard_map/ppermute | solution.py:305
  4.6 0.3 collective-permute-start.4
  5.0 3.0 %collective-permute-start.3 = (f32[1040,128]{1,0:T(8,128)}, f32[1040,128]{1,0:T(8,128)S(1)}, u32[]{:S(2)}, u32[]{:S(2)}) collective-permute-start(f32[1040,128]{1,0:T(8,128)} %pack.1.own_ref), channel_id=1, source_target_pairs={{0,0},{1,9},{2,18},{3,27},{4,28},{5,21},{6,14},{7,7},{8,8},{9,1},{... | collective-permute-start | bytes 1597448 | tf_op jit(solution)/shard_map/ppermute | solution.py:294
  8.0 0.0 collective-permute-done.1.other_ref
  8.1 0.0 copy-start
  8.1 1.0 %copy-done = f32[1040,128]{1,0:T(8,128)S(1)} copy-done((f32[1040,128]{1,0:T(8,128)S(1)}, f32[1040,128]{1,0:T(8,128)}, u32[]{:S(2)}) %copy-start) | copy-done | bytes 532504
  9.1 1.3 %spread.2.dense_ref = bf16[16,512,256]{2,1,0:T(8,128)(2,1)S(1)} custom-call(f32[1040,128]{1,0:T(8,128)S(1)} %copy-done, f32[1040,128]{1,0:T(8,128)S(1)} %collective-permute-done.1.other_ref), custom_call_target="tpu_custom_call" | custom-call | flops 20971520 | bytes 41943040 | tf_op jit(solution)/shard_map/spread/pallas_call | solution.py:141
  10.4 6.8 %collective-permute-done.own_ref = f32[1040,128]{1,0:T(8,128)S(1)} collective-permute-done((f32[1040,128]{1,0:T(8,128)}, f32[1040,128]{1,0:T(8,128)S(1)}, u32[]{:S(2)}, u32[]{:S(2)}) %collective-permute-start) | collective-permute-done | bytes 532512 | tf_op jit(solution)/shard_map/ppermute | solution.py:305
  17.3 0.9 %collective-permute-start.9 = (f32[520,128]{1,0:T(8,128)S(1)}, f32[520,128]{1,0:T(8,128)S(1)}, u32[]{:S(2)}, u32[]{:S(2)}) collective-permute-start(f32[520,128]{1,0:T(8,128)S(1)} %get-tuple-element.15), channel_id=1, source_target_pairs={{0,28},{1,21},{2,14},{3,7},{4,0},{5,9},{6,18},{7,27},{8,20},{9,29}... | collective-permute-start | bytes 798728 | tf_op jit(solution)/shard_map/ppermute | solution.py:294
  18.2 3.0 %collective-permute-start.8 = (f32[520,128]{1,0:T(8,128)S(1)}, f32[520,128]{1,0:T(8,128)S(1)}, u32[]{:S(2)}, u32[]{:S(2)}) collective-permute-start(f32[520,128]{1,0:T(8,128)S(1)} %get-tuple-element.15), channel_id=1, source_target_pairs={{0,0},{1,9},{2,18},{3,27},{4,28},{5,21},{6,14},{7,7},{8,8},{9,1},{... | collective-permute-start | bytes 798728 | tf_op jit(solution)/shard_map/ppermute | solution.py:294
  21.2 0.1 collective-permute-start.6
  21.3 0.0 collective-permute-done.4.b_ref
  21.3 3.1 %collective-permute-start.5 = (f32[520,128]{1,0:T(8,128)S(1)}, f32[520,128]{1,0:T(8,128)S(1)}, u32[]{:S(2)}, u32[]{:S(2)}) collective-permute-start(f32[520,128]{1,0:T(8,128)S(1)} %get-tuple-element.16), channel_id=1, source_target_pairs={{0,0},{1,9},{2,18},{3,27},{4,28},{5,21},{6,14},{7,7},{8,8},{9,1},{... | collective-permute-start | bytes 798728 | tf_op jit(solution)/shard_map/ppermute | solution.py:294
  24.4 0.0 collective-permute-done.3.a_ref
  24.4 0.1 collective-permute-start.2
  24.5 1.6 %first.1.acc_ref = f32[2,2,512,128]{3,2,1,0:T(8,128)S(1)} custom-call(bf16[16,512,256]{2,1,0:T(8,128)(2,1)S(1)} %spread.2.dense_ref, f32[1040,128]{1,0:T(8,128)S(1)} %collective-permute-done.3.a_ref, f32[1040,128]{1,0:T(8,128)S(1)} %collective-permute-done.4.b_ref), custom_call_target="tpu_custom_call" | custom-call | flops 10737418240 | bytes 83886080 | tf_op jit(solution)/shard_map/first/pallas_call | solution.py:208
  26.1 0.3 collective-permute-done.2.other_ref
  26.4 1.4 %spread.3.dense_ref = bf16[16,512,256]{2,1,0:T(8,128)(2,1)S(1)} custom-call(f32[1040,128]{1,0:T(8,128)S(1)} %collective-permute-done.own_ref, f32[1040,128]{1,0:T(8,128)S(1)} %collective-permute-done.2.other_ref), custom_call_target="tpu_custom_call" | custom-call | flops 20971520 | bytes 41943040 | tf_op jit(solution)/shard_map/spread/pallas_call | solution.py:141
  27.8 0.0 collective-permute-done.9.b_ref
  27.8 0.7 %collective-permute-done.8.a_ref = f32[520,128]{1,0:T(8,128)S(1)} collective-permute-done((f32[520,128]{1,0:T(8,128)S(1)}, f32[520,128]{1,0:T(8,128)S(1)}, u32[]{:S(2)}, u32[]{:S(2)}) %collective-permute-start.8) | collective-permute-done | bytes 266272 | tf_op jit(solution)/shard_map/ppermute | solution.py:294
  28.6 2.2 %second.3 = (f32[256,256]{1,0:T(8,128)S(1)}, f32[256,256]{1,0:T(8,128)S(1)}) custom-call(bf16[16,512,256]{2,1,0:T(8,128)(2,1)S(1)} %spread.3.dense_ref, f32[2,2,512,128]{3,2,1,0:T(8,128)S(1)} %first.1.acc_ref, f32[520,128]{1,0:T(8,128)S(1)} %collective-permute-done.8.a_ref, f32[520,128]{1,0:T(8,128)S(1)} %collective-permute-done.9.b_ref), custom_call_target="tpu_custom_call" | custom-call | flops 5368709120 | bytes 41943040 | tf_op jit(solution)/shard_map/second/pallas_call | solution.py:240
  30.8 4.2 %collective-permute-start.10 = (f32[256,256]{1,0:T(8,128)S(1)}, f32[256,256]{1,0:T(8,128)S(1)}, u32[]{:S(2)}, u32[]{:S(2)}) collective-permute-start(f32[256,256]{1,0:T(8,128)S(1)} %get-tuple-element.12), channel_id=1, source_target_pairs={{0,0},{1,1},{2,2},{3,3},{4,7},{5,6},{6,5},{7,4},{8,9},{9,8},{10,11... | collective-permute-start | bytes 786440 | tf_op jit(solution)/shard_map/ppermute | solution.py:317
  35.0 3.0 %collective-permute-start.12 = (f32[256,256]{1,0:T(8,128)S(1)}, f32[256,256]{1,0:T(8,128)S(1)}, u32[]{:S(2)}, u32[]{:S(2)}) collective-permute-start(f32[256,256]{1,0:T(8,128)S(1)} %get-tuple-element.14), channel_id=1, source_target_pairs={{0,4},{1,5},{2,6},{3,7},{4,3},{5,2},{6,1},{7,0},{8,13},{9,12},{10,... | collective-permute-start | bytes 786440 | tf_op jit(solution)/shard_map/ppermute | solution.py:318
  38.0 0.0 collective-permute-done.6.b_ref
  38.0 0.0 collective-permute-done.5.a_ref
  38.0 1.9 %second.2 = (f32[256,256]{1,0:T(8,128)S(1)}, f32[256,256]{1,0:T(8,128)S(1)}) custom-call(bf16[16,512,256]{2,1,0:T(8,128)(2,1)S(1)} %spread.3.dense_ref, f32[2,2,512,128]{3,2,1,0:T(8,128)S(1)} %first.1.acc_ref, f32[520,128]{1,0:T(8,128)S(1)} %collective-permute-done.5.a_ref, f32[520,128]{1,0:T(8,128)S(1)} %collective-permute-done.6.b_ref), custom_call_target="tpu_custom_call" | custom-call | flops 5368709120 | bytes 41943040 | tf_op jit(solution)/shard_map/second/pallas_call | solution.py:240
  40.0 3.0 %collective-permute-start.7 = (f32[256,256]{1,0:T(8,128)S(1)}, f32[256,256]{1,0:T(8,128)S(1)}, u32[]{:S(2)}, u32[]{:S(2)}) collective-permute-start(f32[256,256]{1,0:T(8,128)S(1)} %get-tuple-element.11), channel_id=1, source_target_pairs={{0,0},{1,1},{2,2},{3,3},{4,7},{5,6},{6,5},{7,4},{8,9},{9,8},{10,11... | collective-permute-start | bytes 786440 | tf_op jit(solution)/shard_map/ppermute | solution.py:317
  43.0 0.1 collective-permute-start.11
  43.0 0.0 collective-permute-done.10.refs_1_
  43.0 5.6 %collective-permute-done.12.refs_3_ = f32[256,256]{1,0:T(8,128)S(1)} collective-permute-done((f32[256,256]{1,0:T(8,128)S(1)}, f32[256,256]{1,0:T(8,128)S(1)}, u32[]{:S(2)}, u32[]{:S(2)}) %collective-permute-start.12) | collective-permute-done | bytes 262176 | tf_op jit(solution)/shard_map/ppermute | solution.py:318
  48.7 2.8 %collective-permute-done.7.refs_0_ = f32[256,256]{1,0:T(8,128)S(1)} collective-permute-done((f32[256,256]{1,0:T(8,128)S(1)}, f32[256,256]{1,0:T(8,128)S(1)}, u32[]{:S(2)}, u32[]{:S(2)}) %collective-permute-start.7) | collective-permute-done | bytes 262176 | tf_op jit(solution)/shard_map/ppermute | solution.py:317
  51.5 9.0 %collective-permute-done.11.refs_2_ = f32[256,256]{1,0:T(8,128)S(1)} collective-permute-done((f32[256,256]{1,0:T(8,128)S(1)}, f32[256,256]{1,0:T(8,128)S(1)}, u32[]{:S(2)}, u32[]{:S(2)}) %collective-permute-start.11) | collective-permute-done | bytes 262176 | tf_op jit(solution)/shard_map/ppermute | solution.py:318
  60.5 1.0 %join.1 = f32[256,512]{1,0:T(8,128)} custom-call(f32[256,256]{1,0:T(8,128)S(1)} %collective-permute-done.7.refs_0_, f32[256,256]{1,0:T(8,128)S(1)} %collective-permute-done.10.refs_1_, f32[256,256]{1,0:T(8,128)S(1)} %collective-permute-done.11.refs_2_, f32[256,256]{1,0:T(8,128)S(1)} %collective-permute-done.12.refs_3_), custom_call_target="tpu_custom_call" | custom-call | flops 2621440 | bytes 2621440 | tf_op jit(solution)/shard_map/join/pallas_call | solution.py:261
  (1 shorter events, 0.0 us)
Async XLA Ops:
  2.6 5.5 %collective-permute-start.1 = (f32[1040,128]{1,0:T(8,128)}, f32[1040,128]{1,0:T(8,128)S(1)}, u32[]{:S(2)}, u32[]{:S(2)}) collective-permute-start(f32[1040,128]{1,0:T(8,128)} %pack.1.own_ref), channel_id=1, source_target_pairs={{0,4},{1,5},{2,6},{3,7},{4,0},{5,1},{6,2},{7,3},{8,12},{9,13},{10,... | collective-permute-start | bytes 1597448 | tf_op jit(solution)/shard_map/ppermute | solution.py:294
  3.3 13.9 %collective-permute-start = (f32[1040,128]{1,0:T(8,128)}, f32[1040,128]{1,0:T(8,128)S(1)}, u32[]{:S(2)}, u32[]{:S(2)}) collective-permute-start(f32[1040,128]{1,0:T(8,128)} %pack.1.own_ref), channel_id=1, source_target_pairs={{0,1},{1,0},{2,3},{3,2},{4,5},{5,4},{6,7},{7,6},{8,9},{9,8},{10,11... | collective-permute-start | bytes 1597448 | tf_op jit(solution)/shard_map/ppermute | solution.py:305
  4.6 16.6 %collective-permute-start.4 = (f32[1040,128]{1,0:T(8,128)}, f32[1040,128]{1,0:T(8,128)S(1)}, u32[]{:S(2)}, u32[]{:S(2)}) collective-permute-start(f32[1040,128]{1,0:T(8,128)} %pack.1.own_ref), channel_id=1, source_target_pairs={{0,28},{1,21},{2,14},{3,7},{4,0},{5,9},{6,18},{7,27},{8,20},{9,29}... | collective-permute-start | bytes 1597448 | tf_op jit(solution)/shard_map/ppermute | solution.py:294
  5.0 19.4 %collective-permute-start.3 = (f32[1040,128]{1,0:T(8,128)}, f32[1040,128]{1,0:T(8,128)S(1)}, u32[]{:S(2)}, u32[]{:S(2)}) collective-permute-start(f32[1040,128]{1,0:T(8,128)} %pack.1.own_ref), channel_id=1, source_target_pairs={{0,0},{1,9},{2,18},{3,27},{4,28},{5,21},{6,14},{7,7},{8,8},{9,1},{... | collective-permute-start | bytes 1597448 | tf_op jit(solution)/shard_map/ppermute | solution.py:294
  8.1 1.0 %copy-start = (f32[1040,128]{1,0:T(8,128)S(1)}, f32[1040,128]{1,0:T(8,128)}, u32[]{:S(2)}) copy-start(f32[1040,128]{1,0:T(8,128)} %pack.1.own_ref) | copy-start | bytes 1597444
  17.3 10.6 %collective-permute-start.9 = (f32[520,128]{1,0:T(8,128)S(1)}, f32[520,128]{1,0:T(8,128)S(1)}, u32[]{:S(2)}, u32[]{:S(2)}) collective-permute-start(f32[520,128]{1,0:T(8,128)S(1)} %get-tuple-element.15), channel_id=1, source_target_pairs={{0,28},{1,21},{2,14},{3,7},{4,0},{5,9},{6,18},{7,27},{8,20},{9,29}... | collective-permute-start | bytes 798728 | tf_op jit(solution)/shard_map/ppermute | solution.py:294
  18.2 10.4 %collective-permute-start.8 = (f32[520,128]{1,0:T(8,128)S(1)}, f32[520,128]{1,0:T(8,128)S(1)}, u32[]{:S(2)}, u32[]{:S(2)}) collective-permute-start(f32[520,128]{1,0:T(8,128)S(1)} %get-tuple-element.15), channel_id=1, source_target_pairs={{0,0},{1,9},{2,18},{3,27},{4,28},{5,21},{6,14},{7,7},{8,8},{9,1},{... | collective-permute-start | bytes 798728 | tf_op jit(solution)/shard_map/ppermute | solution.py:294
  21.2 16.8 %collective-permute-start.6 = (f32[520,128]{1,0:T(8,128)S(1)}, f32[520,128]{1,0:T(8,128)S(1)}, u32[]{:S(2)}, u32[]{:S(2)}) collective-permute-start(f32[520,128]{1,0:T(8,128)S(1)} %get-tuple-element.16), channel_id=1, source_target_pairs={{0,28},{1,21},{2,14},{3,7},{4,0},{5,9},{6,18},{7,27},{8,20},{9,29}... | collective-permute-start | bytes 798728 | tf_op jit(solution)/shard_map/ppermute | solution.py:294
  21.3 16.7 %collective-permute-start.5 = (f32[520,128]{1,0:T(8,128)S(1)}, f32[520,128]{1,0:T(8,128)S(1)}, u32[]{:S(2)}, u32[]{:S(2)}) collective-permute-start(f32[520,128]{1,0:T(8,128)S(1)} %get-tuple-element.16), channel_id=1, source_target_pairs={{0,0},{1,9},{2,18},{3,27},{4,28},{5,21},{6,14},{7,7},{8,8},{9,1},{... | collective-permute-start | bytes 798728 | tf_op jit(solution)/shard_map/ppermute | solution.py:294
  24.4 2.0 %collective-permute-start.2 = (f32[1040,128]{1,0:T(8,128)S(1)}, f32[1040,128]{1,0:T(8,128)S(1)}, u32[]{:S(2)}, u32[]{:S(2)}) collective-permute-start(f32[1040,128]{1,0:T(8,128)S(1)} %collective-permute-done.own_ref), channel_id=1, source_target_pairs={{0,4},{1,5},{2,6},{3,7},{4,0},{5,1},{6,2},{7,3},{8,12},{9,13},{10,... | collective-permute-start | bytes 1597448 | tf_op jit(solution)/shard_map/ppermute | solution.py:309
  30.8 12.2 %collective-permute-start.10 = (f32[256,256]{1,0:T(8,128)S(1)}, f32[256,256]{1,0:T(8,128)S(1)}, u32[]{:S(2)}, u32[]{:S(2)}) collective-permute-start(f32[256,256]{1,0:T(8,128)S(1)} %get-tuple-element.12), channel_id=1, source_target_pairs={{0,0},{1,1},{2,2},{3,3},{4,7},{5,6},{6,5},{7,4},{8,9},{9,8},{10,11... | collective-permute-start | bytes 786440 | tf_op jit(solution)/shard_map/ppermute | solution.py:317
  35.0 13.7 %collective-permute-start.12 = (f32[256,256]{1,0:T(8,128)S(1)}, f32[256,256]{1,0:T(8,128)S(1)}, u32[]{:S(2)}, u32[]{:S(2)}) collective-permute-start(f32[256,256]{1,0:T(8,128)S(1)} %get-tuple-element.14), channel_id=1, source_target_pairs={{0,4},{1,5},{2,6},{3,7},{4,3},{5,2},{6,1},{7,0},{8,13},{9,12},{10,... | collective-permute-start | bytes 786440 | tf_op jit(solution)/shard_map/ppermute | solution.py:318
  40.0 11.5 %collective-permute-start.7 = (f32[256,256]{1,0:T(8,128)S(1)}, f32[256,256]{1,0:T(8,128)S(1)}, u32[]{:S(2)}, u32[]{:S(2)}) collective-permute-start(f32[256,256]{1,0:T(8,128)S(1)} %get-tuple-element.11), channel_id=1, source_target_pairs={{0,0},{1,1},{2,2},{3,3},{4,7},{5,6},{6,5},{7,4},{8,9},{9,8},{10,11... | collective-permute-start | bytes 786440 | tf_op jit(solution)/shard_map/ppermute | solution.py:317
  43.0 17.6 %collective-permute-start.11 = (f32[256,256]{1,0:T(8,128)S(1)}, f32[256,256]{1,0:T(8,128)S(1)}, u32[]{:S(2)}, u32[]{:S(2)}) collective-permute-start(f32[256,256]{1,0:T(8,128)S(1)} %get-tuple-element.13), channel_id=1, source_target_pairs={{0,4},{1,5},{2,6},{3,7},{4,3},{5,2},{6,1},{7,0},{8,13},{9,12},{10,... | collective-permute-start | bytes 786440 | tf_op jit(solution)/shard_map/ppermute | solution.py:318

commit v3 on v2

--- a/solution.py
+++ b/solution.py
@@ -13,8 +13,6 @@
 PANEL = RB * TB
 META = 8
 FEW = 5
-CUTS = 2
-CUT = TB // CUTS
 AXES = ("rows", "cols")
 VMEM_LIMIT = 16 * 1024 * 1024
 PACK_LIMIT = 60 * 1024 * 1024
@@ -27,7 +25,7 @@
 
 
 def cost(flops, nbytes):
-    return pl.CostEstimate(flops=flops * 20, bytes_accessed=nbytes * 20, transcendentals=0)
+    return pl.CostEstimate(flops=flops, bytes_accessed=nbytes, transcendentals=0)
 
 
 def pack_kernel(slots, rows_hbm, cols_hbm, counts_hbm, tiles_hbm, scale_hbm, *refs):
@@ -61,21 +59,15 @@
         codes = jnp.where(lane == slot, code, codes)
     copies[4].wait()
     for slot in range(slots):
-        for cut in range(CUTS):
-            start = cut * (slots * CUT + META) + slot * CUT
-            part = tiles_ref[0, slot, cut * CUT : (cut + 1) * CUT, :]
-            whole_ref[start : start + CUT, :] = part * factors[slot]
-    for cut in range(CUTS):
-        start = cut * (slots * CUT + META) + slots * CUT
-        whole_ref[start : start + META, :] = codes
+        whole_ref[slot * TB : (slot + 1) * TB, :] = tiles_ref[0, slot] * factors[slot]
+    whole_ref[slots * TB :, :] = codes
 
 
 def pack(tiles, tile_rows, tile_cols, counts, scaling):
     slots = tiles.shape[1]
-    piece = slots * CUT + META
     return pl.pallas_call(
         functools.partial(pack_kernel, slots),
-        out_shape=jax.ShapeDtypeStruct((CUTS * piece, TB), jnp.float32),
+        out_shape=jax.ShapeDtypeStruct((slots * TB + META, TB), jnp.float32),
         in_specs=[HSPEC] * 5,
         out_specs=VSPEC,
         scratch_shapes=[
@@ -93,7 +85,7 @@
 
 
 def read_codes(piece_ref, slots):
-    row = piece_ref[slots * CUT : slots * CUT + META, :].astype(jnp.int32)
+    row = piece_ref[slots * TB : slots * TB + META, :].astype(jnp.int32)
     return [row[0, slot] for slot in range(slots)]
 
 
@@ -115,11 +107,8 @@
                     sum_ref[col] = jnp.zeros_like(sum_ref[col])
 
                 start = pl.multiple_of(side * PANEL + (code & 1) * TB, TB)
-                for cut in range(CUTS):
-                    piece_ref = own_ref if side == 0 else other_ref
-                    base = cut * (slots * CUT + META) + slot * CUT
-                    place = pl.ds(start + cut * CUT, CUT)
-                    sum_ref[col, place, :] += piece_ref[base : base + CUT, :]
+                piece_ref = own_ref if side == 0 else other_ref
+                sum_ref[col, pl.ds(start, TB), :] += piece_ref[slot * TB : (slot + 1) * TB, :]
 
     def convert(col, carry):
         @pl.when(used_ref[col] == 1)
@@ -148,7 +137,7 @@
             pltpu.SMEM((CB_DEV,), jnp.int32),
         ],
         compiler_params=params(),
-        cost_estimate=cost(1 << 20, 1 << 21),
+        cost_estimate=cost(1 << 25, 1 << 25),
         name="spread",
     )(own, other)
 
@@ -171,106 +160,69 @@
     return nt_dot(left, right)
 
 
-def for_tiles(slots, piece_refs, body):
+def multiply_kernel(slots, *refs):
+    dense_refs, piece_refs = refs[:2], refs[2:4]
+    kept_ref, other_ref, sum_ref = refs[4:]
+    sum_ref[...] = jnp.zeros_like(sum_ref)
     codes = [read_codes(piece_ref, slots) for piece_ref in piece_refs]
-    core = lax.axis_index("rows") & 1
-
-    def some(which, slot_range):
+
+    def some(group, slot_range):
         for slot in slot_range:
-            code = jnp.maximum(codes[which][slot], 0)
-            body(which, slot, code >> 1, core if which == 0 else 1 - core, code & 1)
+            code = jnp.maximum(codes[group][slot], 0)
+            tile = piece_refs[group][slot * TB : (slot + 1) * TB, :]
+            both = product(dense_refs[group][code >> 1], tile)
+            sum_ref[code & 1] += both[:, :TB] + both[:, TB:]
 
     few = min(FEW, slots)
-    for which in range(2):
-        some(which, range(few))
+    for group in range(2):
+        some(group, range(few))
     if few < slots:
-        for which in range(2):
-
-            @pl.when(codes[which][few] >= 0)
-            def _(which=which):
-                some(which, range(few, slots))
-
-
-def first_kernel(slots, dense_ref, a_ref, b_ref, acc_ref):
-    acc_ref[...] = jnp.zeros_like(acc_ref)
-
-    def body(which, slot, col, panel, block):
-        piece_ref = a_ref if which == 0 else b_ref
-        starts = [cut * (slots * CUT + META) + slot * CUT for cut in range(CUTS)]
-        tile = jnp.concatenate([piece_ref[start : start + CUT, :] for start in starts], axis=0)
-        both = product(dense_ref[col], tile)
-        acc_ref[panel, block] += both[:, :TB] + both[:, TB:]
-
-    for_tiles(slots, (a_ref, b_ref), body)
-
-
-def first(dense, right_a, right_b, slots):
+        for group in range(2):
+
+            @pl.when(codes[group][few] >= 0)
+            def _(group=group):
+                some(group, range(few, slots))
+
+    for block in range(RB):
+        lanes = slice(block * TB, (block + 1) * TB)
+        kept_ref[:, lanes] = sum_ref[block, :PANEL, :]
+        other_ref[:, lanes] = sum_ref[block, PANEL:, :]
+
+
+def multiply(denses, pieces, slots):
     return pl.pallas_call(
-        functools.partial(first_kernel, slots),
-        out_shape=jax.ShapeDtypeStruct((2, RB, 2 * PANEL, TB), jnp.float32),
-        in_specs=[VSPEC] * 3,
-        out_specs=VSPEC,
-        compiler_params=params(),
-        cost_estimate=cost(slots * 4 * 4 * PANEL * TB * TB, 1 << 22),
-        name="first",
-    )(dense, right_a, right_b)
-
-
-def second_kernel(slots, cut, dense_ref, acc_ref, a_ref, b_ref, own_ref, other_ref, sum_ref):
-    sum_ref[...] = jnp.zeros_like(sum_ref)
-
-    def body(which, slot, col, panel, block):
-        piece_ref = a_ref if which == 0 else b_ref
-        sum_ref[panel, block] += product(dense_ref[col], piece_ref[slot * CUT : (slot + 1) * CUT, :])
-
-    for_tiles(slots, (a_ref, b_ref), body)
-    for side, out_ref in enumerate((own_ref, other_ref)):
-        rows = slice(side * PANEL, (side + 1) * PANEL)
-        parts = []
-        for panel in range(2):
-            for block in range(RB):
-                both = sum_ref[panel, block, rows, :]
-                before = acc_ref[panel, block, rows, cut * CUT : (cut + 1) * CUT]
-                parts.append(both[:, :CUT] + both[:, CUT:] + before)
-        out_ref[...] = jnp.concatenate(parts, axis=1)
-
-
-def second(cut, dense, acc, piece_a, piece_b, slots):
-    shape = jax.ShapeDtypeStruct((PANEL, 2 * RB * CUT), jnp.float32)
-    return pl.pallas_call(
-        functools.partial(second_kernel, slots, cut),
-        out_shape=[shape] * 2,
+        functools.partial(multiply_kernel, slots),
+        out_shape=[jax.ShapeDtypeStruct((PANEL, PANEL), jnp.float32)] * 2,
         in_specs=[VSPEC] * 4,
         out_specs=[VSPEC] * 2,
-        scratch_shapes=[pltpu.VMEM((2, RB, 2 * PANEL, 2 * CUT), jnp.float32)],
+        scratch_shapes=[pltpu.VMEM((RB, 2 * PANEL, TB), jnp.float32)],
         compiler_params=params(),
-        cost_estimate=cost(slots * 2 * 4 * PANEL * TB * TB, 1 << 21),
-        name="second",
-    )(dense, acc, piece_a, piece_b)
-
-
-def join_kernel(*refs):
-    out_ref = refs[-1]
-    for place in range(2 * RB):
-        lanes = slice(place * CUT, (place + 1) * CUT)
-        parts = [refs[cut][:, lanes] + refs[CUTS + cut][:, lanes] for cut in range(CUTS)]
-        out_ref[:, place * TB : (place + 1) * TB] = parts[0] if CUTS == 1 else jnp.concatenate(parts, axis=1)
-
-
-def join(from_same, from_cross):
+        cost_estimate=cost(1 << 25, 1 << 25),
+        name="multiply",
+    )(*denses, *pieces)
+
+
+def join_kernel(same_own_ref, same_far_ref, cross_own_ref, cross_far_ref, out_ref):
+    core = lax.axis_index("rows") & 1
+    start = pl.multiple_of(core * PANEL, PANEL)
+    out_ref[:, pl.ds(start, PANEL)] = same_own_ref[...] + cross_far_ref[...]
+    out_ref[:, pl.ds(PANEL - start, PANEL)] = same_far_ref[...] + cross_own_ref[...]
+
+
+def join(*results):
     return pl.pallas_call(
         join_kernel,
         out_shape=jax.ShapeDtypeStruct((PANEL, 2 * PANEL), jnp.float32),
-        in_specs=[VSPEC] * (2 * CUTS),
+        in_specs=[VSPEC] * 4,
         out_specs=VSPEC,
         compiler_params=params(),
         cost_estimate=cost(1 << 17, 1 << 17),
         name="join",
-    )(*from_same, *from_cross)
+    )(*results)
 
 
 def chunk(k, i, p):
-    return k ^ p ^ (3 * i)
+    return k ^ p ^ (3 * (i ^ (p & 1) ^ (p >> 1)))
 
 
 def pairs(place):
@@ -301,22 +253,18 @@
 def per_device(tiles, tile_rows, tile_cols, counts, scaling):
     slots = tiles.shape[1]
     own = pack(tiles, tile_rows, tile_cols, counts, scaling)
-    piece = slots * CUT + META
-    near_own = lax.ppermute(own, AXES, NEXT)
-    own_a, own_b, own_other = send([own] * 3, (SEND_SAME, SEND_CROSS, SWAP))
+    near = lax.ppermute(own, AXES, NEXT)
+    own_same, own_cross, own_other = send([own] * 3, (SEND_SAME, SEND_CROSS, SWAP))
     own_dense = spread(own, own_other, slots)
-    acc = first(own_dense, own_a, own_b, slots)
-    near_other = lax.ppermute(after(near_own, own_dense), AXES, SWAP)
-    near_dense = spread(near_own, near_other, slots)
-    starts = (after(near_own, own_dense), after(near_own, own_dense))
-    from_same, from_cross = [], []
-    for cut in range(CUTS):
-        part = lax.slice_in_dim(starts[cut], cut * piece, (cut + 1) * piece)
-        part_a, part_b = send([part] * 2, (SEND_SAME, SEND_CROSS))
-        kept, other = second(cut, near_dense, acc, part_a, part_b, slots)
-        from_same.append(lax.ppermute(kept, AXES, DONE_SAME))
-        from_cross.append(lax.ppermute(other, AXES, DONE_CROSS))
-    return join(from_same, from_cross)
+    near_other = lax.ppermute(after(near, own_dense), AXES, SWAP)
+    near_dense = spread(near, near_other, slots)
+    near_same, near_cross = send((after(near, own_same), after(near, own_cross)), (SEND_SAME, SEND_CROSS))
+    same, cross = [], []
+    for pieces in ((own_same, near_same), (own_cross, near_cross)):
+        kept, other = multiply((own_dense, near_dense), pieces, slots)
+        same.append(lax.ppermute(kept, AXES, DONE_SAME))
+        cross.append(lax.ppermute(other, AXES, DONE_CROSS))
+    return join(*same, *cross)
 
 
 def densify(tile_set, row_ids, col_ids, live_mask, scale_set, block_count):

time: 61.7 us -> 59.5 us (0.964)
  the two profiles are of different devices: /device:TPU:5 before, /device:TPU:4 now
where the time goes in v3:
time: 59.5 us; the launch traced here: 59 us
  waiting for transfers between devices  30.8 us (52%)
  starting transfers between devices  18.3 us (31%)
  Pallas kernels  8.15 us (14%)
  local copies, waits for them, and re-layouts  1.04 us (2%)
  between operations  0.75 us (1%)
    ppermute x2, waiting for transfers between devices, per_device(): same.append(lax.ppermute(kept, AXES, DONE_SAME))  8.7 us
    ppermute x1, waiting for transfers between devices, per_device(): near = lax.ppermute(own, AXES, NEXT)  7.92 us
    ppermute x5, waiting for transfers between devices, send(): lax.ppermute(piece, AXES, perm)  7.67 us
    ppermute x2, starting transfers between devices, per_device(): same.append(lax.ppermute(kept, AXES, DONE_SAME))  6.79 us
    ppermute x2, waiting for transfers between devices, per_device(): cross.append(lax.ppermute(other, AXES, DONE_CROSS))  6.48 us
    ppermute x5, starting transfers between devices, send(): lax.ppermute(piece, AXES, perm)  5.55 us
    ppermute x2, starting transfers between devices, per_device(): cross.append(lax.ppermute(other, AXES, DONE_CROSS))  4.34 us
    pallas_call x2, Pallas kernels, multiply(): pl.pallas_call(functools.partial(multiply_kernel, slots), out_shape=[jax....  3.3 us
  transfers between devices with their start and end apart: 11, of which 5 were waited for; matrix products, arithmetic and copies ran while one was open for 0% of the time, Pallas kernels for 9%

profile of v3, /device:TPU:4, one launch (start us, length us, event | category | flops | bytes accessed | tf_op | source)
XLA Modules:
  0.0 59.0 jit_solution(16107846810988485134)
XLA Ops:
  0.7 1.9 %pack.1.own_ref = f32[1032,128]{1,0:T(8,128)} custom-call(s32[1,8]{1,0:T(1,128)} %rows_hbm.1, s32[1,8]{1,0:T(1,128)} %cols_hbm.1, s32[1,1]{1,0:T(1,128)S(6)} %copy.6.counts_hbm, f32[1,8,128,128]{3,2,1,0:T(8,128)} %tiles_hbm.1, f32[16,128]{1,0:T(8,128)} %bitcast.1), custom_call_target="tpu_custom_call" | custom-call | flops 131072 | bytes 1572864 | tf_op jit(solution)/shard_map/pack/pallas_call | solution.py:68
  2.6 0.1 collective-permute-start
  2.7 1.6 %collective-permute-start.1 = (f32[1032,128]{1,0:T(8,128)}, f32[1032,128]{1,0:T(8,128)S(1)}, u32[]{:S(2)}, u32[]{:S(2)}) collective-permute-start(f32[1032,128]{1,0:T(8,128)} %pack.1.own_ref), channel_id=1, source_target_pairs={{0,1},{1,0},{2,3},{3,2},{4,5},{5,4},{6,7},{7,6},{8,9},{9,8},{10,11... | collective-permute-start | bytes 1585160 | tf_op jit(solution)/shard_map/ppermute | solution.py:256
  4.3 1.2 %collective-permute-start.6 = (f32[1032,128]{1,0:T(8,128)}, f32[1032,128]{1,0:T(8,128)S(1)}, u32[]{:S(2)}, u32[]{:S(2)}) collective-permute-start(f32[1032,128]{1,0:T(8,128)} %pack.1.own_ref), channel_id=1, source_target_pairs={{0,28},{1,13},{2,22},{3,7},{4,0},{5,17},{6,10},{7,27},{8,20},{9,5}... | collective-permute-start | bytes 1585160 | tf_op jit(solution)/shard_map/ppermute | solution.py:246
  5.5 1.7 %collective-permute-start.3 = (f32[1032,128]{1,0:T(8,128)}, f32[1032,128]{1,0:T(8,128)S(1)}, u32[]{:S(2)}, u32[]{:S(2)}) collective-permute-start(f32[1032,128]{1,0:T(8,128)} %pack.1.own_ref), channel_id=1, source_target_pairs={{0,0},{1,17},{2,10},{3,27},{4,28},{5,13},{6,22},{7,7},{8,8},{9,25}... | collective-permute-start | bytes 1585160 | tf_op jit(solution)/shard_map/ppermute | solution.py:246
  7.2 0.0 collective-permute-done.other_ref
  7.2 0.0 copy-start
  7.2 1.0 %copy-done = f32[1032,128]{1,0:T(8,128)S(1)} copy-done((f32[1032,128]{1,0:T(8,128)S(1)}, f32[1032,128]{1,0:T(8,128)}, u32[]{:S(2)}) %copy-start) | copy-done | bytes 528408
  8.3 1.1 %spread.2.refs_0_ = bf16[16,512,256]{2,1,0:T(8,128)(2,1)S(1)} custom-call(f32[1032,128]{1,0:T(8,128)S(1)} %copy-done, f32[1032,128]{1,0:T(8,128)S(1)} %collective-permute-done.other_ref), custom_call_target="tpu_custom_call" | custom-call | flops 33554432 | bytes 33554432 | tf_op jit(solution)/shard_map/spread/pallas_call | solution.py:130
  9.4 7.9 %collective-permute-done.1.own_ref = f32[1032,128]{1,0:T(8,128)S(1)} collective-permute-done((f32[1032,128]{1,0:T(8,128)}, f32[1032,128]{1,0:T(8,128)S(1)}, u32[]{:S(2)}, u32[]{:S(2)}) %collective-permute-start.1) | collective-permute-done | bytes 528416 | tf_op jit(solution)/shard_map/ppermute | solution.py:256
  17.3 0.0 collective-permute-start.2
  17.3 0.0 collective-permute-done.6.refs_2_
  17.3 1.9 %collective-permute-start.7 = (f32[1032,128]{1,0:T(8,128)S(1)}, f32[1032,128]{1,0:T(8,128)S(1)}, u32[]{:S(2)}, u32[]{:S(2)}) collective-permute-start(f32[1032,128]{1,0:T(8,128)S(1)} %collective-permute-done.1.own_ref), channel_id=1, source_target_pairs={{0,28},{1,13},{2,22},{3,7},{4,0},{5,17},{6,10},{7,27},{8,20},{9,5}... | collective-permute-start | bytes 1585160 | tf_op jit(solution)/shard_map/ppermute | solution.py:246
  19.2 0.0 collective-permute-done.3.refs_2_
  19.2 0.7 %collective-permute-start.4 = (f32[1032,128]{1,0:T(8,128)S(1)}, f32[1032,128]{1,0:T(8,128)S(1)}, u32[]{:S(2)}, u32[]{:S(2)}) collective-permute-start(f32[1032,128]{1,0:T(8,128)S(1)} %collective-permute-done.1.own_ref), channel_id=1, source_target_pairs={{0,0},{1,17},{2,10},{3,27},{4,28},{5,13},{6,22},{7,7},{8,8},{9,25}... | collective-permute-start | bytes 1585160 | tf_op jit(solution)/shard_map/ppermute | solution.py:246
  19.9 0.0 collective-permute-done.2.other_ref
  19.9 0.9 %spread.3.refs_1_ = bf16[16,512,256]{2,1,0:T(8,128)(2,1)S(1)} custom-call(f32[1032,128]{1,0:T(8,128)S(1)} %collective-permute-done.1.own_ref, f32[1032,128]{1,0:T(8,128)S(1)} %collective-permute-done.2.other_ref), custom_call_target="tpu_custom_call" | custom-call | flops 33554432 | bytes 33554432 | tf_op jit(solution)/shard_map/spread/pallas_call | solution.py:130
  20.9 7.7 %collective-permute-done.7.refs_3_ = f32[1032,128]{1,0:T(8,128)S(1)} collective-permute-done((f32[1032,128]{1,0:T(8,128)S(1)}, f32[1032,128]{1,0:T(8,128)S(1)}, u32[]{:S(2)}, u32[]{:S(2)}) %collective-permute-start.7) | collective-permute-done | bytes 528416 | tf_op jit(solution)/shard_map/ppermute | solution.py:246
  28.5 1.6 %multiply.3 = (f32[256,256]{1,0:T(8,128)S(1)}, f32[256,256]{1,0:T(8,128)S(1)}) custom-call(bf16[16,512,256]{2,1,0:T(8,128)(2,1)S(1)} %spread.2.refs_0_, bf16[16,512,256]{2,1,0:T(8,128)(2,1)S(1)} %spread.3.refs_1_, f32[1032,128]{1,0:T(8,128)S(1)} %collective-permute-done.6.refs_2_, f32[1032,128]{1,0:T(8,128)S(1)} %collective-permute-done.7.refs_3_), custom_call_target="tpu_custom_call" | custom-call | flops 33554432 | bytes 33554432 | tf_op jit(solution)/shard_map/multiply/pallas_call | solution.py:193
  30.2 3.6 %collective-permute-start.10 = (f32[256,256]{1,0:T(8,128)S(1)}, f32[256,256]{1,0:T(8,128)S(1)}, u32[]{:S(2)}, u32[]{:S(2)}) collective-permute-start(f32[256,256]{1,0:T(8,128)S(1)} %get-tuple-element.18), channel_id=1, source_target_pairs={{0,4},{1,6},{2,5},{3,7},{4,3},{5,1},{6,2},{7,0},{8,13},{9,15},{10,... | collective-permute-start | bytes 786440 | tf_op jit(solution)/shard_map/ppermute | solution.py:266
  33.8 1.9 %collective-permute-start.8 = (f32[256,256]{1,0:T(8,128)S(1)}, f32[256,256]{1,0:T(8,128)S(1)}, u32[]{:S(2)}, u32[]{:S(2)}) collective-permute-start(f32[256,256]{1,0:T(8,128)S(1)} %get-tuple-element.16), channel_id=1, source_target_pairs={{0,0},{1,2},{2,1},{3,3},{4,7},{5,5},{6,6},{7,4},{8,9},{9,11},{10,8... | collective-permute-start | bytes 786440 | tf_op jit(solution)/shard_map/ppermute | solution.py:265
  35.7 0.0 collective-permute-done.4.refs_3_
  35.7 1.6 %multiply.2 = (f32[256,256]{1,0:T(8,128)S(1)}, f32[256,256]{1,0:T(8,128)S(1)}) custom-call(bf16[16,512,256]{2,1,0:T(8,128)(2,1)S(1)} %spread.2.refs_0_, bf16[16,512,256]{2,1,0:T(8,128)(2,1)S(1)} %spread.3.refs_1_, f32[1032,128]{1,0:T(8,128)S(1)} %collective-permute-done.3.refs_2_, f32[1032,128]{1,0:T(8,128)S(1)} %collective-permute-done.4.refs_3_), custom_call_target="tpu_custom_call" | custom-call | flops 33554432 | bytes 33554432 | tf_op jit(solution)/shard_map/multiply/pallas_call | solution.py:193
  37.4 4.9 %collective-permute-start.5 = (f32[256,256]{1,0:T(8,128)S(1)}, f32[256,256]{1,0:T(8,128)S(1)}, u32[]{:S(2)}, u32[]{:S(2)}) collective-permute-start(f32[256,256]{1,0:T(8,128)S(1)} %get-tuple-element.14), channel_id=1, source_target_pairs={{0,0},{1,2},{2,1},{3,3},{4,7},{5,5},{6,6},{7,4},{8,9},{9,11},{10,8... | collective-permute-start | bytes 786440 | tf_op jit(solution)/shard_map/ppermute | solution.py:265
  42.2 0.8 %collective-permute-start.9 = (f32[256,256]{1,0:T(8,128)S(1)}, f32[256,256]{1,0:T(8,128)S(1)}, u32[]{:S(2)}, u32[]{:S(2)}) collective-permute-start(f32[256,256]{1,0:T(8,128)S(1)} %get-tuple-element.17), channel_id=1, source_target_pairs={{0,4},{1,6},{2,5},{3,7},{4,3},{5,1},{6,2},{7,0},{8,13},{9,15},{10,... | collective-permute-start | bytes 786440 | tf_op jit(solution)/shard_map/ppermute | solution.py:266
  43.0 0.0 collective-permute-done.10.cross_far_ref
  43.0 3.1 %collective-permute-done.8.same_far_ref = f32[256,256]{1,0:T(8,128)S(1)} collective-permute-done((f32[256,256]{1,0:T(8,128)S(1)}, f32[256,256]{1,0:T(8,128)S(1)}, u32[]{:S(2)}, u32[]{:S(2)}) %collective-permute-start.8) | collective-permute-done | bytes 262176 | tf_op jit(solution)/shard_map/ppermute | solution.py:265
  46.1 5.6 %collective-permute-done.5.same_own_ref = f32[256,256]{1,0:T(8,128)S(1)} collective-permute-done((f32[256,256]{1,0:T(8,128)S(1)}, f32[256,256]{1,0:T(8,128)S(1)}, u32[]{:S(2)}, u32[]{:S(2)}) %collective-permute-start.5) | collective-permute-done | bytes 262176 | tf_op jit(solution)/shard_map/ppermute | solution.py:265
  51.7 6.5 %collective-permute-done.9.cross_own_ref = f32[256,256]{1,0:T(8,128)S(1)} collective-permute-done((f32[256,256]{1,0:T(8,128)S(1)}, f32[256,256]{1,0:T(8,128)S(1)}, u32[]{:S(2)}, u32[]{:S(2)}) %collective-permute-start.9) | collective-permute-done | bytes 262176 | tf_op jit(solution)/shard_map/ppermute | solution.py:266
  58.2 0.8 %join.1 = f32[256,512]{1,0:T(8,128)} custom-call(f32[256,256]{1,0:T(8,128)S(1)} %collective-permute-done.5.same_own_ref, f32[256,256]{1,0:T(8,128)S(1)} %collective-permute-done.8.same_far_ref, f32[256,256]{1,0:T(8,128)S(1)} %collective-permute-done.9.cross_own_ref, f32[256,256]{1,0:T(8,128)S(1)} %collective-permute-done.10.cross_far_ref), custom_call_target="tpu_custom_call" | custom-call | flops 131072 | bytes 131072 | tf_op jit(solution)/shard_map/join/pallas_call | solution.py:213
Async XLA Ops:
  2.6 4.6 %collective-permute-start = (f32[1032,128]{1,0:T(8,128)}, f32[1032,128]{1,0:T(8,128)S(1)}, u32[]{:S(2)}, u32[]{:S(2)}) collective-permute-start(f32[1032,128]{1,0:T(8,128)} %pack.1.own_ref), channel_id=1, source_target_pairs={{0,4},{1,5},{2,6},{3,7},{4,0},{5,1},{6,2},{7,3},{8,12},{9,13},{10,... | collective-permute-start | bytes 1585160 | tf_op jit(solution)/shard_map/ppermute | solution.py:246
  2.7 14.6 %collective-permute-start.1 = (f32[1032,128]{1,0:T(8,128)}, f32[1032,128]{1,0:T(8,128)S(1)}, u32[]{:S(2)}, u32[]{:S(2)}) collective-permute-start(f32[1032,128]{1,0:T(8,128)} %pack.1.own_ref), channel_id=1, source_target_pairs={{0,1},{1,0},{2,3},{3,2},{4,5},{5,4},{6,7},{7,6},{8,9},{9,8},{10,11... | collective-permute-start | bytes 1585160 | tf_op jit(solution)/shard_map/ppermute | solution.py:256
  4.3 13.0 %collective-permute-start.6 = (f32[1032,128]{1,0:T(8,128)}, f32[1032,128]{1,0:T(8,128)S(1)}, u32[]{:S(2)}, u32[]{:S(2)}) collective-permute-start(f32[1032,128]{1,0:T(8,128)} %pack.1.own_ref), channel_id=1, source_target_pairs={{0,28},{1,13},{2,22},{3,7},{4,0},{5,17},{6,10},{7,27},{8,20},{9,5}... | collective-permute-start | bytes 1585160 | tf_op jit(solution)/shard_map/ppermute | solution.py:246
  5.5 13.7 %collective-permute-start.3 = (f32[1032,128]{1,0:T(8,128)}, f32[1032,128]{1,0:T(8,128)S(1)}, u32[]{:S(2)}, u32[]{:S(2)}) collective-permute-start(f32[1032,128]{1,0:T(8,128)} %pack.1.own_ref), channel_id=1, source_target_pairs={{0,0},{1,17},{2,10},{3,27},{4,28},{5,13},{6,22},{7,7},{8,8},{9,25}... | collective-permute-start | bytes 1585160 | tf_op jit(solution)/shard_map/ppermute | solution.py:246
  7.2 1.0 %copy-start = (f32[1032,128]{1,0:T(8,128)S(1)}, f32[1032,128]{1,0:T(8,128)}, u32[]{:S(2)}) copy-start(f32[1032,128]{1,0:T(8,128)} %pack.1.own_ref) | copy-start | bytes 1585156
  17.3 2.6 %collective-permute-start.2 = (f32[1032,128]{1,0:T(8,128)S(1)}, f32[1032,128]{1,0:T(8,128)S(1)}, u32[]{:S(2)}, u32[]{:S(2)}) collective-permute-start(f32[1032,128]{1,0:T(8,128)S(1)} %collective-permute-done.1.own_ref), channel_id=1, source_target_pairs={{0,4},{1,5},{2,6},{3,7},{4,0},{5,1},{6,2},{7,3},{8,12},{9,13},{10,... | collective-permute-start | bytes 1585160 | tf_op jit(solution)/shard_map/ppermute | solution.py:259
  17.3 11.2 %collective-permute-start.7 = (f32[1032,128]{1,0:T(8,128)S(1)}, f32[1032,128]{1,0:T(8,128)S(1)}, u32[]{:S(2)}, u32[]{:S(2)}) collective-permute-start(f32[1032,128]{1,0:T(8,128)S(1)} %collective-permute-done.1.own_ref), channel_id=1, source_target_pairs={{0,28},{1,13},{2,22},{3,7},{4,0},{5,17},{6,10},{7,27},{8,20},{9,5}... | collective-permute-start | bytes 1585160 | tf_op jit(solution)/shard_map/ppermute | solution.py:246
  19.2 16.5 %collective-permute-start.4 = (f32[1032,128]{1,0:T(8,128)S(1)}, f32[1032,128]{1,0:T(8,128)S(1)}, u32[]{:S(2)}, u32[]{:S(2)}) collective-permute-start(f32[1032,128]{1,0:T(8,128)S(1)} %collective-permute-done.1.own_ref), channel_id=1, source_target_pairs={{0,0},{1,17},{2,10},{3,27},{4,28},{5,13},{6,22},{7,7},{8,8},{9,25}... | collective-permute-start | bytes 1585160 | tf_op jit(solution)/shard_map/ppermute | solution.py:246
  30.2 12.8 %collective-permute-start.10 = (f32[256,256]{1,0:T(8,128)S(1)}, f32[256,256]{1,0:T(8,128)S(1)}, u32[]{:S(2)}, u32[]{:S(2)}) collective-permute-start(f32[256,256]{1,0:T(8,128)S(1)} %get-tuple-element.18), channel_id=1, source_target_pairs={{0,4},{1,6},{2,5},{3,7},{4,3},{5,1},{6,2},{7,0},{8,13},{9,15},{10,... | collective-permute-start | bytes 786440 | tf_op jit(solution)/shard_map/ppermute | solution.py:266
  33.8 12.3 %collective-permute-start.8 = (f32[256,256]{1,0:T(8,128)S(1)}, f32[256,256]{1,0:T(8,128)S(1)}, u32[]{:S(2)}, u32[]{:S(2)}) collective-permute-start(f32[256,256]{1,0:T(8,128)S(1)} %get-tuple-element.16), channel_id=1, source_target_pairs={{0,0},{1,2},{2,1},{3,3},{4,7},{5,5},{6,6},{7,4},{8,9},{9,11},{10,8... | collective-permute-start | bytes 786440 | tf_op jit(solution)/shard_map/ppermute | solution.py:265
  37.4 14.3 %collective-permute-start.5 = (f32[256,256]{1,0:T(8,128)S(1)}, f32[256,256]{1,0:T(8,128)S(1)}, u32[]{:S(2)}, u32[]{:S(2)}) collective-permute-start(f32[256,256]{1,0:T(8,128)S(1)} %get-tuple-element.14), channel_id=1, source_target_pairs={{0,0},{1,2},{2,1},{3,3},{4,7},{5,5},{6,6},{7,4},{8,9},{9,11},{10,8... | collective-permute-start | bytes 786440 | tf_op jit(solution)/shard_map/ppermute | solution.py:265
  42.2 15.9 %collective-permute-start.9 = (f32[256,256]{1,0:T(8,128)S(1)}, f32[256,256]{1,0:T(8,128)S(1)}, u32[]{:S(2)}, u32[]{:S(2)}) collective-permute-start(f32[256,256]{1,0:T(8,128)S(1)} %get-tuple-element.17), channel_id=1, source_target_pairs={{0,4},{1,6},{2,5},{3,7},{4,3},{5,1},{6,2},{7,0},{8,13},{9,15},{10,... | collective-permute-start | bytes 786440 | tf_op jit(solution)/shard_map/ppermute | solution.py:266

commit v4 on v3

--- a/solution.py
+++ b/solution.py
@@ -160,49 +160,78 @@
     return nt_dot(left, right)
 
 
-def multiply_kernel(slots, *refs):
-    dense_refs, piece_refs = refs[:2], refs[2:4]
-    kept_ref, other_ref, sum_ref = refs[4:]
-    sum_ref[...] = jnp.zeros_like(sum_ref)
+def for_tiles(slots, piece_refs, body):
     codes = [read_codes(piece_ref, slots) for piece_ref in piece_refs]
 
-    def some(group, slot_range):
+    def some(which, slot_range):
         for slot in slot_range:
-            code = jnp.maximum(codes[group][slot], 0)
-            tile = piece_refs[group][slot * TB : (slot + 1) * TB, :]
-            both = product(dense_refs[group][code >> 1], tile)
-            sum_ref[code & 1] += both[:, :TB] + both[:, TB:]
+            code = jnp.maximum(codes[which][slot], 0)
+            body(which, slot, code >> 1, code & 1)
 
     few = min(FEW, slots)
-    for group in range(2):
-        some(group, range(few))
+    for which in range(len(piece_refs)):
+        some(which, range(few))
     if few < slots:
-        for group in range(2):
-
-            @pl.when(codes[group][few] >= 0)
-            def _(group=group):
-                some(group, range(few, slots))
-
+        for which in range(len(piece_refs)):
+
+            @pl.when(codes[which][few] >= 0)
+            def _(which=which):
+                some(which, range(few, slots))
+
+
+def first_kernel(slots, dense_ref, *refs):
+    count = len(refs) // 2
+    piece_refs, acc_refs = refs[:count], refs[count:]
+    for acc_ref in acc_refs:
+        acc_ref[...] = jnp.zeros_like(acc_ref)
+
+    def body(which, slot, col, block):
+        both = product(dense_ref[col], piece_refs[which][slot * TB : (slot + 1) * TB, :])
+        acc_refs[which][block] += both[:, :TB] + both[:, TB:]
+
+    for_tiles(slots, piece_refs, body)
+
+
+def first(dense, pieces, slots):
+    return pl.pallas_call(
+        functools.partial(first_kernel, slots),
+        out_shape=[jax.ShapeDtypeStruct((RB, 2 * PANEL, TB), jnp.float32)] * len(pieces),
+        in_specs=[VSPEC] * (1 + len(pieces)),
+        out_specs=[VSPEC] * len(pieces),
+        compiler_params=params(),
+        cost_estimate=cost(1 << 25, 1 << 25),
+        name="first",
+    )(dense, *pieces)
+
+
+def second_kernel(slots, dense_ref, acc_ref, piece_ref, kept_ref, other_ref, sum_ref):
+    sum_ref[...] = acc_ref[...]
+
+    def body(which, slot, col, block):
+        both = product(dense_ref[col], piece_ref[slot * TB : (slot + 1) * TB, :])
+        sum_ref[block] += both[:, :TB] + both[:, TB:]
+
+    for_tiles(slots, (piece_ref,), body)
     for block in range(RB):
         lanes = slice(block * TB, (block + 1) * TB)
         kept_ref[:, lanes] = sum_ref[block, :PANEL, :]
         other_ref[:, lanes] = sum_ref[block, PANEL:, :]
 
 
-def multiply(denses, pieces, slots):
-    return pl.pallas_call(
-        functools.partial(multiply_kernel, slots),
+def second(dense, acc, piece, slots):
+    return pl.pallas_call(
+        functools.partial(second_kernel, slots),
         out_shape=[jax.ShapeDtypeStruct((PANEL, PANEL), jnp.float32)] * 2,
-        in_specs=[VSPEC] * 4,
+        in_specs=[VSPEC] * 3,
         out_specs=[VSPEC] * 2,
         scratch_shapes=[pltpu.VMEM((RB, 2 * PANEL, TB), jnp.float32)],
         compiler_params=params(),
         cost_estimate=cost(1 << 25, 1 << 25),
-        name="multiply",
-    )(*denses, *pieces)
-
-
-def join_kernel(same_own_ref, same_far_ref, cross_own_ref, cross_far_ref, out_ref):
+        name="second",
+    )(dense, acc, piece)
+
+
+def join_kernel(cross_own_ref, cross_far_ref, same_own_ref, same_far_ref, out_ref):
     core = lax.axis_index("rows") & 1
     start = pl.multiple_of(core * PANEL, PANEL)
     out_ref[:, pl.ds(start, PANEL)] = same_own_ref[...] + cross_far_ref[...]
@@ -259,12 +288,13 @@
     near_other = lax.ppermute(after(near, own_dense), AXES, SWAP)
     near_dense = spread(near, near_other, slots)
     near_same, near_cross = send((after(near, own_same), after(near, own_cross)), (SEND_SAME, SEND_CROSS))
+    accs = first(own_dense, (own_same, own_cross), slots)
     same, cross = [], []
-    for pieces in ((own_same, near_same), (own_cross, near_cross)):
-        kept, other = multiply((own_dense, near_dense), pieces, slots)
+    for acc, piece in zip(accs, (near_same, near_cross)):
+        kept, other = second(near_dense, acc, piece, slots)
         same.append(lax.ppermute(kept, AXES, DONE_SAME))
         cross.append(lax.ppermute(other, AXES, DONE_CROSS))
-    return join(*same, *cross)
+    return join(cross[0], cross[1], same[0], same[1])
 
 
 def densify(tile_set, row_ids, col_ids, live_mask, scale_set, block_count):

time: 59.5 us -> 58.4 us (0.982)
  the two profiles are of different devices: /device:TPU:4 before, /device:TPU:5 now
where the time goes in v4:
time: 58.4 us; the launch traced here: 58.2 us
  waiting for transfers between devices  29.7 us (51%)
  starting transfers between devices  18.4 us (32%)
  Pallas kernels  8.31 us (14%)
  local copies, waits for them, and re-layouts  1.04 us (2%)
  between operations  0.77 us (1%)
    ppermute x2, waiting for transfers between devices, per_device(): cross.append(lax.ppermute(other, AXES, DONE_CROSS))  10.2 us
    ppermute x5, starting transfers between devices, send(): lax.ppermute(piece, AXES, perm)  7.19 us
    ppermute x1, waiting for transfers between devices, per_device(): near = lax.ppermute(own, AXES, NEXT)  6.95 us
    ppermute x5, waiting for transfers between devices, send(): lax.ppermute(piece, AXES, perm)  6.71 us
    ppermute x2, starting transfers between devices, per_device(): same.append(lax.ppermute(kept, AXES, DONE_SAME))  6.27 us
    ppermute x2, waiting for transfers between devices, per_device(): same.append(lax.ppermute(kept, AXES, DONE_SAME))  5.86 us
    ppermute x2, starting transfers between devices, per_device(): cross.append(lax.ppermute(other, AXES, DONE_CROSS))  2.76 us
    pallas_call x2, Pallas kernels, spread(): pl.pallas_call(functools.partial(spread_kernel, slots), out_shape=jax.Sha...  2.23 us
  transfers between devices with their start and end apart: 11, of which 8 were waited for; matrix products, arithmetic and copies ran while one was open for 0% of the time, Pallas kernels for 9%

profile of v4, /device:TPU:5, one launch (start us, length us, event | category | flops | bytes accessed | tf_op | source)
XLA Modules:
  0.0 58.2 jit_solution(9480930191800981287)
XLA Ops:
  0.7 1.9 %pack.1.own_ref = f32[1032,128]{1,0:T(8,128)} custom-call(s32[1,8]{1,0:T(1,128)} %rows_hbm.1, s32[1,8]{1,0:T(1,128)} %cols_hbm.1, s32[1,1]{1,0:T(1,128)S(6)} %copy.6.counts_hbm, f32[1,8,128,128]{3,2,1,0:T(8,128)} %tiles_hbm.1, f32[16,128]{1,0:T(8,128)} %bitcast.1), custom_call_target="tpu_custom_call" | custom-call | flops 131072 | bytes 1572864 | tf_op jit(solution)/shard_map/pack/pallas_call | solution.py:68
  2.6 0.7 %collective-permute-start.1 = (f32[1032,128]{1,0:T(8,128)}, f32[1032,128]{1,0:T(8,128)S(1)}, u32[]{:S(2)}, u32[]{:S(2)}) collective-permute-start(f32[1032,128]{1,0:T(8,128)} %pack.1.own_ref), channel_id=1, source_target_pairs={{0,4},{1,5},{2,6},{3,7},{4,0},{5,1},{6,2},{7,3},{8,12},{9,13},{10,... | collective-permute-start | bytes 1585160 | tf_op jit(solution)/shard_map/ppermute | solution.py:275
  3.3 1.3 %collective-permute-start = (f32[1032,128]{1,0:T(8,128)}, f32[1032,128]{1,0:T(8,128)S(1)}, u32[]{:S(2)}, u32[]{:S(2)}) collective-permute-start(f32[1032,128]{1,0:T(8,128)} %pack.1.own_ref), channel_id=1, source_target_pairs={{0,1},{1,0},{2,3},{3,2},{4,5},{5,4},{6,7},{7,6},{8,9},{9,8},{10,11... | collective-permute-start | bytes 1585160 | tf_op jit(solution)/shard_map/ppermute | solution.py:285
  4.6 0.3 collective-permute-start.4
  5.0 3.0 %collective-permute-start.3 = (f32[1032,128]{1,0:T(8,128)}, f32[1032,128]{1,0:T(8,128)S(1)}, u32[]{:S(2)}, u32[]{:S(2)}) collective-permute-start(f32[1032,128]{1,0:T(8,128)} %pack.1.own_ref), channel_id=1, source_target_pairs={{0,0},{1,17},{2,10},{3,27},{4,28},{5,13},{6,22},{7,7},{8,8},{9,25}... | collective-permute-start | bytes 1585160 | tf_op jit(solution)/shard_map/ppermute | solution.py:275
  8.0 0.0 collective-permute-done.1.other_ref
  8.1 0.0 copy-start
  8.1 1.0 %copy-done = f32[1032,128]{1,0:T(8,128)S(1)} copy-done((f32[1032,128]{1,0:T(8,128)S(1)}, f32[1032,128]{1,0:T(8,128)}, u32[]{:S(2)}) %copy-start) | copy-done | bytes 528408
  9.1 1.1 %spread.2.dense_ref = bf16[16,512,256]{2,1,0:T(8,128)(2,1)S(1)} custom-call(f32[1032,128]{1,0:T(8,128)S(1)} %copy-done, f32[1032,128]{1,0:T(8,128)S(1)} %collective-permute-done.1.other_ref), custom_call_target="tpu_custom_call" | custom-call | flops 33554432 | bytes 33554432 | tf_op jit(solution)/shard_map/spread/pallas_call | solution.py:130
  10.2 7.0 %collective-permute-done.own_ref = f32[1032,128]{1,0:T(8,128)S(1)} collective-permute-done((f32[1032,128]{1,0:T(8,128)}, f32[1032,128]{1,0:T(8,128)S(1)}, u32[]{:S(2)}, u32[]{:S(2)}) %collective-permute-start) | collective-permute-done | bytes 528416 | tf_op jit(solution)/shard_map/ppermute | solution.py:285
  17.1 0.9 %collective-permute-start.2 = (f32[1032,128]{1,0:T(8,128)S(1)}, f32[1032,128]{1,0:T(8,128)S(1)}, u32[]{:S(2)}, u32[]{:S(2)}) collective-permute-start(f32[1032,128]{1,0:T(8,128)S(1)} %collective-permute-done.own_ref), channel_id=1, source_target_pairs={{0,4},{1,5},{2,6},{3,7},{4,0},{5,1},{6,2},{7,3},{8,12},{9,13},{10,... | collective-permute-start | bytes 1585160 | tf_op jit(solution)/shard_map/ppermute | solution.py:288
  18.0 0.4 collective-permute-done.4.refs_1_
  18.3 0.0 collective-permute-start.7
  18.4 1.7 %collective-permute-done.3.refs_0_ = f32[1032,128]{1,0:T(8,128)S(1)} collective-permute-done((f32[1032,128]{1,0:T(8,128)}, f32[1032,128]{1,0:T(8,128)S(1)}, u32[]{:S(2)}, u32[]{:S(2)}) %collective-permute-start.3) | collective-permute-done | bytes 528416 | tf_op jit(solution)/shard_map/ppermute | solution.py:275
  20.1 3.1 %collective-permute-start.5 = (f32[1032,128]{1,0:T(8,128)S(1)}, f32[1032,128]{1,0:T(8,128)S(1)}, u32[]{:S(2)}, u32[]{:S(2)}) collective-permute-start(f32[1032,128]{1,0:T(8,128)S(1)} %collective-permute-done.own_ref), channel_id=1, source_target_pairs={{0,0},{1,17},{2,10},{3,27},{4,28},{5,13},{6,22},{7,7},{8,8},{9,25}... | collective-permute-start | bytes 1585160 | tf_op jit(solution)/shard_map/ppermute | solution.py:275
  23.1 1.5 %first.1 = (f32[2,512,128]{2,1,0:T(8,128)S(1)}, f32[2,512,128]{2,1,0:T(8,128)S(1)}) custom-call(bf16[16,512,256]{2,1,0:T(8,128)(2,1)S(1)} %spread.2.dense_ref, f32[1032,128]{1,0:T(8,128)S(1)} %collective-permute-done.3.refs_0_, f32[1032,128]{1,0:T(8,128)S(1)} %collective-permute-done.4.refs_1_), custom_call_target="tpu_custom_call" | custom-call | flops 33554432 | bytes 33554432 | tf_op jit(solution)/shard_map/first/pallas_call | solution.py:196
  24.7 0.0 collective-permute-done.2.other_ref
  24.7 1.2 %spread.3.dense_ref = bf16[16,512,256]{2,1,0:T(8,128)(2,1)S(1)} custom-call(f32[1032,128]{1,0:T(8,128)S(1)} %collective-permute-done.own_ref, f32[1032,128]{1,0:T(8,128)S(1)} %collective-permute-done.2.other_ref), custom_call_target="tpu_custom_call" | custom-call | flops 33554432 | bytes 33554432 | tf_op jit(solution)/shard_map/spread/pallas_call | solution.py:130
  25.8 4.6 %collective-permute-done.7.piece_ref = f32[1032,128]{1,0:T(8,128)S(1)} collective-permute-done((f32[1032,128]{1,0:T(8,128)S(1)}, f32[1032,128]{1,0:T(8,128)S(1)}, u32[]{:S(2)}, u32[]{:S(2)}) %collective-permute-start.7) | collective-permute-done | bytes 528416 | tf_op jit(solution)/shard_map/ppermute | solution.py:275
  30.5 0.9 %second.3 = (f32[256,256]{1,0:T(8,128)S(1)}, f32[256,256]{1,0:T(8,128)S(1)}) custom-call(bf16[16,512,256]{2,1,0:T(8,128)(2,1)S(1)} %spread.3.dense_ref, f32[2,512,128]{2,1,0:T(8,128)S(1)} %get-tuple-element.18.acc_ref, f32[1032,128]{1,0:T(8,128)S(1)} %collective-permute-done.7.piece_ref), custom_call_target="tpu_custom_call" | custom-call | flops 33554432 | bytes 33554432 | tf_op jit(solution)/shard_map/second/pallas_call | solution.py:222
  31.3 1.3 %collective-permute-start.8 = (f32[256,256]{1,0:T(8,128)S(1)}, f32[256,256]{1,0:T(8,128)S(1)}, u32[]{:S(2)}, u32[]{:S(2)}) collective-permute-start(f32[256,256]{1,0:T(8,128)S(1)} %get-tuple-element.20), channel_id=1, source_target_pairs={{0,4},{1,6},{2,5},{3,7},{4,3},{5,1},{6,2},{7,0},{8,13},{9,15},{10,... | collective-permute-start | bytes 786440 | tf_op jit(solution)/shard_map/ppermute | solution.py:296
  32.6 3.1 %collective-permute-start.10 = (f32[256,256]{1,0:T(8,128)S(1)}, f32[256,256]{1,0:T(8,128)S(1)}, u32[]{:S(2)}, u32[]{:S(2)}) collective-permute-start(f32[256,256]{1,0:T(8,128)S(1)} %get-tuple-element.22), channel_id=1, source_target_pairs={{0,0},{1,2},{2,1},{3,3},{4,7},{5,5},{6,6},{7,4},{8,9},{9,11},{10,8... | collective-permute-start | bytes 786440 | tf_op jit(solution)/shard_map/ppermute | solution.py:295
  35.8 0.0 collective-permute-done.5.piece_ref
  35.8 0.9 %second.2 = (f32[256,256]{1,0:T(8,128)S(1)}, f32[256,256]{1,0:T(8,128)S(1)}) custom-call(bf16[16,512,256]{2,1,0:T(8,128)(2,1)S(1)} %spread.3.dense_ref, f32[2,512,128]{2,1,0:T(8,128)S(1)} %get-tuple-element.15.acc_ref, f32[1032,128]{1,0:T(8,128)S(1)} %collective-permute-done.5.piece_ref), custom_call_target="tpu_custom_call" | custom-call | flops 33554432 | bytes 33554432 | tf_op jit(solution)/shard_map/second/pallas_call | solution.py:222
  36.7 1.5 %collective-permute-start.6 = (f32[256,256]{1,0:T(8,128)S(1)}, f32[256,256]{1,0:T(8,128)S(1)}, u32[]{:S(2)}, u32[]{:S(2)}) collective-permute-start(f32[256,256]{1,0:T(8,128)S(1)} %get-tuple-element.17), channel_id=1, source_target_pairs={{0,4},{1,6},{2,5},{3,7},{4,3},{5,1},{6,2},{7,0},{8,13},{9,15},{10,... | collective-permute-start | bytes 786440 | tf_op jit(solution)/shard_map/ppermute | solution.py:296
  38.2 3.1 %collective-permute-start.9 = (f32[256,256]{1,0:T(8,128)S(1)}, f32[256,256]{1,0:T(8,128)S(1)}, u32[]{:S(2)}, u32[]{:S(2)}) collective-permute-start(f32[256,256]{1,0:T(8,128)S(1)} %get-tuple-element.21), channel_id=1, source_target_pairs={{0,0},{1,2},{2,1},{3,3},{4,7},{5,5},{6,6},{7,4},{8,9},{9,11},{10,8... | collective-permute-start | bytes 786440 | tf_op jit(solution)/shard_map/ppermute | solution.py:295
  41.3 0.5 collective-permute-done.8.cross_far_ref
  41.8 1.6 %collective-permute-done.10.same_far_ref = f32[256,256]{1,0:T(8,128)S(1)} collective-permute-done((f32[256,256]{1,0:T(8,128)S(1)}, f32[256,256]{1,0:T(8,128)S(1)}, u32[]{:S(2)}, u32[]{:S(2)}) %collective-permute-start.10) | collective-permute-done | bytes 262176 | tf_op jit(solution)/shard_map/ppermute | solution.py:295
  43.5 9.6 %collective-permute-done.6.cross_own_ref = f32[256,256]{1,0:T(8,128)S(1)} collective-permute-done((f32[256,256]{1,0:T(8,128)S(1)}, f32[256,256]{1,0:T(8,128)S(1)}, u32[]{:S(2)}, u32[]{:S(2)}) %collective-permute-start.6) | collective-permute-done | bytes 262176 | tf_op jit(solution)/shard_map/ppermute | solution.py:296
  53.1 4.2 %collective-permute-done.9.same_own_ref = f32[256,256]{1,0:T(8,128)S(1)} collective-permute-done((f32[256,256]{1,0:T(8,128)S(1)}, f32[256,256]{1,0:T(8,128)S(1)}, u32[]{:S(2)}, u32[]{:S(2)}) %collective-permute-start.9) | collective-permute-done | bytes 262176 | tf_op jit(solution)/shard_map/ppermute | solution.py:295
  57.3 0.9 %join.1 = f32[256,512]{1,0:T(8,128)} custom-call(f32[256,256]{1,0:T(8,128)S(1)} %collective-permute-done.6.cross_own_ref, f32[256,256]{1,0:T(8,128)S(1)} %collective-permute-done.8.cross_far_ref, f32[256,256]{1,0:T(8,128)S(1)} %collective-permute-done.9.same_own_ref, f32[256,256]{1,0:T(8,128)S(1)} %collective-permute-done.10.same_far_ref), custom_call_target="tpu_custom_call" | custom-call | flops 131072 | bytes 131072 | tf_op jit(solution)/shard_map/join/pallas_call | solution.py:242
Async XLA Ops:
  2.6 5.5 %collective-permute-start.1 = (f32[1032,128]{1,0:T(8,128)}, f32[1032,128]{1,0:T(8,128)S(1)}, u32[]{:S(2)}, u32[]{:S(2)}) collective-permute-start(f32[1032,128]{1,0:T(8,128)} %pack.1.own_ref), channel_id=1, source_target_pairs={{0,4},{1,5},{2,6},{3,7},{4,0},{5,1},{6,2},{7,3},{8,12},{9,13},{10,... | collective-permute-start | bytes 1585160 | tf_op jit(solution)/shard_map/ppermute | solution.py:275
  3.3 13.8 %collective-permute-start = (f32[1032,128]{1,0:T(8,128)}, f32[1032,128]{1,0:T(8,128)S(1)}, u32[]{:S(2)}, u32[]{:S(2)}) collective-permute-start(f32[1032,128]{1,0:T(8,128)} %pack.1.own_ref), channel_id=1, source_target_pairs={{0,1},{1,0},{2,3},{3,2},{4,5},{5,4},{6,7},{7,6},{8,9},{9,8},{10,11... | collective-permute-start | bytes 1585160 | tf_op jit(solution)/shard_map/ppermute | solution.py:285
  4.6 13.7 %collective-permute-start.4 = (f32[1032,128]{1,0:T(8,128)}, f32[1032,128]{1,0:T(8,128)S(1)}, u32[]{:S(2)}, u32[]{:S(2)}) collective-permute-start(f32[1032,128]{1,0:T(8,128)} %pack.1.own_ref), channel_id=1, source_target_pairs={{0,28},{1,13},{2,22},{3,7},{4,0},{5,17},{6,10},{7,27},{8,20},{9,5}... | collective-permute-start | bytes 1585160 | tf_op jit(solution)/shard_map/ppermute | solution.py:275
  5.0 15.1 %collective-permute-start.3 = (f32[1032,128]{1,0:T(8,128)}, f32[1032,128]{1,0:T(8,128)S(1)}, u32[]{:S(2)}, u32[]{:S(2)}) collective-permute-start(f32[1032,128]{1,0:T(8,128)} %pack.1.own_ref), channel_id=1, source_target_pairs={{0,0},{1,17},{2,10},{3,27},{4,28},{5,13},{6,22},{7,7},{8,8},{9,25}... | collective-permute-start | bytes 1585160 | tf_op jit(solution)/shard_map/ppermute | solution.py:275
  8.1 1.0 %copy-start = (f32[1032,128]{1,0:T(8,128)S(1)}, f32[1032,128]{1,0:T(8,128)}, u32[]{:S(2)}) copy-start(f32[1032,128]{1,0:T(8,128)} %pack.1.own_ref) | copy-start | bytes 1585156
  17.1 7.5 %collective-permute-start.2 = (f32[1032,128]{1,0:T(8,128)S(1)}, f32[1032,128]{1,0:T(8,128)S(1)}, u32[]{:S(2)}, u32[]{:S(2)}) collective-permute-start(f32[1032,128]{1,0:T(8,128)S(1)} %collective-permute-done.own_ref), channel_id=1, source_target_pairs={{0,4},{1,5},{2,6},{3,7},{4,0},{5,1},{6,2},{7,3},{8,12},{9,13},{10,... | collective-permute-start | bytes 1585160 | tf_op jit(solution)/shard_map/ppermute | solution.py:288
  18.3 12.1 %collective-permute-start.7 = (f32[1032,128]{1,0:T(8,128)S(1)}, f32[1032,128]{1,0:T(8,128)S(1)}, u32[]{:S(2)}, u32[]{:S(2)}) collective-permute-start(f32[1032,128]{1,0:T(8,128)S(1)} %collective-permute-done.own_ref), channel_id=1, source_target_pairs={{0,28},{1,13},{2,22},{3,7},{4,0},{5,17},{6,10},{7,27},{8,20},{9,5}... | collective-permute-start | bytes 1585160 | tf_op jit(solution)/shard_map/ppermute | solution.py:275
  20.1 15.7 %collective-permute-start.5 = (f32[1032,128]{1,0:T(8,128)S(1)}, f32[1032,128]{1,0:T(8,128)S(1)}, u32[]{:S(2)}, u32[]{:S(2)}) collective-permute-start(f32[1032,128]{1,0:T(8,128)S(1)} %collective-permute-done.own_ref), channel_id=1, source_target_pairs={{0,0},{1,17},{2,10},{3,27},{4,28},{5,13},{6,22},{7,7},{8,8},{9,25}... | collective-permute-start | bytes 1585160 | tf_op jit(solution)/shard_map/ppermute | solution.py:275
  31.3 10.5 %collective-permute-start.8 = (f32[256,256]{1,0:T(8,128)S(1)}, f32[256,256]{1,0:T(8,128)S(1)}, u32[]{:S(2)}, u32[]{:S(2)}) collective-permute-start(f32[256,256]{1,0:T(8,128)S(1)} %get-tuple-element.20), channel_id=1, source_target_pairs={{0,4},{1,6},{2,5},{3,7},{4,3},{5,1},{6,2},{7,0},{8,13},{9,15},{10,... | collective-permute-start | bytes 786440 | tf_op jit(solution)/shard_map/ppermute | solution.py:296
  32.6 10.8 %collective-permute-start.10 = (f32[256,256]{1,0:T(8,128)S(1)}, f32[256,256]{1,0:T(8,128)S(1)}, u32[]{:S(2)}, u32[]{:S(2)}) collective-permute-start(f32[256,256]{1,0:T(8,128)S(1)} %get-tuple-element.22), channel_id=1, source_target_pairs={{0,0},{1,2},{2,1},{3,3},{4,7},{5,5},{6,6},{7,4},{8,9},{9,11},{10,8... | collective-permute-start | bytes 786440 | tf_op jit(solution)/shard_map/ppermute | solution.py:295
  36.7 16.4 %collective-permute-start.6 = (f32[256,256]{1,0:T(8,128)S(1)}, f32[256,256]{1,0:T(8,128)S(1)}, u32[]{:S(2)}, u32[]{:S(2)}) collective-permute-start(f32[256,256]{1,0:T(8,128)S(1)} %get-tuple-element.17), channel_id=1, source_target_pairs={{0,4},{1,6},{2,5},{3,7},{4,3},{5,1},{6,2},{7,0},{8,13},{9,15},{10,... | collective-permute-start | bytes 786440 | tf_op jit(solution)/shard_map/ppermute | solution.py:296
  38.2 19.2 %collective-permute-start.9 = (f32[256,256]{1,0:T(8,128)S(1)}, f32[256,256]{1,0:T(8,128)S(1)}, u32[]{:S(2)}, u32[]{:S(2)}) collective-permute-start(f32[256,256]{1,0:T(8,128)S(1)} %get-tuple-element.21), channel_id=1, source_target_pairs={{0,0},{1,2},{2,1},{3,3},{4,7},{5,5},{6,6},{7,4},{8,9},{9,11},{10,8... | collective-permute-start | bytes 786440 | tf_op jit(solution)/shard_map/ppermute | solution.py:295

commit v5 on v4

--- a/solution.py
+++ b/solution.py
@@ -13,6 +13,7 @@
 PANEL = RB * TB
 META = 8
 FEW = 5
+STEPS = 4
 AXES = ("rows", "cols")
 VMEM_LIMIT = 16 * 1024 * 1024
 PACK_LIMIT = 60 * 1024 * 1024
@@ -28,39 +29,46 @@
     return pl.CostEstimate(flops=flops, bytes_accessed=nbytes, transcendentals=0)
 
 
-def pack_kernel(slots, rows_hbm, cols_hbm, counts_hbm, tiles_hbm, scale_hbm, *refs):
-    whole_ref, rows_ref, cols_ref, counts_ref, tiles_ref, scale_ref, sems = refs
-    copies = [
-        pltpu.make_async_copy(source, target, sems.at[index])
+def pack_kernel(slots, rows_hbm, cols_hbm, counts_hbm, tiles_hbm, scale_hbm, whole_hbm, *scratch):
+    rows_ref, cols_ref, counts_ref, scale_ref, tiles_ref, whole_ref, small_sems, in_sems, out_sems = scratch
+    small = [
+        pltpu.make_async_copy(source, target, small_sems.at[index])
         for index, (source, target) in enumerate(
-            (
-                (rows_hbm, rows_ref),
-                (cols_hbm, cols_ref),
-                (counts_hbm, counts_ref),
-                (scale_hbm, scale_ref),
-                (tiles_hbm, tiles_ref),
-            )
+            ((rows_hbm, rows_ref), (cols_hbm, cols_ref), (counts_hbm, counts_ref), (scale_hbm, scale_ref))
         )
     ]
-    for copy in copies:
+    arrive = [
+        pltpu.make_async_copy(tiles_hbm.at[0, slot], tiles_ref.at[slot], in_sems.at[slot])
+        for slot in range(slots)
+    ]
+    for copy in small + arrive:
         copy.start()
-    for copy in copies[:4]:
+    for copy in small:
         copy.wait()
+    leave = []
+
+    def send_rows(start, size):
+        rows = pl.ds(start, size)
+        copy = pltpu.make_async_copy(whole_ref.at[rows], whole_hbm.at[rows], out_sems.at[len(leave)])
+        copy.start()
+        leave.append(copy)
+
     lane = lax.broadcasted_iota(jnp.int32, (META, TB), 1)
     codes = jnp.full((META, TB), -1.0, jnp.float32)
     count = counts_ref[0, 0]
-    factors = []
     for slot in range(slots):
         live = slot < count
-        row = rows_ref[0, slot]
         col = cols_ref[0, slot]
-        factors.append(jnp.where(live, jnp.sqrt(scale_ref[pl.ds(col, 1), :]), 0.0))
-        code = jnp.where(live, col * RB + row, -1).astype(jnp.float32)
+        code = jnp.where(live, col * RB + rows_ref[0, slot], -1).astype(jnp.float32)
         codes = jnp.where(lane == slot, code, codes)
-    copies[4].wait()
-    for slot in range(slots):
-        whole_ref[slot * TB : (slot + 1) * TB, :] = tiles_ref[0, slot] * factors[slot]
+        factor = jnp.where(live, jnp.sqrt(scale_ref[pl.ds(col, 1), :]), 0.0)
+        arrive[slot].wait()
+        whole_ref[slot * TB : (slot + 1) * TB, :] = tiles_ref[slot] * factor
+        send_rows(slot * TB, TB)
     whole_ref[slots * TB :, :] = codes
+    send_rows(slots * TB, META)
+    for copy in leave:
+        copy.wait()
 
 
 def pack(tiles, tile_rows, tile_cols, counts, scaling):
@@ -69,14 +77,17 @@
         functools.partial(pack_kernel, slots),
         out_shape=jax.ShapeDtypeStruct((slots * TB + META, TB), jnp.float32),
         in_specs=[HSPEC] * 5,
-        out_specs=VSPEC,
+        out_specs=HSPEC,
         scratch_shapes=[
             pltpu.SMEM(tile_rows.shape, jnp.int32),
             pltpu.SMEM(tile_cols.shape, jnp.int32),
             pltpu.SMEM(counts.shape, jnp.int32),
-            pltpu.VMEM(tiles.shape, jnp.float32),
             pltpu.VMEM((CB_DEV, TB), jnp.float32),
-            pltpu.SemaphoreType.DMA((5,)),
+            pltpu.VMEM((slots, TB, TB), jnp.float32),
+            pltpu.VMEM((slots * TB + META, TB), jnp.float32),
+            pltpu.SemaphoreType.DMA((4,)),
+            pltpu.SemaphoreType.DMA((slots,)),
+            pltpu.SemaphoreType.DMA((slots + 1,)),
         ],
         compiler_params=params(PACK_LIMIT),
         cost_estimate=cost(slots * TB * TB, 3 * slots * TB * TB * 4),
@@ -231,19 +242,29 @@
     )(dense, acc, piece)
 
 
-def join_kernel(cross_own_ref, cross_far_ref, same_own_ref, same_far_ref, out_ref):
+def join_kernel(cross_own_ref, cross_far_ref, same_own_ref, same_far_ref, out_hbm, out_ref, sems):
     core = lax.axis_index("rows") & 1
     start = pl.multiple_of(core * PANEL, PANEL)
-    out_ref[:, pl.ds(start, PANEL)] = same_own_ref[...] + cross_far_ref[...]
-    out_ref[:, pl.ds(PANEL - start, PANEL)] = same_far_ref[...] + cross_own_ref[...]
+    size = PANEL // STEPS
+    copies = []
+    for step in range(STEPS):
+        rows = pl.ds(step * size, size)
+        out_ref[rows, pl.ds(start, PANEL)] = same_own_ref[rows, :] + cross_far_ref[rows, :]
+        out_ref[rows, pl.ds(PANEL - start, PANEL)] = same_far_ref[rows, :] + cross_own_ref[rows, :]
+        copies.append(pltpu.make_async_copy(out_ref.at[rows], out_hbm.at[rows], sems.at[step]))
+        copies[-1].start()
+    for copy in copies:
+        copy.wait()
 
 
 def join(*results):
+    shape = (PANEL, 2 * PANEL)
     return pl.pallas_call(
         join_kernel,
-        out_shape=jax.ShapeDtypeStruct((PANEL, 2 * PANEL), jnp.float32),
+        out_shape=jax.ShapeDtypeStruct(shape, jnp.float32),
         in_specs=[VSPEC] * 4,
-        out_specs=VSPEC,
+        out_specs=HSPEC,
+        scratch_shapes=[pltpu.VMEM(shape, jnp.float32), pltpu.SemaphoreType.DMA((STEPS,))],
         compiler_params=params(),
         cost_estimate=cost(1 << 17, 1 << 17),
         name="join",

time: 58.4 us -> 58.4 us (level)
  no operation moved by 1% of the time
where the time goes in v5:
time: 58.4 us; the launch traced here: 58.1 us
  waiting for transfers between devices  29.8 us (51%)
  starting transfers between devices  18.3 us (31%)
  Pallas kernels  8.23 us (14%)
  local copies, waits for them, and re-layouts  1.04 us (2%)
  between operations  0.77 us (1%)
    ppermute x2, waiting for transfers between devices, per_device(): cross.append(lax.ppermute(other, AXES, DONE_CROSS))  10.4 us
    ppermute x5, starting transfers between devices, send(): lax.ppermute(piece, AXES, perm)  7.19 us
    ppermute x1, waiting for transfers between devices, per_device(): near = lax.ppermute(own, AXES, NEXT)  6.92 us
    ppermute x5, waiting for transfers between devices, send(): lax.ppermute(piece, AXES, perm)  6.81 us
    ppermute x2, starting transfers between devices, per_device(): same.append(lax.ppermute(kept, AXES, DONE_SAME))  6.15 us
    ppermute x2, waiting for transfers between devices, per_device(): same.append(lax.ppermute(kept, AXES, DONE_SAME))  5.67 us
    ppermute x2, starting transfers between devices, per_device(): cross.append(lax.ppermute(other, AXES, DONE_CROSS))  2.79 us
    pallas_call x2, Pallas kernels, spread(): pl.pallas_call(functools.partial(spread_kernel, slots), out_shape=jax.Sha...  2.16 us
  transfers between devices with their start and end apart: 11, of which 8 were waited for; matrix products, arithmetic and copies ran while one was open for 0% of the time, Pallas kernels for 9%

profile of v5, /device:TPU:5, one launch (start us, length us, event | category | flops | bytes accessed | tf_op | source)
XLA Modules:
  0.0 58.1 jit_solution(2741579352332761990)
XLA Ops:
  0.7 1.9 %pack.1.own_ref = f32[1032,128]{1,0:T(8,128)} custom-call(s32[1,8]{1,0:T(1,128)} %rows_hbm.1, s32[1,8]{1,0:T(1,128)} %cols_hbm.1, s32[1,1]{1,0:T(1,128)S(6)} %copy.6.counts_hbm, f32[1,8,128,128]{3,2,1,0:T(8,128)} %tiles_hbm.1, f32[16,128]{1,0:T(8,128)} %bitcast.1), custom_call_target="tpu_custom_call" | custom-call | flops 131072 | bytes 1572864 | tf_op jit(solution)/shard_map/pack/pallas_call | solution.py:76
  2.6 0.7 %collective-permute-start.1 = (f32[1032,128]{1,0:T(8,128)}, f32[1032,128]{1,0:T(8,128)S(1)}, u32[]{:S(2)}, u32[]{:S(2)}) collective-permute-start(f32[1032,128]{1,0:T(8,128)} %pack.1.own_ref), channel_id=1, source_target_pairs={{0,4},{1,5},{2,6},{3,7},{4,0},{5,1},{6,2},{7,3},{8,12},{9,13},{10,... | collective-permute-start | bytes 1585160 | tf_op jit(solution)/shard_map/ppermute | solution.py:296
  3.3 1.3 %collective-permute-start = (f32[1032,128]{1,0:T(8,128)}, f32[1032,128]{1,0:T(8,128)S(1)}, u32[]{:S(2)}, u32[]{:S(2)}) collective-permute-start(f32[1032,128]{1,0:T(8,128)} %pack.1.own_ref), channel_id=1, source_target_pairs={{0,1},{1,0},{2,3},{3,2},{4,5},{5,4},{6,7},{7,6},{8,9},{9,8},{10,11... | collective-permute-start | bytes 1585160 | tf_op jit(solution)/shard_map/ppermute | solution.py:306
  4.6 0.3 collective-permute-start.4
  5.0 3.0 %collective-permute-start.3 = (f32[1032,128]{1,0:T(8,128)}, f32[1032,128]{1,0:T(8,128)S(1)}, u32[]{:S(2)}, u32[]{:S(2)}) collective-permute-start(f32[1032,128]{1,0:T(8,128)} %pack.1.own_ref), channel_id=1, source_target_pairs={{0,0},{1,17},{2,10},{3,27},{4,28},{5,13},{6,22},{7,7},{8,8},{9,25}... | collective-permute-start | bytes 1585160 | tf_op jit(solution)/shard_map/ppermute | solution.py:296
  8.0 0.0 collective-permute-done.1.other_ref
  8.1 0.0 copy-start
  8.1 1.0 %copy-done = f32[1032,128]{1,0:T(8,128)S(1)} copy-done((f32[1032,128]{1,0:T(8,128)S(1)}, f32[1032,128]{1,0:T(8,128)}, u32[]{:S(2)}) %copy-start) | copy-done | bytes 528408
  9.1 1.1 %spread.2.dense_ref = bf16[16,512,256]{2,1,0:T(8,128)(2,1)S(1)} custom-call(f32[1032,128]{1,0:T(8,128)S(1)} %copy-done, f32[1032,128]{1,0:T(8,128)S(1)} %collective-permute-done.1.other_ref), custom_call_target="tpu_custom_call" | custom-call | flops 33554432 | bytes 33554432 | tf_op jit(solution)/shard_map/spread/pallas_call | solution.py:141
  10.2 6.9 %collective-permute-done.own_ref = f32[1032,128]{1,0:T(8,128)S(1)} collective-permute-done((f32[1032,128]{1,0:T(8,128)}, f32[1032,128]{1,0:T(8,128)S(1)}, u32[]{:S(2)}, u32[]{:S(2)}) %collective-permute-start) | collective-permute-done | bytes 528416 | tf_op jit(solution)/shard_map/ppermute | solution.py:306
  17.1 0.9 %collective-permute-start.2 = (f32[1032,128]{1,0:T(8,128)S(1)}, f32[1032,128]{1,0:T(8,128)S(1)}, u32[]{:S(2)}, u32[]{:S(2)}) collective-permute-start(f32[1032,128]{1,0:T(8,128)S(1)} %collective-permute-done.own_ref), channel_id=1, source_target_pairs={{0,4},{1,5},{2,6},{3,7},{4,0},{5,1},{6,2},{7,3},{8,12},{9,13},{10,... | collective-permute-start | bytes 1585160 | tf_op jit(solution)/shard_map/ppermute | solution.py:309
  18.0 0.4 collective-permute-done.4.refs_1_
  18.3 0.0 collective-permute-start.7
  18.4 1.7 %collective-permute-done.3.refs_0_ = f32[1032,128]{1,0:T(8,128)S(1)} collective-permute-done((f32[1032,128]{1,0:T(8,128)}, f32[1032,128]{1,0:T(8,128)S(1)}, u32[]{:S(2)}, u32[]{:S(2)}) %collective-permute-start.3) | collective-permute-done | bytes 528416 | tf_op jit(solution)/shard_map/ppermute | solution.py:296
  20.1 3.0 %collective-permute-start.5 = (f32[1032,128]{1,0:T(8,128)S(1)}, f32[1032,128]{1,0:T(8,128)S(1)}, u32[]{:S(2)}, u32[]{:S(2)}) collective-permute-start(f32[1032,128]{1,0:T(8,128)S(1)} %collective-permute-done.own_ref), channel_id=1, source_target_pairs={{0,0},{1,17},{2,10},{3,27},{4,28},{5,13},{6,22},{7,7},{8,8},{9,25}... | collective-permute-start | bytes 1585160 | tf_op jit(solution)/shard_map/ppermute | solution.py:296
  23.1 1.5 %first.1 = (f32[2,512,128]{2,1,0:T(8,128)S(1)}, f32[2,512,128]{2,1,0:T(8,128)S(1)}) custom-call(bf16[16,512,256]{2,1,0:T(8,128)(2,1)S(1)} %spread.2.dense_ref, f32[1032,128]{1,0:T(8,128)S(1)} %collective-permute-done.3.refs_0_, f32[1032,128]{1,0:T(8,128)S(1)} %collective-permute-done.4.refs_1_), custom_call_target="tpu_custom_call" | custom-call | flops 33554432 | bytes 33554432 | tf_op jit(solution)/shard_map/first/pallas_call | solution.py:207
  24.7 0.0 collective-permute-done.2.other_ref
  24.7 1.1 %spread.3.dense_ref = bf16[16,512,256]{2,1,0:T(8,128)(2,1)S(1)} custom-call(f32[1032,128]{1,0:T(8,128)S(1)} %collective-permute-done.own_ref, f32[1032,128]{1,0:T(8,128)S(1)} %collective-permute-done.2.other_ref), custom_call_target="tpu_custom_call" | custom-call | flops 33554432 | bytes 33554432 | tf_op jit(solution)/shard_map/spread/pallas_call | solution.py:141
  25.7 4.7 %collective-permute-done.7.piece_ref = f32[1032,128]{1,0:T(8,128)S(1)} collective-permute-done((f32[1032,128]{1,0:T(8,128)S(1)}, f32[1032,128]{1,0:T(8,128)S(1)}, u32[]{:S(2)}, u32[]{:S(2)}) %collective-permute-start.7) | collective-permute-done | bytes 528416 | tf_op jit(solution)/shard_map/ppermute | solution.py:296
  30.5 0.9 %second.3 = (f32[256,256]{1,0:T(8,128)S(1)}, f32[256,256]{1,0:T(8,128)S(1)}) custom-call(bf16[16,512,256]{2,1,0:T(8,128)(2,1)S(1)} %spread.3.dense_ref, f32[2,512,128]{2,1,0:T(8,128)S(1)} %get-tuple-element.18.acc_ref, f32[1032,128]{1,0:T(8,128)S(1)} %collective-permute-done.7.piece_ref), custom_call_target="tpu_custom_call" | custom-call | flops 33554432 | bytes 33554432 | tf_op jit(solution)/shard_map/second/pallas_call | solution.py:233
  31.3 1.3 %collective-permute-start.8 = (f32[256,256]{1,0:T(8,128)S(1)}, f32[256,256]{1,0:T(8,128)S(1)}, u32[]{:S(2)}, u32[]{:S(2)}) collective-permute-start(f32[256,256]{1,0:T(8,128)S(1)} %get-tuple-element.20), channel_id=1, source_target_pairs={{0,4},{1,6},{2,5},{3,7},{4,3},{5,1},{6,2},{7,0},{8,13},{9,15},{10,... | collective-permute-start | bytes 786440 | tf_op jit(solution)/shard_map/ppermute | solution.py:317
  32.6 3.1 %collective-permute-start.10 = (f32[256,256]{1,0:T(8,128)S(1)}, f32[256,256]{1,0:T(8,128)S(1)}, u32[]{:S(2)}, u32[]{:S(2)}) collective-permute-start(f32[256,256]{1,0:T(8,128)S(1)} %get-tuple-element.22), channel_id=1, source_target_pairs={{0,0},{1,2},{2,1},{3,3},{4,7},{5,5},{6,6},{7,4},{8,9},{9,11},{10,8... | collective-permute-start | bytes 786440 | tf_op jit(solution)/shard_map/ppermute | solution.py:316
  35.7 0.0 collective-permute-done.5.piece_ref
  35.7 0.9 %second.2 = (f32[256,256]{1,0:T(8,128)S(1)}, f32[256,256]{1,0:T(8,128)S(1)}) custom-call(bf16[16,512,256]{2,1,0:T(8,128)(2,1)S(1)} %spread.3.dense_ref, f32[2,512,128]{2,1,0:T(8,128)S(1)} %get-tuple-element.15.acc_ref, f32[1032,128]{1,0:T(8,128)S(1)} %collective-permute-done.5.piece_ref), custom_call_target="tpu_custom_call" | custom-call | flops 33554432 | bytes 33554432 | tf_op jit(solution)/shard_map/second/pallas_call | solution.py:233
  36.6 1.5 %collective-permute-start.6 = (f32[256,256]{1,0:T(8,128)S(1)}, f32[256,256]{1,0:T(8,128)S(1)}, u32[]{:S(2)}, u32[]{:S(2)}) collective-permute-start(f32[256,256]{1,0:T(8,128)S(1)} %get-tuple-element.17), channel_id=1, source_target_pairs={{0,4},{1,6},{2,5},{3,7},{4,3},{5,1},{6,2},{7,0},{8,13},{9,15},{10,... | collective-permute-start | bytes 786440 | tf_op jit(solution)/shard_map/ppermute | solution.py:317
  38.2 3.1 %collective-permute-start.9 = (f32[256,256]{1,0:T(8,128)S(1)}, f32[256,256]{1,0:T(8,128)S(1)}, u32[]{:S(2)}, u32[]{:S(2)}) collective-permute-start(f32[256,256]{1,0:T(8,128)S(1)} %get-tuple-element.21), channel_id=1, source_target_pairs={{0,0},{1,2},{2,1},{3,3},{4,7},{5,5},{6,6},{7,4},{8,9},{9,11},{10,8... | collective-permute-start | bytes 786440 | tf_op jit(solution)/shard_map/ppermute | solution.py:316
  41.2 0.7 %collective-permute-done.8.cross_far_ref = f32[256,256]{1,0:T(8,128)S(1)} collective-permute-done((f32[256,256]{1,0:T(8,128)S(1)}, f32[256,256]{1,0:T(8,128)S(1)}, u32[]{:S(2)}, u32[]{:S(2)}) %collective-permute-start.8) | collective-permute-done | bytes 262176 | tf_op jit(solution)/shard_map/ppermute | solution.py:317
  41.9 1.5 %collective-permute-done.10.same_far_ref = f32[256,256]{1,0:T(8,128)S(1)} collective-permute-done((f32[256,256]{1,0:T(8,128)S(1)}, f32[256,256]{1,0:T(8,128)S(1)}, u32[]{:S(2)}, u32[]{:S(2)}) %collective-permute-start.10) | collective-permute-done | bytes 262176 | tf_op jit(solution)/shard_map/ppermute | solution.py:316
  43.4 9.7 %collective-permute-done.6.cross_own_ref = f32[256,256]{1,0:T(8,128)S(1)} collective-permute-done((f32[256,256]{1,0:T(8,128)S(1)}, f32[256,256]{1,0:T(8,128)S(1)}, u32[]{:S(2)}, u32[]{:S(2)}) %collective-permute-start.6) | collective-permute-done | bytes 262176 | tf_op jit(solution)/shard_map/ppermute | solution.py:317
  53.1 4.1 %collective-permute-done.9.same_own_ref = f32[256,256]{1,0:T(8,128)S(1)} collective-permute-done((f32[256,256]{1,0:T(8,128)S(1)}, f32[256,256]{1,0:T(8,128)S(1)}, u32[]{:S(2)}, u32[]{:S(2)}) %collective-permute-start.9) | collective-permute-done | bytes 262176 | tf_op jit(solution)/shard_map/ppermute | solution.py:316
  57.3 0.8 %join.1 = f32[256,512]{1,0:T(8,128)} custom-call(f32[256,256]{1,0:T(8,128)S(1)} %collective-permute-done.6.cross_own_ref, f32[256,256]{1,0:T(8,128)S(1)} %collective-permute-done.8.cross_far_ref, f32[256,256]{1,0:T(8,128)S(1)} %collective-permute-done.9.same_own_ref, f32[256,256]{1,0:T(8,128)S(1)} %collective-permute-done.10.same_far_ref), custom_call_target="tpu_custom_call" | custom-call | flops 131072 | bytes 131072 | tf_op jit(solution)/shard_map/join/pallas_call | solution.py:262
Async XLA Ops:
  2.6 5.5 %collective-permute-start.1 = (f32[1032,128]{1,0:T(8,128)}, f32[1032,128]{1,0:T(8,128)S(1)}, u32[]{:S(2)}, u32[]{:S(2)}) collective-permute-start(f32[1032,128]{1,0:T(8,128)} %pack.1.own_ref), channel_id=1, source_target_pairs={{0,4},{1,5},{2,6},{3,7},{4,0},{5,1},{6,2},{7,3},{8,12},{9,13},{10,... | collective-permute-start | bytes 1585160 | tf_op jit(solution)/shard_map/ppermute | solution.py:296
  3.3 13.8 %collective-permute-start = (f32[1032,128]{1,0:T(8,128)}, f32[1032,128]{1,0:T(8,128)S(1)}, u32[]{:S(2)}, u32[]{:S(2)}) collective-permute-start(f32[1032,128]{1,0:T(8,128)} %pack.1.own_ref), channel_id=1, source_target_pairs={{0,1},{1,0},{2,3},{3,2},{4,5},{5,4},{6,7},{7,6},{8,9},{9,8},{10,11... | collective-permute-start | bytes 1585160 | tf_op jit(solution)/shard_map/ppermute | solution.py:306
  4.6 13.7 %collective-permute-start.4 = (f32[1032,128]{1,0:T(8,128)}, f32[1032,128]{1,0:T(8,128)S(1)}, u32[]{:S(2)}, u32[]{:S(2)}) collective-permute-start(f32[1032,128]{1,0:T(8,128)} %pack.1.own_ref), channel_id=1, source_target_pairs={{0,28},{1,13},{2,22},{3,7},{4,0},{5,17},{6,10},{7,27},{8,20},{9,5}... | collective-permute-start | bytes 1585160 | tf_op jit(solution)/shard_map/ppermute | solution.py:296
  5.0 15.1 %collective-permute-start.3 = (f32[1032,128]{1,0:T(8,128)}, f32[1032,128]{1,0:T(8,128)S(1)}, u32[]{:S(2)}, u32[]{:S(2)}) collective-permute-start(f32[1032,128]{1,0:T(8,128)} %pack.1.own_ref), channel_id=1, source_target_pairs={{0,0},{1,17},{2,10},{3,27},{4,28},{5,13},{6,22},{7,7},{8,8},{9,25}... | collective-permute-start | bytes 1585160 | tf_op jit(solution)/shard_map/ppermute | solution.py:296
  8.1 1.0 %copy-start = (f32[1032,128]{1,0:T(8,128)S(1)}, f32[1032,128]{1,0:T(8,128)}, u32[]{:S(2)}) copy-start(f32[1032,128]{1,0:T(8,128)} %pack.1.own_ref) | copy-start | bytes 1585156
  17.1 7.5 %collective-permute-start.2 = (f32[1032,128]{1,0:T(8,128)S(1)}, f32[1032,128]{1,0:T(8,128)S(1)}, u32[]{:S(2)}, u32[]{:S(2)}) collective-permute-start(f32[1032,128]{1,0:T(8,128)S(1)} %collective-permute-done.own_ref), channel_id=1, source_target_pairs={{0,4},{1,5},{2,6},{3,7},{4,0},{5,1},{6,2},{7,3},{8,12},{9,13},{10,... | collective-permute-start | bytes 1585160 | tf_op jit(solution)/shard_map/ppermute | solution.py:309
  18.3 12.1 %collective-permute-start.7 = (f32[1032,128]{1,0:T(8,128)S(1)}, f32[1032,128]{1,0:T(8,128)S(1)}, u32[]{:S(2)}, u32[]{:S(2)}) collective-permute-start(f32[1032,128]{1,0:T(8,128)S(1)} %collective-permute-done.own_ref), channel_id=1, source_target_pairs={{0,28},{1,13},{2,22},{3,7},{4,0},{5,17},{6,10},{7,27},{8,20},{9,5}... | collective-permute-start | bytes 1585160 | tf_op jit(solution)/shard_map/ppermute | solution.py:296
  20.1 15.7 %collective-permute-start.5 = (f32[1032,128]{1,0:T(8,128)S(1)}, f32[1032,128]{1,0:T(8,128)S(1)}, u32[]{:S(2)}, u32[]{:S(2)}) collective-permute-start(f32[1032,128]{1,0:T(8,128)S(1)} %collective-permute-done.own_ref), channel_id=1, source_target_pairs={{0,0},{1,17},{2,10},{3,27},{4,28},{5,13},{6,22},{7,7},{8,8},{9,25}... | collective-permute-start | bytes 1585160 | tf_op jit(solution)/shard_map/ppermute | solution.py:296
  31.3 10.6 %collective-permute-start.8 = (f32[256,256]{1,0:T(8,128)S(1)}, f32[256,256]{1,0:T(8,128)S(1)}, u32[]{:S(2)}, u32[]{:S(2)}) collective-permute-start(f32[256,256]{1,0:T(8,128)S(1)} %get-tuple-element.20), channel_id=1, source_target_pairs={{0,4},{1,6},{2,5},{3,7},{4,3},{5,1},{6,2},{7,0},{8,13},{9,15},{10,... | collective-permute-start | bytes 786440 | tf_op jit(solution)/shard_map/ppermute | solution.py:317
  32.6 10.8 %collective-permute-start.10 = (f32[256,256]{1,0:T(8,128)S(1)}, f32[256,256]{1,0:T(8,128)S(1)}, u32[]{:S(2)}, u32[]{:S(2)}) collective-permute-start(f32[256,256]{1,0:T(8,128)S(1)} %get-tuple-element.22), channel_id=1, source_target_pairs={{0,0},{1,2},{2,1},{3,3},{4,7},{5,5},{6,6},{7,4},{8,9},{9,11},{10,8... | collective-permute-start | bytes 786440 | tf_op jit(solution)/shard_map/ppermute | solution.py:316
  36.6 16.5 %collective-permute-start.6 = (f32[256,256]{1,0:T(8,128)S(1)}, f32[256,256]{1,0:T(8,128)S(1)}, u32[]{:S(2)}, u32[]{:S(2)}) collective-permute-start(f32[256,256]{1,0:T(8,128)S(1)} %get-tuple-element.17), channel_id=1, source_target_pairs={{0,4},{1,6},{2,5},{3,7},{4,3},{5,1},{6,2},{7,0},{8,13},{9,15},{10,... | collective-permute-start | bytes 786440 | tf_op jit(solution)/shard_map/ppermute | solution.py:317
  38.2 19.1 %collective-permute-start.9 = (f32[256,256]{1,0:T(8,128)S(1)}, f32[256,256]{1,0:T(8,128)S(1)}, u32[]{:S(2)}, u32[]{:S(2)}) collective-permute-start(f32[256,256]{1,0:T(8,128)S(1)} %get-tuple-element.21), channel_id=1, source_target_pairs={{0,0},{1,2},{2,1},{3,3},{4,7},{5,5},{6,6},{7,4},{8,9},{9,11},{10,8... | collective-permute-start | bytes 786440 | tf_op jit(solution)/shard_map/ppermute | solution.py:316

commit v6 on v5

--- a/solution.py
+++ b/solution.py
@@ -242,7 +242,7 @@
     )(dense, acc, piece)
 
 
-def join_kernel(cross_own_ref, cross_far_ref, same_own_ref, same_far_ref, out_hbm, out_ref, sems):
+def join_kernel(same_own_ref, cross_own_ref, cross_far_ref, same_far_ref, out_hbm, out_ref, sems):
     core = lax.axis_index("rows") & 1
     start = pl.multiple_of(core * PANEL, PANEL)
     size = PANEL // STEPS
@@ -315,7 +315,7 @@
         kept, other = second(near_dense, acc, piece, slots)
         same.append(lax.ppermute(kept, AXES, DONE_SAME))
         cross.append(lax.ppermute(other, AXES, DONE_CROSS))
-    return join(cross[0], cross[1], same[0], same[1])
+    return join(same[0], cross[0], cross[1], same[1])
 
 
 def densify(tile_set, row_ids, col_ids, live_mask, scale_set, block_count):

time: 58.4 us -> 58.1 us (level)
  starting transfers between devices: 18.3 us -> 17.2 us
  Pallas kernels: 8.23 us -> 8.83 us
    ppermute x2, waiting for transfers between devices: 5.67 us -> 7.17 us  [per_device(): same.append(lax.ppermute(kept, AXES, DONE_SAME))]
    ppermute x2, starting transfers between devices: 6.15 us -> 5.01 us  [per_device(): same.append(lax.ppermute(kept, AXES, DONE_SAME))]
    ppermute x2, waiting for transfers between devices: 10.4 us -> 9.43 us  [per_device(): cross.append(lax.ppermute(other, AXES, DONE_CROSS))]
    pallas_call x2, Pallas kernels: 2.16 us -> 2.75 us  [spread(): pl.pallas_call(functools.partial(spread_kernel, slots), out_shape=jax.Sha...]
  transfers between devices with their start and end apart: 11 -> 11, of which waited for: 8 -> 8; matrix products, arithmetic and copies ran while one was open for 0% -> 0% of each run, Pallas kernels for 9% -> 11%
where the time goes in v6:
time: 58.1 us; the launch traced here: 57.6 us
  waiting for transfers between devices  29.7 us (51%)
  starting transfers between devices  17.2 us (30%)
  Pallas kernels  8.83 us (15%)
  local copies, waits for them, and re-layouts  1.04 us (2%)
  between operations  0.77 us (1%)
    ppermute x2, waiting for transfers between devices, per_device(): cross.append(lax.ppermute(other, AXES, DONE_CROSS))  9.43 us
    ppermute x5, starting transfers between devices, send(): lax.ppermute(piece, AXES, perm)  7.19 us
    ppermute x2, waiting for transfers between devices, per_device(): same.append(lax.ppermute(kept, AXES, DONE_SAME))  7.17 us
    ppermute x1, waiting for transfers between devices, per_device(): near = lax.ppermute(own, AXES, NEXT)  6.72 us
    ppermute x5, waiting for transfers between devices, send(): lax.ppermute(piece, AXES, perm)  6.42 us
    ppermute x2, starting transfers between devices, per_device(): same.append(lax.ppermute(kept, AXES, DONE_SAME))  5.01 us
    ppermute x2, starting transfers between devices, per_device(): cross.append(lax.ppermute(other, AXES, DONE_CROSS))  2.82 us
    pallas_call x2, Pallas kernels, spread(): pl.pallas_call(functools.partial(spread_kernel, slots), out_shape=jax.Sha...  2.75 us
  transfers between devices with their start and end apart: 11, of which 8 were waited for; matrix products, arithmetic and copies ran while one was open for 0% of the time, Pallas kernels for 11%

profile of v6, /device:TPU:5, one launch (start us, length us, event | category | flops | bytes accessed | tf_op | source)
XLA Modules:
  0.0 57.6 jit_solution(17959278669683797252)
XLA Ops:
  0.7 1.9 %pack.1.own_ref = f32[1032,128]{1,0:T(8,128)} custom-call(s32[1,8]{1,0:T(1,128)} %rows_hbm.1, s32[1,8]{1,0:T(1,128)} %cols_hbm.1, s32[1,1]{1,0:T(1,128)S(6)} %copy.6.counts_hbm, f32[1,8,128,128]{3,2,1,0:T(8,128)} %tiles_hbm.1, f32[16,128]{1,0:T(8,128)} %bitcast.1), custom_call_target="tpu_custom_call" | custom-call | flops 131072 | bytes 1572864 | tf_op jit(solution)/shard_map/pack/pallas_call | solution.py:76
  2.6 0.7 %collective-permute-start.1 = (f32[1032,128]{1,0:T(8,128)}, f32[1032,128]{1,0:T(8,128)S(1)}, u32[]{:S(2)}, u32[]{:S(2)}) collective-permute-start(f32[1032,128]{1,0:T(8,128)} %pack.1.own_ref), channel_id=1, source_target_pairs={{0,4},{1,5},{2,6},{3,7},{4,0},{5,1},{6,2},{7,3},{8,12},{9,13},{10,... | collective-permute-start | bytes 1585160 | tf_op jit(solution)/shard_map/ppermute | solution.py:296
  3.3 1.3 %collective-permute-start = (f32[1032,128]{1,0:T(8,128)}, f32[1032,128]{1,0:T(8,128)S(1)}, u32[]{:S(2)}, u32[]{:S(2)}) collective-permute-start(f32[1032,128]{1,0:T(8,128)} %pack.1.own_ref), channel_id=1, source_target_pairs={{0,1},{1,0},{2,3},{3,2},{4,5},{5,4},{6,7},{7,6},{8,9},{9,8},{10,11... | collective-permute-start | bytes 1585160 | tf_op jit(solution)/shard_map/ppermute | solution.py:306
  4.6 0.3 collective-permute-start.4
  5.0 3.0 %collective-permute-start.3 = (f32[1032,128]{1,0:T(8,128)}, f32[1032,128]{1,0:T(8,128)S(1)}, u32[]{:S(2)}, u32[]{:S(2)}) collective-permute-start(f32[1032,128]{1,0:T(8,128)} %pack.1.own_ref), channel_id=1, source_target_pairs={{0,0},{1,17},{2,10},{3,27},{4,28},{5,13},{6,22},{7,7},{8,8},{9,25}... | collective-permute-start | bytes 1585160 | tf_op jit(solution)/shard_map/ppermute | solution.py:296
  8.0 0.0 collective-permute-done.1.other_ref
  8.1 0.0 copy-start
  8.1 1.0 %copy-done = f32[1032,128]{1,0:T(8,128)S(1)} copy-done((f32[1032,128]{1,0:T(8,128)S(1)}, f32[1032,128]{1,0:T(8,128)}, u32[]{:S(2)}) %copy-start) | copy-done | bytes 528408
  9.1 1.3 %spread.2.dense_ref = bf16[16,512,256]{2,1,0:T(8,128)(2,1)S(1)} custom-call(f32[1032,128]{1,0:T(8,128)S(1)} %copy-done, f32[1032,128]{1,0:T(8,128)S(1)} %collective-permute-done.1.other_ref), custom_call_target="tpu_custom_call" | custom-call | flops 33554432 | bytes 33554432 | tf_op jit(solution)/shard_map/spread/pallas_call | solution.py:141
  10.4 6.7 %collective-permute-done.own_ref = f32[1032,128]{1,0:T(8,128)S(1)} collective-permute-done((f32[1032,128]{1,0:T(8,128)}, f32[1032,128]{1,0:T(8,128)S(1)}, u32[]{:S(2)}, u32[]{:S(2)}) %collective-permute-start) | collective-permute-done | bytes 528416 | tf_op jit(solution)/shard_map/ppermute | solution.py:306
  17.1 0.9 %collective-permute-start.2 = (f32[1032,128]{1,0:T(8,128)S(1)}, f32[1032,128]{1,0:T(8,128)S(1)}, u32[]{:S(2)}, u32[]{:S(2)}) collective-permute-start(f32[1032,128]{1,0:T(8,128)S(1)} %collective-permute-done.own_ref), channel_id=1, source_target_pairs={{0,4},{1,5},{2,6},{3,7},{4,0},{5,1},{6,2},{7,3},{8,12},{9,13},{10,... | collective-permute-start | bytes 1585160 | tf_op jit(solution)/shard_map/ppermute | solution.py:309
  18.0 0.4 collective-permute-done.4.refs_1_
  18.3 0.0 collective-permute-start.8
  18.4 1.7 %collective-permute-done.3.refs_0_ = f32[1032,128]{1,0:T(8,128)S(1)} collective-permute-done((f32[1032,128]{1,0:T(8,128)}, f32[1032,128]{1,0:T(8,128)S(1)}, u32[]{:S(2)}, u32[]{:S(2)}) %collective-permute-start.3) | collective-permute-done | bytes 528416 | tf_op jit(solution)/shard_map/ppermute | solution.py:296
  20.1 3.0 %collective-permute-start.5 = (f32[1032,128]{1,0:T(8,128)S(1)}, f32[1032,128]{1,0:T(8,128)S(1)}, u32[]{:S(2)}, u32[]{:S(2)}) collective-permute-start(f32[1032,128]{1,0:T(8,128)S(1)} %collective-permute-done.own_ref), channel_id=1, source_target_pairs={{0,0},{1,17},{2,10},{3,27},{4,28},{5,13},{6,22},{7,7},{8,8},{9,25}... | collective-permute-start | bytes 1585160 | tf_op jit(solution)/shard_map/ppermute | solution.py:296
  23.1 1.5 %first.1 = (f32[2,512,128]{2,1,0:T(8,128)S(1)}, f32[2,512,128]{2,1,0:T(8,128)S(1)}) custom-call(bf16[16,512,256]{2,1,0:T(8,128)(2,1)S(1)} %spread.2.dense_ref, f32[1032,128]{1,0:T(8,128)S(1)} %collective-permute-done.3.refs_0_, f32[1032,128]{1,0:T(8,128)S(1)} %collective-permute-done.4.refs_1_), custom_call_target="tpu_custom_call" | custom-call | flops 33554432 | bytes 33554432 | tf_op jit(solution)/shard_map/first/pallas_call | solution.py:207
  24.7 0.0 collective-permute-done.2.other_ref
  24.7 1.4 %spread.3.dense_ref = bf16[16,512,256]{2,1,0:T(8,128)(2,1)S(1)} custom-call(f32[1032,128]{1,0:T(8,128)S(1)} %collective-permute-done.own_ref, f32[1032,128]{1,0:T(8,128)S(1)} %collective-permute-done.2.other_ref), custom_call_target="tpu_custom_call" | custom-call | flops 33554432 | bytes 33554432 | tf_op jit(solution)/shard_map/spread/pallas_call | solution.py:141
  26.1 4.3 %collective-permute-done.8.piece_ref = f32[1032,128]{1,0:T(8,128)S(1)} collective-permute-done((f32[1032,128]{1,0:T(8,128)S(1)}, f32[1032,128]{1,0:T(8,128)S(1)}, u32[]{:S(2)}, u32[]{:S(2)}) %collective-permute-start.8) | collective-permute-done | bytes 528416 | tf_op jit(solution)/shard_map/ppermute | solution.py:296
  30.5 0.9 %second.3 = (f32[256,256]{1,0:T(8,128)S(1)}, f32[256,256]{1,0:T(8,128)S(1)}) custom-call(bf16[16,512,256]{2,1,0:T(8,128)(2,1)S(1)} %spread.3.dense_ref, f32[2,512,128]{2,1,0:T(8,128)S(1)} %get-tuple-element.19.acc_ref, f32[1032,128]{1,0:T(8,128)S(1)} %collective-permute-done.8.piece_ref), custom_call_target="tpu_custom_call" | custom-call | flops 33554432 | bytes 33554432 | tf_op jit(solution)/shard_map/second/pallas_call | solution.py:233
  31.4 1.3 %collective-permute-start.9 = (f32[256,256]{1,0:T(8,128)S(1)}, f32[256,256]{1,0:T(8,128)S(1)}, u32[]{:S(2)}, u32[]{:S(2)}) collective-permute-start(f32[256,256]{1,0:T(8,128)S(1)} %get-tuple-element.21), channel_id=1, source_target_pairs={{0,4},{1,6},{2,5},{3,7},{4,3},{5,1},{6,2},{7,0},{8,13},{9,15},{10,... | collective-permute-start | bytes 786440 | tf_op jit(solution)/shard_map/ppermute | solution.py:317
  32.6 3.1 %collective-permute-start.10 = (f32[256,256]{1,0:T(8,128)S(1)}, f32[256,256]{1,0:T(8,128)S(1)}, u32[]{:S(2)}, u32[]{:S(2)}) collective-permute-start(f32[256,256]{1,0:T(8,128)S(1)} %get-tuple-element.22), channel_id=1, source_target_pairs={{0,0},{1,2},{2,1},{3,3},{4,7},{5,5},{6,6},{7,4},{8,9},{9,11},{10,8... | collective-permute-start | bytes 786440 | tf_op jit(solution)/shard_map/ppermute | solution.py:316
  35.7 0.0 collective-permute-done.5.piece_ref
  35.7 0.9 %second.2 = (f32[256,256]{1,0:T(8,128)S(1)}, f32[256,256]{1,0:T(8,128)S(1)}) custom-call(bf16[16,512,256]{2,1,0:T(8,128)(2,1)S(1)} %spread.3.dense_ref, f32[2,512,128]{2,1,0:T(8,128)S(1)} %get-tuple-element.15.acc_ref, f32[1032,128]{1,0:T(8,128)S(1)} %collective-permute-done.5.piece_ref), custom_call_target="tpu_custom_call" | custom-call | flops 33554432 | bytes 33554432 | tf_op jit(solution)/shard_map/second/pallas_call | solution.py:233
  36.6 1.9 %collective-permute-start.6 = (f32[256,256]{1,0:T(8,128)S(1)}, f32[256,256]{1,0:T(8,128)S(1)}, u32[]{:S(2)}, u32[]{:S(2)}) collective-permute-start(f32[256,256]{1,0:T(8,128)S(1)} %get-tuple-element.17), channel_id=1, source_target_pairs={{0,0},{1,2},{2,1},{3,3},{4,7},{5,5},{6,6},{7,4},{8,9},{9,11},{10,8... | collective-permute-start | bytes 786440 | tf_op jit(solution)/shard_map/ppermute | solution.py:316
  38.6 1.5 %collective-permute-start.7 = (f32[256,256]{1,0:T(8,128)S(1)}, f32[256,256]{1,0:T(8,128)S(1)}, u32[]{:S(2)}, u32[]{:S(2)}) collective-permute-start(f32[256,256]{1,0:T(8,128)S(1)} %get-tuple-element.18), channel_id=1, source_target_pairs={{0,4},{1,6},{2,5},{3,7},{4,3},{5,1},{6,2},{7,0},{8,13},{9,15},{10,... | collective-permute-start | bytes 786440 | tf_op jit(solution)/shard_map/ppermute | solution.py:317
  40.1 1.8 %collective-permute-done.9.cross_far_ref = f32[256,256]{1,0:T(8,128)S(1)} collective-permute-done((f32[256,256]{1,0:T(8,128)S(1)}, f32[256,256]{1,0:T(8,128)S(1)}, u32[]{:S(2)}, u32[]{:S(2)}) %collective-permute-start.9) | collective-permute-done | bytes 262176 | tf_op jit(solution)/shard_map/ppermute | solution.py:317
  41.9 1.6 %collective-permute-done.10.same_far_ref = f32[256,256]{1,0:T(8,128)S(1)} collective-permute-done((f32[256,256]{1,0:T(8,128)S(1)}, f32[256,256]{1,0:T(8,128)S(1)}, u32[]{:S(2)}, u32[]{:S(2)}) %collective-permute-start.10) | collective-permute-done | bytes 262176 | tf_op jit(solution)/shard_map/ppermute | solution.py:316
  43.4 5.6 %collective-permute-done.6.same_own_ref = f32[256,256]{1,0:T(8,128)S(1)} collective-permute-done((f32[256,256]{1,0:T(8,128)S(1)}, f32[256,256]{1,0:T(8,128)S(1)}, u32[]{:S(2)}, u32[]{:S(2)}) %collective-permute-start.6) | collective-permute-done | bytes 262176 | tf_op jit(solution)/shard_map/ppermute | solution.py:316
  49.1 7.7 %collective-permute-done.7.cross_own_ref = f32[256,256]{1,0:T(8,128)S(1)} collective-permute-done((f32[256,256]{1,0:T(8,128)S(1)}, f32[256,256]{1,0:T(8,128)S(1)}, u32[]{:S(2)}, u32[]{:S(2)}) %collective-permute-start.7) | collective-permute-done | bytes 262176 | tf_op jit(solution)/shard_map/ppermute | solution.py:317
  56.7 0.8 %join.1 = f32[256,512]{1,0:T(8,128)} custom-call(f32[256,256]{1,0:T(8,128)S(1)} %collective-permute-done.6.same_own_ref, f32[256,256]{1,0:T(8,128)S(1)} %collective-permute-done.7.cross_own_ref, f32[256,256]{1,0:T(8,128)S(1)} %collective-permute-done.9.cross_far_ref, f32[256,256]{1,0:T(8,128)S(1)} %collective-permute-done.10.same_far_ref), custom_call_target="tpu_custom_call" | custom-call | flops 131072 | bytes 131072 | tf_op jit(solution)/shard_map/join/pallas_call | solution.py:262
Async XLA Ops:
  2.6 5.5 %collective-permute-start.1 = (f32[1032,128]{1,0:T(8,128)}, f32[1032,128]{1,0:T(8,128)S(1)}, u32[]{:S(2)}, u32[]{:S(2)}) collective-permute-start(f32[1032,128]{1,0:T(8,128)} %pack.1.own_ref), channel_id=1, source_target_pairs={{0,4},{1,5},{2,6},{3,7},{4,0},{5,1},{6,2},{7,3},{8,12},{9,13},{10,... | collective-permute-start | bytes 1585160 | tf_op jit(solution)/shard_map/ppermute | solution.py:296
  3.3 13.8 %collective-permute-start = (f32[1032,128]{1,0:T(8,128)}, f32[1032,128]{1,0:T(8,128)S(1)}, u32[]{:S(2)}, u32[]{:S(2)}) collective-permute-start(f32[1032,128]{1,0:T(8,128)} %pack.1.own_ref), channel_id=1, source_target_pairs={{0,1},{1,0},{2,3},{3,2},{4,5},{5,4},{6,7},{7,6},{8,9},{9,8},{10,11... | collective-permute-start | bytes 1585160 | tf_op jit(solution)/shard_map/ppermute | solution.py:306
  4.6 13.7 %collective-permute-start.4 = (f32[1032,128]{1,0:T(8,128)}, f32[1032,128]{1,0:T(8,128)S(1)}, u32[]{:S(2)}, u32[]{:S(2)}) collective-permute-start(f32[1032,128]{1,0:T(8,128)} %pack.1.own_ref), channel_id=1, source_target_pairs={{0,28},{1,13},{2,22},{3,7},{4,0},{5,17},{6,10},{7,27},{8,20},{9,5}... | collective-permute-start | bytes 1585160 | tf_op jit(solution)/shard_map/ppermute | solution.py:296
  5.0 15.1 %collective-permute-start.3 = (f32[1032,128]{1,0:T(8,128)}, f32[1032,128]{1,0:T(8,128)S(1)}, u32[]{:S(2)}, u32[]{:S(2)}) collective-permute-start(f32[1032,128]{1,0:T(8,128)} %pack.1.own_ref), channel_id=1, source_target_pairs={{0,0},{1,17},{2,10},{3,27},{4,28},{5,13},{6,22},{7,7},{8,8},{9,25}... | collective-permute-start | bytes 1585160 | tf_op jit(solution)/shard_map/ppermute | solution.py:296
  8.1 1.0 %copy-start = (f32[1032,128]{1,0:T(8,128)S(1)}, f32[1032,128]{1,0:T(8,128)}, u32[]{:S(2)}) copy-start(f32[1032,128]{1,0:T(8,128)} %pack.1.own_ref) | copy-start | bytes 1585156
  17.1 7.5 %collective-permute-start.2 = (f32[1032,128]{1,0:T(8,128)S(1)}, f32[1032,128]{1,0:T(8,128)S(1)}, u32[]{:S(2)}, u32[]{:S(2)}) collective-permute-start(f32[1032,128]{1,0:T(8,128)S(1)} %collective-permute-done.own_ref), channel_id=1, source_target_pairs={{0,4},{1,5},{2,6},{3,7},{4,0},{5,1},{6,2},{7,3},{8,12},{9,13},{10,... | collective-permute-start | bytes 1585160 | tf_op jit(solution)/shard_map/ppermute | solution.py:309
  18.3 12.1 %collective-permute-start.8 = (f32[1032,128]{1,0:T(8,128)S(1)}, f32[1032,128]{1,0:T(8,128)S(1)}, u32[]{:S(2)}, u32[]{:S(2)}) collective-permute-start(f32[1032,128]{1,0:T(8,128)S(1)} %collective-permute-done.own_ref), channel_id=1, source_target_pairs={{0,28},{1,13},{2,22},{3,7},{4,0},{5,17},{6,10},{7,27},{8,20},{9,5}... | collective-permute-start | bytes 1585160 | tf_op jit(solution)/shard_map/ppermute | solution.py:296
  20.1 15.7 %collective-permute-start.5 = (f32[1032,128]{1,0:T(8,128)S(1)}, f32[1032,128]{1,0:T(8,128)S(1)}, u32[]{:S(2)}, u32[]{:S(2)}) collective-permute-start(f32[1032,128]{1,0:T(8,128)S(1)} %collective-permute-done.own_ref), channel_id=1, source_target_pairs={{0,0},{1,17},{2,10},{3,27},{4,28},{5,13},{6,22},{7,7},{8,8},{9,25}... | collective-permute-start | bytes 1585160 | tf_op jit(solution)/shard_map/ppermute | solution.py:296
  31.4 10.5 %collective-permute-start.9 = (f32[256,256]{1,0:T(8,128)S(1)}, f32[256,256]{1,0:T(8,128)S(1)}, u32[]{:S(2)}, u32[]{:S(2)}) collective-permute-start(f32[256,256]{1,0:T(8,128)S(1)} %get-tuple-element.21), channel_id=1, source_target_pairs={{0,4},{1,6},{2,5},{3,7},{4,3},{5,1},{6,2},{7,0},{8,13},{9,15},{10,... | collective-permute-start | bytes 786440 | tf_op jit(solution)/shard_map/ppermute | solution.py:317
  32.6 10.8 %collective-permute-start.10 = (f32[256,256]{1,0:T(8,128)S(1)}, f32[256,256]{1,0:T(8,128)S(1)}, u32[]{:S(2)}, u32[]{:S(2)}) collective-permute-start(f32[256,256]{1,0:T(8,128)S(1)} %get-tuple-element.22), channel_id=1, source_target_pairs={{0,0},{1,2},{2,1},{3,3},{4,7},{5,5},{6,6},{7,4},{8,9},{9,11},{10,8... | collective-permute-start | bytes 786440 | tf_op jit(solution)/shard_map/ppermute | solution.py:316
  36.6 12.4 %collective-permute-start.6 = (f32[256,256]{1,0:T(8,128)S(1)}, f32[256,256]{1,0:T(8,128)S(1)}, u32[]{:S(2)}, u32[]{:S(2)}) collective-permute-start(f32[256,256]{1,0:T(8,128)S(1)} %get-tuple-element.17), channel_id=1, source_target_pairs={{0,0},{1,2},{2,1},{3,3},{4,7},{5,5},{6,6},{7,4},{8,9},{9,11},{10,8... | collective-permute-start | bytes 786440 | tf_op jit(solution)/shard_map/ppermute | solution.py:316
  38.6 18.1 %collective-permute-start.7 = (f32[256,256]{1,0:T(8,128)S(1)}, f32[256,256]{1,0:T(8,128)S(1)}, u32[]{:S(2)}, u32[]{:S(2)}) collective-permute-start(f32[256,256]{1,0:T(8,128)S(1)} %get-tuple-element.18), channel_id=1, source_target_pairs={{0,4},{1,6},{2,5},{3,7},{4,3},{5,1},{6,2},{7,0},{8,13},{9,15},{10,... | collective-permute-start | bytes 786440 | tf_op jit(solution)/shard_map/ppermute | solution.py:317

commit v7 on v6

--- a/solution.py
+++ b/solution.py
@@ -12,7 +12,7 @@
 CB_DEV = 16
 PANEL = RB * TB
 META = 8
-FEW = 5
+FEW = 8
 STEPS = 4
 AXES = ("rows", "cols")
 VMEM_LIMIT = 16 * 1024 * 1024

time: 58.1 us -> 58.5 us (level)
  Pallas kernels: 8.83 us -> 10.3 us
  waiting for transfers between devices: 29.7 us -> 28.7 us
    pallas_call x1, Pallas kernels: 1.53 us -> 2.41 us  [first(): pl.pallas_call(functools.partial(first_kernel, slots), out_shape=[jax.Sha...]
    pallas_call x2, Pallas kernels: 1.78 us -> 2.61 us  [second(): pl.pallas_call(functools.partial(second_kernel, slots), out_shape=[jax.Sh...]
    ppermute x5, waiting for transfers between devices: 6.42 us -> 5.66 us  [send(): lax.ppermute(piece, AXES, perm)]
  transfers between devices with their start and end apart: 11 -> 11, of which waited for: 8 -> 8; matrix products, arithmetic and copies ran while one was open for 0% -> 0% of each run, Pallas kernels for 11% -> 13%
where the time goes in v7:
time: 58.5 us; the launch traced here: 58 us
  waiting for transfers between devices  28.7 us (49%)
  starting transfers between devices  17.2 us (29%)
  Pallas kernels  10.3 us (18%)
  local copies, waits for them, and re-layouts  1.04 us (2%)
  between operations  0.76 us (1%)
    ppermute x2, waiting for transfers between devices, per_device(): cross.append(lax.ppermute(other, AXES, DONE_CROSS))  9.04 us
    ppermute x5, starting transfers between devices, send(): lax.ppermute(piece, AXES, perm)  7.19 us
    ppermute x2, waiting for transfers between devices, per_device(): same.append(lax.ppermute(kept, AXES, DONE_SAME))  7.17 us
    ppermute x1, waiting for transfers between devices, per_device(): near = lax.ppermute(own, AXES, NEXT)  6.85 us
    ppermute x5, waiting for transfers between devices, send(): lax.ppermute(piece, AXES, perm)  5.66 us
    ppermute x2, starting transfers between devices, per_device(): same.append(lax.ppermute(kept, AXES, DONE_SAME))  5 us
    ppermute x2, starting transfers between devices, per_device(): cross.append(lax.ppermute(other, AXES, DONE_CROSS))  2.83 us
    pallas_call x2, Pallas kernels, second(): pl.pallas_call(functools.partial(second_kernel, slots), out_shape=[jax.Sh...  2.61 us
  transfers between devices with their start and end apart: 11, of which 8 were waited for; matrix products, arithmetic and copies ran while one was open for 0% of the time, Pallas kernels for 13%

profile of v7, /device:TPU:5, one launch (start us, length us, event | category | flops | bytes accessed | tf_op | source)
XLA Modules:
  0.0 58.0 jit_solution(1700656089033032250)
XLA Ops:
  0.7 1.9 %pack.1.own_ref = f32[1032,128]{1,0:T(8,128)} custom-call(s32[1,8]{1,0:T(1,128)} %rows_hbm.1, s32[1,8]{1,0:T(1,128)} %cols_hbm.1, s32[1,1]{1,0:T(1,128)S(6)} %copy.6.counts_hbm, f32[1,8,128,128]{3,2,1,0:T(8,128)} %tiles_hbm.1, f32[16,128]{1,0:T(8,128)} %bitcast.1), custom_call_target="tpu_custom_call" | custom-call | flops 131072 | bytes 1572864 | tf_op jit(solution)/shard_map/pack/pallas_call | solution.py:76
  2.6 0.7 %collective-permute-start.1 = (f32[1032,128]{1,0:T(8,128)}, f32[1032,128]{1,0:T(8,128)S(1)}, u32[]{:S(2)}, u32[]{:S(2)}) collective-permute-start(f32[1032,128]{1,0:T(8,128)} %pack.1.own_ref), channel_id=1, source_target_pairs={{0,4},{1,5},{2,6},{3,7},{4,0},{5,1},{6,2},{7,3},{8,12},{9,13},{10,... | collective-permute-start | bytes 1585160 | tf_op jit(solution)/shard_map/ppermute | solution.py:296
  3.3 1.3 %collective-permute-start = (f32[1032,128]{1,0:T(8,128)}, f32[1032,128]{1,0:T(8,128)S(1)}, u32[]{:S(2)}, u32[]{:S(2)}) collective-permute-start(f32[1032,128]{1,0:T(8,128)} %pack.1.own_ref), channel_id=1, source_target_pairs={{0,1},{1,0},{2,3},{3,2},{4,5},{5,4},{6,7},{7,6},{8,9},{9,8},{10,11... | collective-permute-start | bytes 1585160 | tf_op jit(solution)/shard_map/ppermute | solution.py:306
  4.6 0.3 collective-permute-start.4
  5.0 3.0 %collective-permute-start.3 = (f32[1032,128]{1,0:T(8,128)}, f32[1032,128]{1,0:T(8,128)S(1)}, u32[]{:S(2)}, u32[]{:S(2)}) collective-permute-start(f32[1032,128]{1,0:T(8,128)} %pack.1.own_ref), channel_id=1, source_target_pairs={{0,0},{1,17},{2,10},{3,27},{4,28},{5,13},{6,22},{7,7},{8,8},{9,25}... | collective-permute-start | bytes 1585160 | tf_op jit(solution)/shard_map/ppermute | solution.py:296
  8.0 0.0 collective-permute-done.1.other_ref
  8.1 0.0 copy-start
  8.1 1.0 %copy-done = f32[1032,128]{1,0:T(8,128)S(1)} copy-done((f32[1032,128]{1,0:T(8,128)S(1)}, f32[1032,128]{1,0:T(8,128)}, u32[]{:S(2)}) %copy-start) | copy-done | bytes 528408
  9.1 1.2 %spread.2.dense_ref = bf16[16,512,256]{2,1,0:T(8,128)(2,1)S(1)} custom-call(f32[1032,128]{1,0:T(8,128)S(1)} %copy-done, f32[1032,128]{1,0:T(8,128)S(1)} %collective-permute-done.1.other_ref), custom_call_target="tpu_custom_call" | custom-call | flops 33554432 | bytes 33554432 | tf_op jit(solution)/shard_map/spread/pallas_call | solution.py:141
  10.3 6.9 %collective-permute-done.own_ref = f32[1032,128]{1,0:T(8,128)S(1)} collective-permute-done((f32[1032,128]{1,0:T(8,128)}, f32[1032,128]{1,0:T(8,128)S(1)}, u32[]{:S(2)}, u32[]{:S(2)}) %collective-permute-start) | collective-permute-done | bytes 528416 | tf_op jit(solution)/shard_map/ppermute | solution.py:306
  17.1 0.9 %collective-permute-start.2 = (f32[1032,128]{1,0:T(8,128)S(1)}, f32[1032,128]{1,0:T(8,128)S(1)}, u32[]{:S(2)}, u32[]{:S(2)}) collective-permute-start(f32[1032,128]{1,0:T(8,128)S(1)} %collective-permute-done.own_ref), channel_id=1, source_target_pairs={{0,4},{1,5},{2,6},{3,7},{4,0},{5,1},{6,2},{7,3},{8,12},{9,13},{10,... | collective-permute-start | bytes 1585160 | tf_op jit(solution)/shard_map/ppermute | solution.py:309
  18.0 0.4 collective-permute-done.4.refs_1_
  18.3 0.0 collective-permute-start.8
  18.4 1.7 %collective-permute-done.3.refs_0_ = f32[1032,128]{1,0:T(8,128)S(1)} collective-permute-done((f32[1032,128]{1,0:T(8,128)}, f32[1032,128]{1,0:T(8,128)S(1)}, u32[]{:S(2)}, u32[]{:S(2)}) %collective-permute-start.3) | collective-permute-done | bytes 528416 | tf_op jit(solution)/shard_map/ppermute | solution.py:296
  20.1 3.1 %collective-permute-start.5 = (f32[1032,128]{1,0:T(8,128)S(1)}, f32[1032,128]{1,0:T(8,128)S(1)}, u32[]{:S(2)}, u32[]{:S(2)}) collective-permute-start(f32[1032,128]{1,0:T(8,128)S(1)} %collective-permute-done.own_ref), channel_id=1, source_target_pairs={{0,0},{1,17},{2,10},{3,27},{4,28},{5,13},{6,22},{7,7},{8,8},{9,25}... | collective-permute-start | bytes 1585160 | tf_op jit(solution)/shard_map/ppermute | solution.py:296
  23.1 2.4 %first.1 = (f32[2,512,128]{2,1,0:T(8,128)S(1)}, f32[2,512,128]{2,1,0:T(8,128)S(1)}) custom-call(bf16[16,512,256]{2,1,0:T(8,128)(2,1)S(1)} %spread.2.dense_ref, f32[1032,128]{1,0:T(8,128)S(1)} %collective-permute-done.3.refs_0_, f32[1032,128]{1,0:T(8,128)S(1)} %collective-permute-done.4.refs_1_), custom_call_target="tpu_custom_call" | custom-call | flops 33554432 | bytes 33554432 | tf_op jit(solution)/shard_map/first/pallas_call | solution.py:207
  25.5 0.0 collective-permute-done.2.other_ref
  25.6 1.3 %spread.3.dense_ref = bf16[16,512,256]{2,1,0:T(8,128)(2,1)S(1)} custom-call(f32[1032,128]{1,0:T(8,128)S(1)} %collective-permute-done.own_ref, f32[1032,128]{1,0:T(8,128)S(1)} %collective-permute-done.2.other_ref), custom_call_target="tpu_custom_call" | custom-call | flops 33554432 | bytes 33554432 | tf_op jit(solution)/shard_map/spread/pallas_call | solution.py:141
  26.9 3.6 %collective-permute-done.8.piece_ref = f32[1032,128]{1,0:T(8,128)S(1)} collective-permute-done((f32[1032,128]{1,0:T(8,128)S(1)}, f32[1032,128]{1,0:T(8,128)S(1)}, u32[]{:S(2)}, u32[]{:S(2)}) %collective-permute-start.8) | collective-permute-done | bytes 528416 | tf_op jit(solution)/shard_map/ppermute | solution.py:296
  30.5 1.3 %second.3 = (f32[256,256]{1,0:T(8,128)S(1)}, f32[256,256]{1,0:T(8,128)S(1)}) custom-call(bf16[16,512,256]{2,1,0:T(8,128)(2,1)S(1)} %spread.3.dense_ref, f32[2,512,128]{2,1,0:T(8,128)S(1)} %get-tuple-element.19.acc_ref, f32[1032,128]{1,0:T(8,128)S(1)} %collective-permute-done.8.piece_ref), custom_call_target="tpu_custom_call" | custom-call | flops 33554432 | bytes 33554432 | tf_op jit(solution)/shard_map/second/pallas_call | solution.py:233
  31.8 1.3 %collective-permute-start.9 = (f32[256,256]{1,0:T(8,128)S(1)}, f32[256,256]{1,0:T(8,128)S(1)}, u32[]{:S(2)}, u32[]{:S(2)}) collective-permute-start(f32[256,256]{1,0:T(8,128)S(1)} %get-tuple-element.21), channel_id=1, source_target_pairs={{0,4},{1,6},{2,5},{3,7},{4,3},{5,1},{6,2},{7,0},{8,13},{9,15},{10,... | collective-permute-start | bytes 786440 | tf_op jit(solution)/shard_map/ppermute | solution.py:317
  33.0 3.1 %collective-permute-start.10 = (f32[256,256]{1,0:T(8,128)S(1)}, f32[256,256]{1,0:T(8,128)S(1)}, u32[]{:S(2)}, u32[]{:S(2)}) collective-permute-start(f32[256,256]{1,0:T(8,128)S(1)} %get-tuple-element.22), channel_id=1, source_target_pairs={{0,0},{1,2},{2,1},{3,3},{4,7},{5,5},{6,6},{7,4},{8,9},{9,11},{10,8... | collective-permute-start | bytes 786440 | tf_op jit(solution)/shard_map/ppermute | solution.py:316
  36.1 0.0 collective-permute-done.5.piece_ref
  36.1 1.3 %second.2 = (f32[256,256]{1,0:T(8,128)S(1)}, f32[256,256]{1,0:T(8,128)S(1)}) custom-call(bf16[16,512,256]{2,1,0:T(8,128)(2,1)S(1)} %spread.3.dense_ref, f32[2,512,128]{2,1,0:T(8,128)S(1)} %get-tuple-element.15.acc_ref, f32[1032,128]{1,0:T(8,128)S(1)} %collective-permute-done.5.piece_ref), custom_call_target="tpu_custom_call" | custom-call | flops 33554432 | bytes 33554432 | tf_op jit(solution)/shard_map/second/pallas_call | solution.py:233
  37.5 1.9 %collective-permute-start.6 = (f32[256,256]{1,0:T(8,128)S(1)}, f32[256,256]{1,0:T(8,128)S(1)}, u32[]{:S(2)}, u32[]{:S(2)}) collective-permute-start(f32[256,256]{1,0:T(8,128)S(1)} %get-tuple-element.17), channel_id=1, source_target_pairs={{0,0},{1,2},{2,1},{3,3},{4,7},{5,5},{6,6},{7,4},{8,9},{9,11},{10,8... | collective-permute-start | bytes 786440 | tf_op jit(solution)/shard_map/ppermute | solution.py:316
  39.4 1.6 %collective-permute-start.7 = (f32[256,256]{1,0:T(8,128)S(1)}, f32[256,256]{1,0:T(8,128)S(1)}, u32[]{:S(2)}, u32[]{:S(2)}) collective-permute-start(f32[256,256]{1,0:T(8,128)S(1)} %get-tuple-element.18), channel_id=1, source_target_pairs={{0,4},{1,6},{2,5},{3,7},{4,3},{5,1},{6,2},{7,0},{8,13},{9,15},{10,... | collective-permute-start | bytes 786440 | tf_op jit(solution)/shard_map/ppermute | solution.py:317
  40.9 1.4 %collective-permute-done.9.cross_far_ref = f32[256,256]{1,0:T(8,128)S(1)} collective-permute-done((f32[256,256]{1,0:T(8,128)S(1)}, f32[256,256]{1,0:T(8,128)S(1)}, u32[]{:S(2)}, u32[]{:S(2)}) %collective-permute-start.9) | collective-permute-done | bytes 262176 | tf_op jit(solution)/shard_map/ppermute | solution.py:317
  42.3 1.6 %collective-permute-done.10.same_far_ref = f32[256,256]{1,0:T(8,128)S(1)} collective-permute-done((f32[256,256]{1,0:T(8,128)S(1)}, f32[256,256]{1,0:T(8,128)S(1)}, u32[]{:S(2)}, u32[]{:S(2)}) %collective-permute-start.10) | collective-permute-done | bytes 262176 | tf_op jit(solution)/shard_map/ppermute | solution.py:316
  43.9 5.6 %collective-permute-done.6.same_own_ref = f32[256,256]{1,0:T(8,128)S(1)} collective-permute-done((f32[256,256]{1,0:T(8,128)S(1)}, f32[256,256]{1,0:T(8,128)S(1)}, u32[]{:S(2)}, u32[]{:S(2)}) %collective-permute-start.6) | collective-permute-done | bytes 262176 | tf_op jit(solution)/shard_map/ppermute | solution.py:316
  49.5 7.7 %collective-permute-done.7.cross_own_ref = f32[256,256]{1,0:T(8,128)S(1)} collective-permute-done((f32[256,256]{1,0:T(8,128)S(1)}, f32[256,256]{1,0:T(8,128)S(1)}, u32[]{:S(2)}, u32[]{:S(2)}) %collective-permute-start.7) | collective-permute-done | bytes 262176 | tf_op jit(solution)/shard_map/ppermute | solution.py:317
  57.1 0.8 %join.1 = f32[256,512]{1,0:T(8,128)} custom-call(f32[256,256]{1,0:T(8,128)S(1)} %collective-permute-done.6.same_own_ref, f32[256,256]{1,0:T(8,128)S(1)} %collective-permute-done.7.cross_own_ref, f32[256,256]{1,0:T(8,128)S(1)} %collective-permute-done.9.cross_far_ref, f32[256,256]{1,0:T(8,128)S(1)} %collective-permute-done.10.same_far_ref), custom_call_target="tpu_custom_call" | custom-call | flops 131072 | bytes 131072 | tf_op jit(solution)/shard_map/join/pallas_call | solution.py:262
Async XLA Ops:
  2.6 5.5 %collective-permute-start.1 = (f32[1032,128]{1,0:T(8,128)}, f32[1032,128]{1,0:T(8,128)S(1)}, u32[]{:S(2)}, u32[]{:S(2)}) collective-permute-start(f32[1032,128]{1,0:T(8,128)} %pack.1.own_ref), channel_id=1, source_target_pairs={{0,4},{1,5},{2,6},{3,7},{4,0},{5,1},{6,2},{7,3},{8,12},{9,13},{10,... | collective-permute-start | bytes 1585160 | tf_op jit(solution)/shard_map/ppermute | solution.py:296
  3.3 13.8 %collective-permute-start = (f32[1032,128]{1,0:T(8,128)}, f32[1032,128]{1,0:T(8,128)S(1)}, u32[]{:S(2)}, u32[]{:S(2)}) collective-permute-start(f32[1032,128]{1,0:T(8,128)} %pack.1.own_ref), channel_id=1, source_target_pairs={{0,1},{1,0},{2,3},{3,2},{4,5},{5,4},{6,7},{7,6},{8,9},{9,8},{10,11... | collective-permute-start | bytes 1585160 | tf_op jit(solution)/shard_map/ppermute | solution.py:306
  4.6 13.7 %collective-permute-start.4 = (f32[1032,128]{1,0:T(8,128)}, f32[1032,128]{1,0:T(8,128)S(1)}, u32[]{:S(2)}, u32[]{:S(2)}) collective-permute-start(f32[1032,128]{1,0:T(8,128)} %pack.1.own_ref), channel_id=1, source_target_pairs={{0,28},{1,13},{2,22},{3,7},{4,0},{5,17},{6,10},{7,27},{8,20},{9,5}... | collective-permute-start | bytes 1585160 | tf_op jit(solution)/shard_map/ppermute | solution.py:296
  5.0 15.1 %collective-permute-start.3 = (f32[1032,128]{1,0:T(8,128)}, f32[1032,128]{1,0:T(8,128)S(1)}, u32[]{:S(2)}, u32[]{:S(2)}) collective-permute-start(f32[1032,128]{1,0:T(8,128)} %pack.1.own_ref), channel_id=1, source_target_pairs={{0,0},{1,17},{2,10},{3,27},{4,28},{5,13},{6,22},{7,7},{8,8},{9,25}... | collective-permute-start | bytes 1585160 | tf_op jit(solution)/shard_map/ppermute | solution.py:296
  8.1 1.0 %copy-start = (f32[1032,128]{1,0:T(8,128)S(1)}, f32[1032,128]{1,0:T(8,128)}, u32[]{:S(2)}) copy-start(f32[1032,128]{1,0:T(8,128)} %pack.1.own_ref) | copy-start | bytes 1585156
  17.1 8.4 %collective-permute-start.2 = (f32[1032,128]{1,0:T(8,128)S(1)}, f32[1032,128]{1,0:T(8,128)S(1)}, u32[]{:S(2)}, u32[]{:S(2)}) collective-permute-start(f32[1032,128]{1,0:T(8,128)S(1)} %collective-permute-done.own_ref), channel_id=1, source_target_pairs={{0,4},{1,5},{2,6},{3,7},{4,0},{5,1},{6,2},{7,3},{8,12},{9,13},{10,... | collective-permute-start | bytes 1585160 | tf_op jit(solution)/shard_map/ppermute | solution.py:309
  18.3 12.1 %collective-permute-start.8 = (f32[1032,128]{1,0:T(8,128)S(1)}, f32[1032,128]{1,0:T(8,128)S(1)}, u32[]{:S(2)}, u32[]{:S(2)}) collective-permute-start(f32[1032,128]{1,0:T(8,128)S(1)} %collective-permute-done.own_ref), channel_id=1, source_target_pairs={{0,28},{1,13},{2,22},{3,7},{4,0},{5,17},{6,10},{7,27},{8,20},{9,5}... | collective-permute-start | bytes 1585160 | tf_op jit(solution)/shard_map/ppermute | solution.py:296
  20.1 16.1 %collective-permute-start.5 = (f32[1032,128]{1,0:T(8,128)S(1)}, f32[1032,128]{1,0:T(8,128)S(1)}, u32[]{:S(2)}, u32[]{:S(2)}) collective-permute-start(f32[1032,128]{1,0:T(8,128)S(1)} %collective-permute-done.own_ref), channel_id=1, source_target_pairs={{0,0},{1,17},{2,10},{3,27},{4,28},{5,13},{6,22},{7,7},{8,8},{9,25}... | collective-permute-start | bytes 1585160 | tf_op jit(solution)/shard_map/ppermute | solution.py:296
  31.8 10.5 %collective-permute-start.9 = (f32[256,256]{1,0:T(8,128)S(1)}, f32[256,256]{1,0:T(8,128)S(1)}, u32[]{:S(2)}, u32[]{:S(2)}) collective-permute-start(f32[256,256]{1,0:T(8,128)S(1)} %get-tuple-element.21), channel_id=1, source_target_pairs={{0,4},{1,6},{2,5},{3,7},{4,3},{5,1},{6,2},{7,0},{8,13},{9,15},{10,... | collective-permute-start | bytes 786440 | tf_op jit(solution)/shard_map/ppermute | solution.py:317
  33.0 10.8 %collective-permute-start.10 = (f32[256,256]{1,0:T(8,128)S(1)}, f32[256,256]{1,0:T(8,128)S(1)}, u32[]{:S(2)}, u32[]{:S(2)}) collective-permute-start(f32[256,256]{1,0:T(8,128)S(1)} %get-tuple-element.22), channel_id=1, source_target_pairs={{0,0},{1,2},{2,1},{3,3},{4,7},{5,5},{6,6},{7,4},{8,9},{9,11},{10,8... | collective-permute-start | bytes 786440 | tf_op jit(solution)/shard_map/ppermute | solution.py:316
  37.5 12.0 %collective-permute-start.6 = (f32[256,256]{1,0:T(8,128)S(1)}, f32[256,256]{1,0:T(8,128)S(1)}, u32[]{:S(2)}, u32[]{:S(2)}) collective-permute-start(f32[256,256]{1,0:T(8,128)S(1)} %get-tuple-element.17), channel_id=1, source_target_pairs={{0,0},{1,2},{2,1},{3,3},{4,7},{5,5},{6,6},{7,4},{8,9},{9,11},{10,8... | collective-permute-start | bytes 786440 | tf_op jit(solution)/shard_map/ppermute | solution.py:316
  39.4 17.8 %collective-permute-start.7 = (f32[256,256]{1,0:T(8,128)S(1)}, f32[256,256]{1,0:T(8,128)S(1)}, u32[]{:S(2)}, u32[]{:S(2)}) collective-permute-start(f32[256,256]{1,0:T(8,128)S(1)} %get-tuple-element.18), channel_id=1, source_target_pairs={{0,4},{1,6},{2,5},{3,7},{4,3},{5,1},{6,2},{7,0},{8,13},{9,15},{10,... | collective-permute-start | bytes 786440 | tf_op jit(solution)/shard_map/ppermute | solution.py:317
